TPU v7x, 256 devices: a whole 4x4x8 slice. The times are simulated.
256 devices in a mesh: dp: 32 (over z, x), tensor: 8 (over y, core).
Axes of the slice: x: 4, y: 4, z: 8, core: 2. Of those that a mesh axis runs over, the one named last changes fastest.
Arguments:
- activations: bfloat16 [16384, 128, 128], P('dp', 'tensor'), may hold values from -6 to 6
- cotangent: bfloat16 [16384, 128, 128], P('dp', 'tensor'), may hold values from -0.004119873 to 0.004119873
- left_factor: bfloat16 [128, 128], replicated, may hold values from -0.5 to 0.5
- right_factor: bfloat16 [128, 128], replicated, may hold values from -0.5 to 0.5
- scale_power: int32 [128, 128], replicated, may hold values from -5 to -3
- grid_bits: int32 [128, 128], replicated, may hold values from 4 to 7
Outputs:
- grad_left: float32 [128, 128], replicated
- grad_right: float32 [128, 128], replicated
All inputs are finite; a program needn't handle non-finite values.
Results may differ from a plain program's by a relative error of at most 0.009.
The roundings to bfloat16 on the way count: a program that leaves them out, or rounds other values in their place, can miss the bound.
Values may be sent and summed in bfloat16 or wider, within the bound.
No kernel may reach another device: no remote copies, remote signals or barrier semaphores. Data moves between devices by JAX's collectives and lax.ppermute only.
A program may use at most 64 MiB of HBM per device.

v0:
```python
import jax
import jax.numpy as jnp
from jax import lax
from jax.sharding import PartitionSpec as P


def on_device(activations, cotangent, left_factor, right_factor, scale_power, grid_bits):
    rotated = jnp.einsum(
        "tij,jb->tib", activations, right_factor, preferred_element_type=jnp.float32
    ).astype(jnp.bfloat16)
    tok_rot, tok_cot = (
        lax.all_to_all(rotated, "tensor", split_axis=0, concat_axis=1, tiled=True),
        lax.all_to_all(cotangent, "tensor", split_axis=0, concat_axis=1, tiled=True),
    )
    transformed = jnp.einsum(
        "ia,tib->tab", left_factor, tok_rot, preferred_element_type=jnp.float32
    )
    step_size = jnp.exp2(scale_power.astype(jnp.float32))
    half_grid = jnp.exp2((grid_bits - 1).astype(jnp.float32))
    lower_edge = -half_grid * step_size
    upper_edge = (half_grid - 1.0) * step_size
    inside = (transformed >= lower_edge) & (transformed <= upper_edge)
    grad_mid = jnp.where(inside, tok_cot.astype(jnp.float32), jnp.float32(0.0)).astype(jnp.bfloat16)
    grad_rot = jnp.einsum(
        "ia,tab->tib", left_factor, grad_mid, preferred_element_type=jnp.float32
    ).astype(jnp.bfloat16)
    grad_left = jnp.einsum("tib,tab->ia", tok_rot, grad_mid, preferred_element_type=jnp.float32)
    back_grad = lax.all_to_all(grad_rot, "tensor", split_axis=1, concat_axis=0, tiled=True)
    grad_right = jnp.einsum(
        "tij,tib->jb", activations, back_grad, preferred_element_type=jnp.float32
    )
    grad_left, grad_right = lax.psum((grad_left, grad_right), ("dp", "tensor"))
    return (grad_left, grad_right)


def solution(mesh):
    return jax.shard_map(
        on_device,
        mesh=mesh,
        in_specs=(P("dp", "tensor", None), P("dp", "tensor", None), P(), P(), P(), P()),
        out_specs=(P(), P()),
        check_vma=False,
    )
```

profile of v0, /device:TPU:1, one launch (start us, length us, event | category | flops | bytes accessed | tf_op | source)
XLA Modules:
  0.0 381.0 jit_solution(9666594264035312320)
XLA Ops:
  7.2 0.0 copy-start
  7.2 2.4 fusion.3
  9.6 1.4 copy.54
  11.0 32.9 %all_to_all.45 = bf16[512,16,128]{2,1,0:T(8,128)(2,1)} all-to-all(bf16[512,16,128]{2,1,0:T(8,128)(2,1)S(1)} %copy.54), channel_id=1, replica_groups=mesh['dp'=32,'tensor'=8] {'tensor'}, dimensions={0} | all-to-all | bytes 4194304 | tf_op jit(solution)/shard_map/all_to_all | solution.py:12
  43.8 0.0 copy-start.3
  43.8 0.0 copy-start.4
  43.8 5.4 %all-to-all-start.1 = ((bf16[512,16,128]{2,1,0:T(8,128)(2,1)}), bf16[512,16,128]{2,1,0:T(8,128)(2,1)}, u32[]{:S(2)}, u32[]{:S(2)}) async-start(bf16[512,16,128]{2,1,0:T(8,128)(2,1)} %param.7), calls=%async_computation.1 | async-start | bytes 4194304 | tf_op jit(solution)/shard_map/all_to_all | solution.py:13
  49.2 0.0 copy-done.3
  49.2 0.0 copy-done.4
  49.3 0.1 copy.58
  49.4 0.1 copy.57
  49.5 2.2 copy.55
  51.7 24.0 %all-to-all-done.1 = bf16[512,16,128]{2,1,0:T(8,128)(2,1)} async-done(((bf16[512,16,128]{2,1,0:T(8,128)(2,1)}), bf16[512,16,128]{2,1,0:T(8,128)(2,1)}, u32[]{:S(2)}, u32[]{:S(2)}) %all-to-all-start.1) | async-done | bytes 2097184 | tf_op jit(solution)/shard_map/all_to_all | solution.py:13
  75.7 3.5 copy.59
  79.2 4.1 %copy.60 = bf16[64,128,128]{1,2,0:T(8,128)(2,1)} copy(bf16[64,128,128]{2,1,0:T(8,128)(2,1)} %bitcast.48) | data formatting | bytes 4194304 | tf_op jit(solution)/shard_map/convert_element_type | solution.py:23
  83.3 0.0 copy-done
  83.3 2.6 select_convert_fusion
  85.9 0.0 copy-start.1
  85.9 1.3 copy-done.1
  87.2 2.0 convert_bitcast_fusion.1
  89.2 4.1 %copy.62 = bf16[64,128,128]{2,0,1:T(8,128)(2,1)} copy(bf16[64,128,128]{1,2,0:T(8,128)(2,1)} %convert_bitcast_fusion.1) | data formatting | bytes 4194304 | tf_op jit(solution)/shard_map/convert_element_type | solution.py:26
  93.4 5.1 %all-to-all-start.2 = ((bf16[64,128,128]{2,0,1:T(8,128)(2,1)}), bf16[64,128,128]{2,0,1:T(8,128)(2,1)}, u32[]{:S(2)}, u32[]{:S(2)}) async-start(bf16[64,128,128]{2,0,1:T(8,128)(2,1)} %copy.62), calls=%async_computation.2 | async-start | bytes 4194304 | tf_op jit(solution)/shard_map/all_to_all | solution.py:28
  98.5 0.0 all-reduce.3.cloned.1.call-start
  98.5 2.9 convolution_bitcast_fusion.1
  101.4 23.5 %all-to-all-done.2 = bf16[64,128,128]{2,0,1:T(8,128)(2,1)} async-done(((bf16[64,128,128]{2,0,1:T(8,128)(2,1)}), bf16[64,128,128]{2,0,1:T(8,128)(2,1)}, u32[]{:S(2)}, u32[]{:S(2)}) %all-to-all-start.2) | async-done | bytes 2097184 | tf_op jit(solution)/shard_map/all_to_all | solution.py:28
  124.9 0.0 copy-start.2
  124.9 3.1 copy.64
  128.0 0.0 copy-done.2
  128.0 1.4 convolution_bitcast_fusion
  129.4 0.0 all-reduce.3.cloned.1.call-update
  129.4 241.7 %all-reduce.3.cloned.1.call-done = (f32[128,128]{1,0:T(8,128)}, f32[128,128]{0,1:T(8,128)}) async-done(((f32[128,128]{1,0:T(8,128)}, f32[128,128]{0,1:T(8,128)}), (f32[128,128]{1,0:T(8,128)}, f32[128,128]{0,1:T(8,128)})) %all-reduce.3.cloned.1.call-update) | async-done | bytes 131088 | tf_op jit(solution)/shard_map/psum | solution.py:32
  371.2 1.6 copy.65
  372.7 1.5 copy.75
  (1 shorter events, 0.0 us)
Async XLA Ops:
  7.2 76.1 %copy-start = (bf16[128,128]{1,0:T(8,128)(2,1)S(1)}, bf16[128,128]{1,0:T(8,128)(2,1)}, u32[]{:S(2)}) copy-start(bf16[128,128]{1,0:T(8,128)(2,1)} %param.8) | copy-start | bytes 98308
  43.8 5.4 %copy-start.3 = (s32[128,128]{1,0:T(8,128)S(1)}, s32[128,128]{1,0:T(8,128)}, u32[]{:S(2)}) copy-start(s32[128,128]{1,0:T(8,128)} %param.10) | copy-start | bytes 196612
  43.8 5.4 %copy-start.4 = (s32[128,128]{1,0:T(8,128)S(1)}, s32[128,128]{1,0:T(8,128)}, u32[]{:S(2)}) copy-start(s32[128,128]{1,0:T(8,128)} %param.11) | copy-start | bytes 196612
  43.8 31.9 %all-to-all-start.1 = ((bf16[512,16,128]{2,1,0:T(8,128)(2,1)}), bf16[512,16,128]{2,1,0:T(8,128)(2,1)}, u32[]{:S(2)}, u32[]{:S(2)}) async-start(bf16[512,16,128]{2,1,0:T(8,128)(2,1)} %param.7), calls=%async_computation.1 | async-start | bytes 4194304 | tf_op jit(solution)/shard_map/all_to_all | solution.py:13
  85.9 1.3 copy-start.1
  93.4 31.6 %all-to-all-start.2 = ((bf16[64,128,128]{2,0,1:T(8,128)(2,1)}), bf16[64,128,128]{2,0,1:T(8,128)(2,1)}, u32[]{:S(2)}, u32[]{:S(2)}) async-start(bf16[64,128,128]{2,0,1:T(8,128)(2,1)} %copy.62), calls=%async_computation.2 | async-start | bytes 4194304 | tf_op jit(solution)/shard_map/all_to_all | solution.py:28
  98.5 272.7 %all-reduce.3.cloned.1.call-start = ((), (), s32[]{:S(2)}) async-start(), calls=%async_computation.3 | async-start | bytes 262144 | tf_op jit(solution)/shard_map/psum | solution.py:32
  124.9 3.1 copy-start.2
Sparse Core Ops, SparseCore 0:
  129.6 241.5 all-reduce.2
where the time goes:
time: 382 us; the launch traced here: 381 us
  waiting for transfers between devices  289 us (76%)
  blocking collectives  32.9 us (9%)
  local copies, waits for them, and re-layouts  22.9 us (6%)
  between operations  14.1 us (4%)
  matrix products  11.4 us (3%)
  starting transfers between devices  10.5 us (3%)
    psum x1, waiting for transfers between devices, on_device(): grad_left, grad_right = lax.psum((grad_left, grad_right), ('dp', 'tensor'))  242 us
    all_to_all x1, blocking collectives, on_device(): lax.all_to_all(rotated, 'tensor', split_axis=0, concat_axis=1, tiled=True)  32.9 us
    all_to_all x1, waiting for transfers between devices, on_device(): lax.all_to_all(cotangent, 'tensor', split_axis=0, concat_axis=1, tiled=True)  24 us
    all_to_all x1, waiting for transfers between devices, on_device(): lax.all_to_all(grad_rot, 'tensor', split_axis=1, concat_axis=0, tiled=True)  23.5 us
  transfers between devices with their start and end apart: 3, of which 3 were waited for; matrix products, arithmetic and copies ran while one was open for 1% of the time, Pallas kernels for 0%

commit v1 on v0

v1 whole, which is shorter than its diff:
```python
import jax
import jax.numpy as jnp
from jax import lax
from jax.experimental import pallas as pl
from jax.experimental.pallas import tpu as pltpu
from jax.sharding import PartitionSpec as P

F32 = jnp.float32
BF16 = jnp.bfloat16
STEP_TOKENS = 16


def grads_kernel(act_ref, cot_ref, left_ref, left_t_ref, right_ref, lower_ref, upper_ref, gl_ref, gr_ref):
    @pl.when(pl.program_id(0) == 0)
    def _():
        gl_ref[...] = jnp.zeros_like(gl_ref)
        gr_ref[...] = jnp.zeros_like(gr_ref)

    tokens = act_ref.shape[1]
    act = jnp.concatenate([act_ref[:, t].reshape(128, 128) for t in range(tokens)], axis=0)
    rot = jnp.dot(act, right_ref[...], preferred_element_type=F32).astype(BF16)
    rot = jnp.concatenate([rot[t * 128 : (t + 1) * 128] for t in range(tokens)], axis=1)
    trans = jnp.dot(left_t_ref[...], rot, preferred_element_type=F32)
    lower, upper = lower_ref[...], upper_ref[...]
    mids = []
    for t in range(tokens):
        tr = trans[:, t * 128 : (t + 1) * 128]
        cot = cot_ref[:, t].reshape(128, 128).astype(F32)
        mids.append(jnp.where((tr >= lower) & (tr <= upper), cot, 0.0).astype(BF16))
    mid = jnp.concatenate(mids, axis=1)
    back = jnp.dot(left_ref[...], mid, preferred_element_type=F32).astype(BF16)
    gl_ref[...] += lax.dot_general(rot, mid, (((1,), (1,)), ((), ())), preferred_element_type=F32)
    back = jnp.concatenate([back[:, t * 128 : (t + 1) * 128] for t in range(tokens)], axis=0)
    gr_ref[...] += lax.dot_general(act, back, (((0,), (0,)), ((), ())), preferred_element_type=F32)


def local_grads(act, cot, left, left_t, right, lower, upper):
    tokens = act.shape[1]
    whole = pl.BlockSpec((128, 128), lambda s: (0, 0))
    block = pl.BlockSpec((8, STEP_TOKENS, 16, 128), lambda s: (0, s, 0, 0))
    return pl.pallas_call(
        grads_kernel,
        grid=(tokens // STEP_TOKENS,),
        in_specs=[block, block] + [whole] * 5,
        out_specs=[whole, whole],
        out_shape=[jax.ShapeDtypeStruct((128, 128), F32)] * 2,
        compiler_params=pltpu.CompilerParams(vmem_limit_bytes=48 * 2**20),
        cost_estimate=pl.CostEstimate(flops=10 * tokens * 128**3, bytes_accessed=tokens * 2**16, transcendentals=0),
    )(act, cot, left, left_t, right, lower, upper)


def tensor_shift(y, core):
    return [(i, ((i // 2 + y) % 4) * 2 + ((i % 2) ^ core)) for i in range(8)]


def x_shift(s):
    return [(i, (i // 4) * 4 + (i % 4 + s) % 4) for i in range(32)]


def z_flip(b):
    return [(i, ((i // 4) ^ b) * 4 + i % 4) for i in range(32)]


def add_pair(x, axis, perm):
    return x + lax.ppermute(x, axis, perm)


def add_four(x, axis, shift):
    one, two, three = (lax.ppermute(x, axis, shift(s)) for s in (1, 2, 3))
    return (x + two) + (one + three)


def sum_all(grad_left, grad_right):
    core = lax.axis_index("tensor") % 2
    first = core == 0
    keep = jnp.where(first, grad_left, grad_right)
    give = jnp.where(first, grad_right, grad_left)
    swap = tensor_shift(0, 1)
    x = keep + lax.ppermute(give, "tensor", swap)
    x = add_four(x, "tensor", lambda s: tensor_shift(s, 0))
    x = add_four(x, "dp", x_shift)
    for b in (1, 2, 4):
        x = add_pair(x, "dp", z_flip(b))
    other = lax.ppermute(x, "tensor", swap)
    return jnp.where(first, x, other), jnp.where(first, other, x)


def exchange(x):
    return lax.all_to_all(x.reshape(8, -1, 16, 128), "tensor", 0, 0, tiled=False)


def on_device(activations, cotangent, left_factor, right_factor, scale_power, grid_bits):
    act, cot = exchange(activations), exchange(cotangent)
    step_size = jnp.exp2(scale_power.astype(F32))
    half_grid = jnp.exp2((grid_bits - 1).astype(F32))
    lower = -half_grid * step_size
    upper = (half_grid - 1.0) * step_size
    grad_left, grad_right = local_grads(
        act, cot, left_factor, left_factor.T, right_factor, lower, upper
    )
    return sum_all(grad_left, grad_right)


def solution(mesh):
    return jax.shard_map(
        on_device,
        mesh=mesh,
        in_specs=(P("dp", "tensor", None), P("dp", "tensor", None), P(), P(), P(), P()),
        out_specs=(P(), P()),
        check_vma=False,
    )
```

time: 382 us -> 113 us (0.30)
  waiting for transfers between devices: 289 us -> 43.1 us
  local copies, waits for them, and re-layouts: 22.9 us -> 0.12 us
  starting transfers between devices: 10.5 us -> 29.7 us
  between operations: 14.1 us -> 0.72 us
  matrix products: 11.4 us -> 0 us
  Pallas kernels: 0 us -> 5.29 us
    psum x1 -> x0, waiting for transfers between devices: 242 us -> none  [on_device(): grad_left, grad_right = lax.psum((grad_left, grad_right), ('dp', 'tensor'))]
    ppermute x0 -> x11, starting transfers between devices: none -> 24.3 us  [the longest x3 9.43 us: add_pair(): return x + lax.ppermute(x, axis, perm)]
    all_to_all x2 -> x1, waiting for transfers between devices: 47.5 us -> 26.3 us  [exchange(): lax.all_to_all(x.reshape(8, -1, 16, 128), 'tensor', 0, 0, tiled=False)]
    ppermute x0 -> x11, waiting for transfers between devices: none -> 16.9 us  [the longest x6 8.94 us: add_four(): one, two, three = (lax.ppermute(x, axis, shift(s)) for s in (1, 2, 3))]
    convert_element_type x4 -> x0, local copies, waits for them, and re-layouts: 13.1 us -> none  [the longest x2 7.59 us: on_device(): tok_cot.astype(jnp.float32)]
    dot_general x5 -> x0, matrix products: 11.4 us -> none  [the longest x1 2.92 us: on_device(): jnp.einsum('tib,tab->ia', tok_rot, grad_mid, preferred_element_type=jnp.f...]
    all_to_all x2 -> x0, local copies, waits for them, and re-layouts: 5.3 us -> none  [the longest x1 3.11 us: on_device(): lax.all_to_all(grad_rot, 'tensor', split_axis=1, concat_axis=0, tiled=True)]
    pallas_call x0 -> x1, Pallas kernels: none -> 5.29 us  [local_grads(): pl.pallas_call(grads_kernel, grid=(tokens // STEP_TOKENS,), in_specs=[blo...]
  transfers between devices with their start and end apart: 3 -> 12, of which waited for: 3 -> 10; matrix products, arithmetic and copies ran while one was open for 1% -> 0% of each run, Pallas kernels for 0% -> 0%
where the time goes in v1:
time: 113 us
  waiting for transfers between devices  43.1 us (38%)
  blocking collectives  33.2 us (29%)
  starting transfers between devices  29.7 us (26%)
  Pallas kernels  5.29 us (5%)
    all_to_all x1, blocking collectives, exchange(): lax.all_to_all(x.reshape(8, -1, 16, 128), 'tensor', 0, 0, tiled=False)  33.2 us
    all_to_all x1, waiting for transfers between devices, exchange(): lax.all_to_all(x.reshape(8, -1, 16, 128), 'tensor', 0, 0, tiled=False)  26.3 us
    ppermute x3, starting transfers between devices, add_pair(): return x + lax.ppermute(x, axis, perm)  9.43 us
    ppermute x6, waiting for transfers between devices, add_four(): one, two, three = (lax.ppermute(x, axis, shift(s)) for s in (1, 2, 3))  8.94 us
    ppermute x1, starting transfers between devices, sum_all(): other = lax.ppermute(x, 'tensor', swap)  7.6 us
    ppermute x6, starting transfers between devices, add_four(): one, two, three = (lax.ppermute(x, axis, shift(s)) for s in (1, 2, 3))  6.27 us
    ppermute x3, waiting for transfers between devices, add_pair(): return x + lax.ppermute(x, axis, perm)  6.11 us
    all_to_all x1, starting transfers between devices, exchange(): lax.all_to_all(x.reshape(8, -1, 16, 128), 'tensor', 0, 0, tiled=False)  5.4 us
  transfers between devices with their start and end apart: 12, of which 10 were waited for; matrix products, arithmetic and copies ran while one was open for 0% of the time, Pallas kernels for 0%

profile of v1, /device:TPU:1, one launch (start us, length us, event | category | flops | bytes accessed | tf_op | source)
XLA Modules:
  0.0 112.9 jit_solution(18225917173748327923)
XLA Ops:
  0.6 33.2 %all_to_all.10.act_ref = bf16[8,64,16,128]{3,2,1,0:T(8,128)(2,1)S(1)} all-to-all(bf16[8,64,16,128]{3,2,1,0:T(8,128)(2,1)} %bitcast.4), channel_id=1, replica_groups=mesh['dp'=32,'tensor'=8] {'tensor'}, dimensions={0} | all-to-all | bytes 4194304 | tf_op jit(solution)/shard_map/all_to_all | solution.py:89
  33.9 0.0 copy-start
  33.9 0.0 copy-start.2
  33.9 0.0 copy-start.3
  33.9 0.0 copy-start.1
  33.9 5.4 %all-to-all-start.1 = ((bf16[8,64,16,128]{3,2,1,0:T(8,128)(2,1)}), bf16[8,64,16,128]{3,2,1,0:T(8,128)(2,1)}, u32[]{:S(2)}, u32[]{:S(2)}) async-start(bf16[8,64,16,128]{3,2,1,0:T(8,128)(2,1)} %bitcast.5), calls=%async_computation.1 | async-start | bytes 4194304 | tf_op jit(solution)/shard_map/all_to_all | solution.py:89
  39.3 0.0 copy-done
  39.3 0.1 copy.8
  39.4 0.0 copy-done.2
  39.4 0.0 copy-done.3
  39.5 26.3 %all-to-all-done.1.cot_ref = bf16[8,64,16,128]{3,2,1,0:T(8,128)(2,1)} async-done(((bf16[8,64,16,128]{3,2,1,0:T(8,128)(2,1)}), bf16[8,64,16,128]{3,2,1,0:T(8,128)(2,1)}, u32[]{:S(2)}, u32[]{:S(2)}) %all-to-all-start.1) | async-done | bytes 2097184 | tf_op jit(solution)/shard_map/all_to_all | solution.py:89
  65.7 0.0 copy-done.1
  65.7 5.3 %shard_map.77 = (f32[128,128]{1,0:T(8,128)S(1)}, f32[128,128]{1,0:T(8,128)S(1)}) custom-call(bf16[8,64,16,128]{3,2,1,0:T(8,128)(2,1)S(1)} %all_to_all.10.act_ref, bf16[8,64,16,128]{3,2,1,0:T(8,128)(2,1)} %all-to-all-done.1.cot_ref, bf16[128,128]{1,0:T(8,128)(2,1)S(1)} %copy-done, bf16[128,128]{1,0:T(8,128)(2,1)S(1)} %bitcast.3, ...), custom_call_target="tpu_custom_call" | custom-call | flops 1342177280 | bytes 4194304 | tf_op jit(solution)/shard_map/pallas_call | solution.py:41
  71.0 1.0 collective-permute-start
  72.0 0.9 collective-permute-done
  72.9 0.4 collective-permute-start.2
  73.3 2.4 %collective-permute-start.3 = (f32[128,128]{1,0:T(8,128)S(1)}, f32[128,128]{1,0:T(8,128)S(1)}, u32[]{:S(2)}, u32[]{:S(2)}) collective-permute-start(f32[128,128]{1,0:T(8,128)S(1)} %select_add_fusion), channel_id=1, source_target_pairs={{0,6},{1,7},{2,0},{3,1},{4,2},{5,3},{6,4},{7,5},{8,14},{9,15},{10,... | collective-permute-start | bytes 196616 | tf_op jit(solution)/shard_map/ppermute | solution.py:69
  75.7 0.0 collective-permute-start.1
  75.7 1.6 %collective-permute-done.2 = f32[128,128]{1,0:T(8,128)S(1)} collective-permute-done((f32[128,128]{1,0:T(8,128)S(1)}, f32[128,128]{1,0:T(8,128)S(1)}, u32[]{:S(2)}, u32[]{:S(2)}) %collective-permute-start.2) | collective-permute-done | bytes 65568 | tf_op jit(solution)/shard_map/ppermute | solution.py:69
  77.3 0.0 collective-permute-done.3
  77.3 3.0 %collective-permute-done.1 = f32[128,128]{1,0:T(8,128)S(1)} collective-permute-done((f32[128,128]{1,0:T(8,128)S(1)}, f32[128,128]{1,0:T(8,128)S(1)}, u32[]{:S(2)}, u32[]{:S(2)}) %collective-permute-start.1) | collective-permute-done | bytes 65568 | tf_op jit(solution)/shard_map/ppermute | solution.py:69
  80.3 0.5 collective-permute-start.5
  80.8 2.2 %collective-permute-start.6 = (f32[128,128]{1,0:T(8,128)S(1)}, f32[128,128]{1,0:T(8,128)S(1)}, u32[]{:S(2)}, u32[]{:S(2)}) collective-permute-start(f32[128,128]{1,0:T(8,128)S(1)} %add_add_fusion.1), channel_id=1, source_target_pairs={{0,24},{8,0},{16,8},{24,16},{32,56},{40,32},{48,40},{56,48},{64,88... | collective-permute-start | bytes 196616 | tf_op jit(solution)/shard_map/ppermute | solution.py:69
  83.1 0.8 collective-permute-start.4
  83.8 0.9 collective-permute-done.5
  84.7 0.0 collective-permute-done.6
  84.7 3.4 %collective-permute-done.4 = f32[128,128]{1,0:T(8,128)S(1)} collective-permute-done((f32[128,128]{1,0:T(8,128)S(1)}, f32[128,128]{1,0:T(8,128)S(1)}, u32[]{:S(2)}, u32[]{:S(2)}) %collective-permute-start.4) | collective-permute-done | bytes 65568 | tf_op jit(solution)/shard_map/ppermute | solution.py:69
  88.2 0.7 collective-permute-start.7
  88.9 2.5 %collective-permute-done.7 = f32[128,128]{1,0:T(8,128)S(1)} collective-permute-done((f32[128,128]{1,0:T(8,128)S(1)}, f32[128,128]{1,0:T(8,128)S(1)}, u32[]{:S(2)}, u32[]{:S(2)}) %collective-permute-start.7) | collective-permute-done | bytes 65568 | tf_op jit(solution)/shard_map/ppermute | solution.py:65
  91.4 2.2 %collective-permute-start.8 = (f32[128,128]{1,0:T(8,128)S(1)}, f32[128,128]{1,0:T(8,128)S(1)}, u32[]{:S(2)}, u32[]{:S(2)}) collective-permute-start(f32[128,128]{1,0:T(8,128)S(1)} %add.44), channel_id=1, source_target_pairs={{0,64},{8,72},{16,80},{24,88},{32,96},{40,104},{48,112},{56,120},{... | collective-permute-start | bytes 196616 | tf_op jit(solution)/shard_map/ppermute | solution.py:65
  93.6 2.0 %collective-permute-done.8 = f32[128,128]{1,0:T(8,128)S(1)} collective-permute-done((f32[128,128]{1,0:T(8,128)S(1)}, f32[128,128]{1,0:T(8,128)S(1)}, u32[]{:S(2)}, u32[]{:S(2)}) %collective-permute-start.8) | collective-permute-done | bytes 65568 | tf_op jit(solution)/shard_map/ppermute | solution.py:65
  95.6 6.5 %collective-permute-start.9 = (f32[128,128]{1,0:T(8,128)S(1)}, f32[128,128]{1,0:T(8,128)S(1)}, u32[]{:S(2)}, u32[]{:S(2)}) collective-permute-start(f32[128,128]{1,0:T(8,128)S(1)} %add.45), channel_id=1, source_target_pairs={{0,128},{8,136},{16,144},{24,152},{32,160},{40,168},{48,176},{56,1... | collective-permute-start | bytes 196616 | tf_op jit(solution)/shard_map/ppermute | solution.py:65
  102.1 1.7 %collective-permute-done.9 = f32[128,128]{1,0:T(8,128)S(1)} collective-permute-done((f32[128,128]{1,0:T(8,128)S(1)}, f32[128,128]{1,0:T(8,128)S(1)}, u32[]{:S(2)}, u32[]{:S(2)}) %collective-permute-start.9) | collective-permute-done | bytes 65568 | tf_op jit(solution)/shard_map/ppermute | solution.py:65
  103.8 7.6 %collective-permute-start.10 = (f32[128,128]{1,0:T(8,128)S(1)}, f32[128,128]{1,0:T(8,128)S(1)}, u32[]{:S(2)}, u32[]{:S(2)}) collective-permute-start(f32[128,128]{1,0:T(8,128)S(1)} %add.46), channel_id=1, source_target_pairs={{0,1},{1,0},{2,3},{3,2},{4,5},{5,4},{6,7},{7,6},{8,9},{9,8},{10,11... | collective-permute-start | bytes 196616 | tf_op jit(solution)/shard_map/ppermute | solution.py:84
  111.4 0.9 collective-permute-done.10
  112.3 0.7 broadcast_select_fusion
  (8 shorter events, 0.1 us)
Async XLA Ops:
  33.9 5.4 %copy-start = (bf16[128,128]{1,0:T(8,128)(2,1)S(1)}, bf16[128,128]{1,0:T(8,128)(2,1)}, u32[]{:S(2)}) copy-start(bf16[128,128]{1,0:T(8,128)(2,1)} %left_ref.1) | copy-start | bytes 98308
  33.9 5.5 %copy-start.2 = (s32[128,128]{1,0:T(8,128)S(1)}, s32[128,128]{1,0:T(8,128)}, u32[]{:S(2)}) copy-start(s32[128,128]{1,0:T(8,128)} %param.10) | copy-start | bytes 196612
  33.9 5.5 %copy-start.3 = (s32[128,128]{1,0:T(8,128)S(1)}, s32[128,128]{1,0:T(8,128)}, u32[]{:S(2)}) copy-start(s32[128,128]{1,0:T(8,128)} %param.11) | copy-start | bytes 196612
  33.9 31.9 %copy-start.1 = (bf16[128,128]{1,0:T(8,128)(2,1)S(1)}, bf16[128,128]{1,0:T(8,128)(2,1)}, u32[]{:S(2)}) copy-start(bf16[128,128]{1,0:T(8,128)(2,1)} %right_ref.1) | copy-start | bytes 98308
  33.9 31.9 %all-to-all-start.1 = ((bf16[8,64,16,128]{3,2,1,0:T(8,128)(2,1)}), bf16[8,64,16,128]{3,2,1,0:T(8,128)(2,1)}, u32[]{:S(2)}, u32[]{:S(2)}) async-start(bf16[8,64,16,128]{3,2,1,0:T(8,128)(2,1)} %bitcast.5), calls=%async_computation.1 | async-start | bytes 4194304 | tf_op jit(solution)/shard_map/all_to_all | solution.py:89
  71.0 1.9 %collective-permute-start = (f32[128,128]{1,0:T(8,128)S(1)}, f32[128,128]{1,0:T(8,128)S(1)}, u32[]{:S(2)}, u32[]{:S(2)}) collective-permute-start(f32[128,128]{1,0:T(8,128)S(1)} %broadcast_select_fusion.2), channel_id=1, source_target_pairs={{0,1},{1,0},{2,3},{3,2},{4,5},{5,4},{6,7},{7,6},{8,9},{9,8},{10,11... | collective-permute-start | bytes 196616 | tf_op jit(solution)/shard_map/ppermute | solution.py:79
  72.9 4.4 %collective-permute-start.2 = (f32[128,128]{1,0:T(8,128)S(1)}, f32[128,128]{1,0:T(8,128)S(1)}, u32[]{:S(2)}, u32[]{:S(2)}) collective-permute-start(f32[128,128]{1,0:T(8,128)S(1)} %select_add_fusion), channel_id=1, source_target_pairs={{0,2},{1,3},{2,4},{3,5},{4,6},{5,7},{6,0},{7,1},{8,10},{9,11},{10,... | collective-permute-start | bytes 196616 | tf_op jit(solution)/shard_map/ppermute | solution.py:69
  73.3 4.0 %collective-permute-start.3 = (f32[128,128]{1,0:T(8,128)S(1)}, f32[128,128]{1,0:T(8,128)S(1)}, u32[]{:S(2)}, u32[]{:S(2)}) collective-permute-start(f32[128,128]{1,0:T(8,128)S(1)} %select_add_fusion), channel_id=1, source_target_pairs={{0,6},{1,7},{2,0},{3,1},{4,2},{5,3},{6,4},{7,5},{8,14},{9,15},{10,... | collective-permute-start | bytes 196616 | tf_op jit(solution)/shard_map/ppermute | solution.py:69
  75.7 4.6 %collective-permute-start.1 = (f32[128,128]{1,0:T(8,128)S(1)}, f32[128,128]{1,0:T(8,128)S(1)}, u32[]{:S(2)}, u32[]{:S(2)}) collective-permute-start(f32[128,128]{1,0:T(8,128)S(1)} %select_add_fusion), channel_id=1, source_target_pairs={{0,4},{1,5},{2,6},{3,7},{4,0},{5,1},{6,2},{7,3},{8,12},{9,13},{10,... | collective-permute-start | bytes 196616 | tf_op jit(solution)/shard_map/ppermute | solution.py:69
  80.3 4.4 %collective-permute-start.5 = (f32[128,128]{1,0:T(8,128)S(1)}, f32[128,128]{1,0:T(8,128)S(1)}, u32[]{:S(2)}, u32[]{:S(2)}) collective-permute-start(f32[128,128]{1,0:T(8,128)S(1)} %add_add_fusion.1), channel_id=1, source_target_pairs={{0,8},{8,16},{16,24},{24,0},{32,40},{40,48},{48,56},{56,32},{64,72... | collective-permute-start | bytes 196616 | tf_op jit(solution)/shard_map/ppermute | solution.py:69
  80.8 3.9 %collective-permute-start.6 = (f32[128,128]{1,0:T(8,128)S(1)}, f32[128,128]{1,0:T(8,128)S(1)}, u32[]{:S(2)}, u32[]{:S(2)}) collective-permute-start(f32[128,128]{1,0:T(8,128)S(1)} %add_add_fusion.1), channel_id=1, source_target_pairs={{0,24},{8,0},{16,8},{24,16},{32,56},{40,32},{48,40},{56,48},{64,88... | collective-permute-start | bytes 196616 | tf_op jit(solution)/shard_map/ppermute | solution.py:69
  83.1 5.1 %collective-permute-start.4 = (f32[128,128]{1,0:T(8,128)S(1)}, f32[128,128]{1,0:T(8,128)S(1)}, u32[]{:S(2)}, u32[]{:S(2)}) collective-permute-start(f32[128,128]{1,0:T(8,128)S(1)} %add_add_fusion.1), channel_id=1, source_target_pairs={{0,16},{8,24},{16,0},{24,8},{32,48},{40,56},{48,32},{56,40},{64,80... | collective-permute-start | bytes 196616 | tf_op jit(solution)/shard_map/ppermute | solution.py:69
  88.2 3.2 %collective-permute-start.7 = (f32[128,128]{1,0:T(8,128)S(1)}, f32[128,128]{1,0:T(8,128)S(1)}, u32[]{:S(2)}, u32[]{:S(2)}) collective-permute-start(f32[128,128]{1,0:T(8,128)S(1)} %add_add_fusion), channel_id=1, source_target_pairs={{0,32},{8,40},{16,48},{24,56},{32,0},{40,8},{48,16},{56,24},{64,96... | collective-permute-start | bytes 196616 | tf_op jit(solution)/shard_map/ppermute | solution.py:65
  91.4 4.2 %collective-permute-start.8 = (f32[128,128]{1,0:T(8,128)S(1)}, f32[128,128]{1,0:T(8,128)S(1)}, u32[]{:S(2)}, u32[]{:S(2)}) collective-permute-start(f32[128,128]{1,0:T(8,128)S(1)} %add.44), channel_id=1, source_target_pairs={{0,64},{8,72},{16,80},{24,88},{32,96},{40,104},{48,112},{56,120},{... | collective-permute-start | bytes 196616 | tf_op jit(solution)/shard_map/ppermute | solution.py:65
  95.6 8.1 %collective-permute-start.9 = (f32[128,128]{1,0:T(8,128)S(1)}, f32[128,128]{1,0:T(8,128)S(1)}, u32[]{:S(2)}, u32[]{:S(2)}) collective-permute-start(f32[128,128]{1,0:T(8,128)S(1)} %add.45), channel_id=1, source_target_pairs={{0,128},{8,136},{16,144},{24,152},{32,160},{40,168},{48,176},{56,1... | collective-permute-start | bytes 196616 | tf_op jit(solution)/shard_map/ppermute | solution.py:65
  103.8 8.5 %collective-permute-start.10 = (f32[128,128]{1,0:T(8,128)S(1)}, f32[128,128]{1,0:T(8,128)S(1)}, u32[]{:S(2)}, u32[]{:S(2)}) collective-permute-start(f32[128,128]{1,0:T(8,128)S(1)} %add.46), channel_id=1, source_target_pairs={{0,1},{1,0},{2,3},{3,2},{4,5},{5,4},{6,7},{7,6},{8,9},{9,8},{10,11... | collective-permute-start | bytes 196616 | tf_op jit(solution)/shard_map/ppermute | solution.py:84

commit v2 on v1

v2 whole, which is shorter than its diff:
```python
import functools

import jax
import jax.numpy as jnp
from jax import lax
from jax.experimental import pallas as pl
from jax.experimental.pallas import tpu as pltpu
from jax.sharding import PartitionSpec as P

F32 = jnp.float32
BF16 = jnp.bfloat16
STEP_TOKENS = 8
ROWS = 16
PARTS = (32, 32)
WINDOW = 5
HOPS = ((1, 0), (3, 0), (2, 0), (2, 1), (0, 1), (1, 1), (3, 1))


def tensor_shift(y, core):
    return [(i, ((i // 2 + y) % 4) * 2 + ((i % 2) ^ core)) for i in range(8)]


def x_shift(s):
    return [(i, (i // 4) * 4 + (i % 4 + s) % 4) for i in range(32)]


def z_flip(b):
    return [(i, ((i // 4) ^ b) * 4 + i % 4) for i in range(32)]


def place():
    me = lax.axis_index("tensor")
    return me // 2, lax.rem(me, 2)


def peer(dy, dc):
    y, core = place()
    return lax.rem(y + dy + 4, 4) * 2 + (1 - core if dc else core)


def pack_kernel(first, hops, act_ref, cot_ref, *refs):
    outs, sems = refs[:-1], refs[-1]
    tokens = outs[0].shape[1]
    copies = []
    for k, (dy, dc) in enumerate(hops):
        for half, ref in enumerate((act_ref, cot_ref)):
            copies.append(
                pltpu.make_async_copy(
                    ref.at[peer(dy, dc), pl.ds(first, tokens)], outs[k].at[half], sems.at[2 * k + half]
                )
            )
    for copy in copies:
        copy.start()
    for copy in copies:
        copy.wait()


def pack(act, cot, first, tokens, hops):
    return pl.pallas_call(
        functools.partial(pack_kernel, first, hops),
        in_specs=[pl.BlockSpec(memory_space=pl.ANY)] * 2,
        out_specs=[pl.BlockSpec(memory_space=pltpu.VMEM)] * len(hops),
        out_shape=[jax.ShapeDtypeStruct((2, tokens, ROWS, 128), BF16)] * len(hops),
        scratch_shapes=[pltpu.SemaphoreType.DMA((2 * len(hops),))],
        cost_estimate=pl.CostEstimate(flops=0, bytes_accessed=len(hops) * tokens * 2**14, transcendentals=0),
        name="pack",
    )(act, cot)


def grads_kernel(*refs):
    parts, refs = refs[:8], refs[8:]
    (left_ref, left_t_ref, right_ref, lower_ref, upper_ref, gl_in, gr_in), refs = refs[:7], refs[7:]
    gl_ref, gr_ref, act_all, cot_all = refs
    left, left_t, right = left_ref[...], left_t_ref[...], right_ref[...]
    lower, upper = lower_ref[...], upper_ref[...]
    total = parts[0].shape[1]
    tokens = min(STEP_TOKENS, total)
    grad_left, grad_right = gl_in[...], gr_in[...]
    for k, (dy, dc) in enumerate(HOPS + ((0, 0),)):
        source = peer(-dy, dc)
        for t in range(total):
            rows = pl.ds(pl.multiple_of(t * 128 + source * ROWS, ROWS), ROWS)
            act_all[rows, :] = parts[k][0, t]
            cot_all[rows, :] = parts[k][1, t]
    for first in range(0, total, tokens):
        act = act_all[first * 128 : (first + tokens) * 128, :]
        rot = jnp.dot(act, right, preferred_element_type=F32).astype(BF16)
        rot = jnp.concatenate([rot[t * 128 : (t + 1) * 128] for t in range(tokens)], axis=1)
        trans = jnp.dot(left_t, rot, preferred_element_type=F32)
        mids = []
        for t in range(tokens):
            tr = trans[:, t * 128 : (t + 1) * 128]
            cot = cot_all[(first + t) * 128 : (first + t + 1) * 128, :].astype(F32)
            mids.append(jnp.where((tr >= lower) & (tr <= upper), cot, 0.0).astype(BF16))
        mid = jnp.concatenate(mids, axis=1)
        back = jnp.dot(left, mid, preferred_element_type=F32).astype(BF16)
        grad_left += lax.dot_general(rot, mid, (((1,), (1,)), ((), ())), preferred_element_type=F32)
        back = jnp.concatenate([back[:, t * 128 : (t + 1) * 128] for t in range(tokens)], axis=0)
        grad_right += lax.dot_general(act, back, (((0,), (0,)), ((), ())), preferred_element_type=F32)
    gl_ref[...] = grad_left
    gr_ref[...] = grad_right


def local_grads(parts, *rest):
    tokens = parts[0].shape[1]
    return pl.pallas_call(
        grads_kernel,
        in_specs=[pl.BlockSpec(memory_space=pltpu.VMEM)] * 15,
        out_specs=[pl.BlockSpec(memory_space=pltpu.VMEM)] * 2,
        out_shape=[jax.ShapeDtypeStruct((128, 128), F32)] * 2,
        scratch_shapes=[pltpu.VMEM((tokens * 128, 128), BF16)] * 2,
        compiler_params=pltpu.CompilerParams(vmem_limit_bytes=32 * 2**20),
        cost_estimate=pl.CostEstimate(flops=10 * tokens * 128**3, bytes_accessed=tokens * 2**16, transcendentals=0),
        name="grads",
    )(*parts, *rest)


def add_pair(x, axis, perm):
    return x + lax.ppermute(x, axis, perm)


def add_four(x, axis, shift):
    one, two, three = (lax.ppermute(x, axis, shift(s)) for s in (1, 2, 3))
    return (x + two) + (one + three)


def sum_all(grad_left, grad_right):
    core = lax.axis_index("tensor") % 2
    first = core == 0
    keep = jnp.where(first, grad_left, grad_right)
    give = jnp.where(first, grad_right, grad_left)
    swap = tensor_shift(0, 1)
    x = keep + lax.ppermute(give, "tensor", swap)
    x = add_four(x, "tensor", lambda s: tensor_shift(s, 0))
    x = add_four(x, "dp", x_shift)
    for b in (1, 2, 4):
        x = add_pair(x, "dp", z_flip(b))
    other = lax.ppermute(x, "tensor", swap)
    return jnp.where(first, x, other), jnp.where(first, other, x)


def exchange(act, cot):
    plan, first = [], 0
    for p, tokens in enumerate(PARTS):
        plan += [(p, first, tokens, hop) for hop in HOPS + ((0, 0),)]
        first += tokens
    lead = pack(act, cot, 0, PARTS[0], tuple(h for _, _, _, h in plan[:WINDOW]))
    act, cot, *lead = lax.optimization_barrier((act, cot, *lead))
    blocks = list(lead)
    blocks += pack(act, cot, 0, PARTS[0], (HOPS + ((0, 0),))[WINDOW:])
    first = PARTS[0]
    for tokens in PARTS[1:]:
        blocks += pack(act, cot, first, tokens, HOPS + ((0, 0),))
        first += tokens
    got, sent = [], []
    for (p, _, _, (dy, dc)), block in zip(plan, blocks):
        if (dy, dc) != (0, 0):
            if len(sent) >= WINDOW:
                w = sent[-WINDOW]
                block, got[w] = lax.optimization_barrier((block, got[w]))
            block = lax.ppermute(block, "tensor", tensor_shift(dy, dc))
            sent.append(len(got))
        got.append(block)
    return [got[8 * p : 8 * p + 8] for p in range(len(PARTS))]


def on_device(activations, cotangent, left_factor, right_factor, scale_power, grid_bits):
    act, cot = (x.reshape(8, -1, ROWS, 128) for x in (activations, cotangent))
    step_size = jnp.exp2(scale_power.astype(F32))
    half_grid = jnp.exp2((grid_bits - 1).astype(F32))
    lower = -half_grid * step_size
    upper = (half_grid - 1.0) * step_size
    grads = jnp.zeros((128, 128), F32), jnp.zeros((128, 128), F32)
    for part in exchange(act, cot):
        grads = local_grads(part, left_factor, left_factor.T, right_factor, lower, upper, *grads)
    return sum_all(*grads)


def solution(mesh):
    return jax.shard_map(
        on_device,
        mesh=mesh,
        in_specs=(P("dp", "tensor", None), P("dp", "tensor", None), P(), P(), P(), P()),
        out_specs=(P(), P()),
        check_vma=False,
    )
```

time: 113 us -> 98.6 us (0.87)
  blocking collectives: 33.2 us -> 0 us
  starting transfers between devices: 29.7 us -> 51 us
  waiting for transfers between devices: 43.1 us -> 31.4 us
  Pallas kernels: 5.29 us -> 13.2 us
    all_to_all x1 -> x0, blocking collectives: 33.2 us -> none  [exchange(): lax.all_to_all(x.reshape(8, -1, 16, 128), 'tensor', 0, 0, tiled=False)]
    all_to_all x1 -> x0, waiting for transfers between devices: 26.3 us -> none  [exchange(): lax.all_to_all(x.reshape(8, -1, 16, 128), 'tensor', 0, 0, tiled=False)]
    ppermute x0 -> x14, starting transfers between devices: none -> 22.8 us  [exchange(): block = lax.ppermute(block, 'tensor', tensor_shift(dy, dc))]
    ppermute x0 -> x14, waiting for transfers between devices: none -> 18.2 us  [exchange(): block = lax.ppermute(block, 'tensor', tensor_shift(dy, dc))]
    pallas_call x1 -> x5, Pallas kernels: 5.29 us -> 13.2 us  [the longest x3 7.83 us: pack(): pl.pallas_call(functools.partial(pack_kernel, first, hops), in_specs=[pl....]
    all_to_all x1 -> x0, starting transfers between devices: 5.4 us -> none  [exchange(): lax.all_to_all(x.reshape(8, -1, 16, 128), 'tensor', 0, 0, tiled=False)]
    ppermute x6, waiting for transfers between devices: 8.94 us -> 6.43 us  [add_four(): one, two, three = (lax.ppermute(x, axis, shift(s)) for s in (1, 2, 3))]
    ppermute x6, starting transfers between devices: 6.27 us -> 8.65 us  [add_four(): one, two, three = (lax.ppermute(x, axis, shift(s)) for s in (1, 2, 3))]
  transfers between devices with their start and end apart: 12 -> 25, of which waited for: 10 -> 14; matrix products, arithmetic and copies ran while one was open for 0% -> 0% of each run, Pallas kernels for 0% -> 8%
where the time goes in v2:
time: 98.6 us; the launch traced here: 98.4 us
  starting transfers between devices  51 us (52%)
  waiting for transfers between devices  31.4 us (32%)
  Pallas kernels  13.2 us (13%)
  local copies, waits for them, and re-layouts  1.1 us (1%)
    ppermute x14, starting transfers between devices, exchange(): block = lax.ppermute(block, 'tensor', tensor_shift(dy, dc))  22.8 us
    ppermute x14, waiting for transfers between devices, exchange(): block = lax.ppermute(block, 'tensor', tensor_shift(dy, dc))  18.2 us
    ppermute x3, starting transfers between devices, add_pair(): return x + lax.ppermute(x, axis, perm)  11.5 us
    ppermute x6, starting transfers between devices, add_four(): one, two, three = (lax.ppermute(x, axis, shift(s)) for s in (1, 2, 3))  8.65 us
    pallas_call x3, Pallas kernels, pack(): pl.pallas_call(functools.partial(pack_kernel, first, hops), in_specs=[pl....  7.83 us
    ppermute x1, starting transfers between devices, sum_all(): other = lax.ppermute(x, 'tensor', swap)  7.6 us
    ppermute x6, waiting for transfers between devices, add_four(): one, two, three = (lax.ppermute(x, axis, shift(s)) for s in (1, 2, 3))  6.43 us
    pallas_call x2, Pallas kernels, local_grads(): pl.pallas_call(grads_kernel, in_specs=[pl.BlockSpec(memory_space=pltpu.VM...  5.41 us
  transfers between devices with their start and end apart: 25, of which 14 were waited for; matrix products, arithmetic and copies ran while one was open for 0% of the time, Pallas kernels for 8%

profile of v2, /device:TPU:1, one launch (start us, length us, event | category | flops | bytes accessed | tf_op | source)
XLA Modules:
  0.0 98.4 jit_solution(16445112645360381852)
XLA Ops:
  0.6 2.5 %pack.3 = (bf16[2,32,16,128]{3,2,1,0:T(8,128)(2,1)}, bf16[2,32,16,128]{3,2,1,0:T(8,128)(2,1)}, bf16[2,32,16,128]{3,2,1,0:T(8,128)(2,1)}, bf16[2,32,16,128]{3,2,1,0:T(8,128)(2,1)}, bf16[2,32,16,128]{3,2,1,0:T(8,128)(2,1)}) custom-call(bf16[8,64,16,128]{3,2,1,0:T(8,128)(2,1)} %bitcast.5, bf16[8,64,16,128]{3,2,1,0:T(8,128)(2,1)} %bitcast.8), custom_call_target="tpu_custom_call" | custom-call | bytes 2621440 | tf_op jit(solution)/shard_map/pack/pallas_call | solution.py:59
  3.2 3.8 %collective-permute-start = (bf16[2,32,16,128]{3,2,1,0:T(8,128)(2,1)}, bf16[2,32,16,128]{3,2,1,0:T(8,128)(2,1)S(1)}, u32[]{:S(2)}, u32[]{:S(2)}) collective-permute-start(bf16[2,32,16,128]{3,2,1,0:T(8,128)(2,1)} %get-tuple-element.56), channel_id=1, source_target_pairs={{0,4},{1,5},{2,6},{3,7},{4,0},{5,1},{6,2},{7,3},{8,12},{9,13},{10,... | collective-permute-start | bytes 786440 | tf_op jit(solution)/shard_map/ppermute | solution.py:161
  7.0 2.6 %collective-permute-start.2 = (bf16[2,32,16,128]{3,2,1,0:T(8,128)(2,1)}, bf16[2,32,16,128]{3,2,1,0:T(8,128)(2,1)S(1)}, u32[]{:S(2)}, u32[]{:S(2)}) collective-permute-start(bf16[2,32,16,128]{3,2,1,0:T(8,128)(2,1)} %get-tuple-element.61), channel_id=1, source_target_pairs={{0,5},{1,4},{2,7},{3,6},{4,1},{5,0},{6,3},{7,2},{8,13},{9,12},{10,... | collective-permute-start | bytes 786440 | tf_op jit(solution)/shard_map/ppermute | solution.py:161
  9.6 2.7 %collective-permute-start.9 = (bf16[2,32,16,128]{3,2,1,0:T(8,128)(2,1)}, bf16[2,32,16,128]{3,2,1,0:T(8,128)(2,1)S(1)}, u32[]{:S(2)}, u32[]{:S(2)}) collective-permute-start(bf16[2,32,16,128]{3,2,1,0:T(8,128)(2,1)} %get-tuple-element.74), channel_id=1, source_target_pairs={{0,6},{1,7},{2,0},{3,1},{4,2},{5,3},{6,4},{7,5},{8,14},{9,15},{10,... | collective-permute-start | bytes 786440 | tf_op jit(solution)/shard_map/ppermute | solution.py:161
  12.3 3.1 %pack.4 = (bf16[2,32,16,128]{3,2,1,0:T(8,128)(2,1)}, bf16[2,32,16,128]{3,2,1,0:T(8,128)(2,1)}, bf16[2,32,16,128]{3,2,1,0:T(8,128)(2,1)}, bf16[2,32,16,128]{3,2,1...) custom-call(bf16[8,64,16,128]{3,2,1,0:T(8,128)(2,1)} %bitcast.6, ...), custom_call_target="tpu_custom_call" | custom-call | bytes 4194304 | tf_op jit(solution)/shard_map/pack/pallas_call | solution.py:59
  15.4 0.0 copy-start
  15.5 2.2 %pack.5 = (bf16[2,32,16,128]{3,2,1,0:T(8,128)(2,1)}, bf16[2,32,16,128]{3,2,1,0:T(8,128)(2,1)}, bf16[2,32,16,128]{3,2,1,0:T(8,128)(2,1)}) custom-call(bf16[8,64,16,128]{3,2,1,0:T(8,128)(2,1)} %bitcast.7, bf16[8,64,16,128]{3,2,1,0:T(8,128)(2,1)} %bitcast.10), custom_call_target="tpu_custom_call" | custom-call | bytes 1572864 | tf_op jit(solution)/shard_map/pack/pallas_call | solution.py:59
  17.7 0.1 collective-permute-start.1
  17.8 3.7 %collective-permute-done.2.refs_3_ = bf16[2,32,16,128]{3,2,1,0:T(8,128)(2,1)S(1)} collective-permute-done((bf16[2,32,16,128]{3,2,1,0:T(8,128)(2,1)}, bf16[2,32,16,128]{3,2,1,0:T(8,128)(2,1)S(1)}, u32[]{:S(2)}, u32[]{:S(2)}) %collective-permute-start.2) | collective-permute-done | bytes 262176 | tf_op jit(solution)/shard_map/ppermute | solution.py:161
  21.5 1.9 %collective-permute-start.3 = (bf16[2,32,16,128]{3,2,1,0:T(8,128)(2,1)}, bf16[2,32,16,128]{3,2,1,0:T(8,128)(2,1)S(1)}, u32[]{:S(2)}, u32[]{:S(2)}) collective-permute-start(bf16[2,32,16,128]{3,2,1,0:T(8,128)(2,1)} %get-tuple-element.62), channel_id=1, source_target_pairs={{0,6},{1,7},{2,0},{3,1},{4,2},{5,3},{6,4},{7,5},{8,14},{9,15},{10,... | collective-permute-start | bytes 786440 | tf_op jit(solution)/shard_map/ppermute | solution.py:161
  23.4 2.1 %collective-permute-done.6.refs_0_ = bf16[2,32,16,128]{3,2,1,0:T(8,128)(2,1)S(1)} collective-permute-done((bf16[2,32,16,128]{3,2,1,0:T(8,128)(2,1)}, bf16[2,32,16,128]{3,2,1,0:T(8,128)(2,1)S(1)}, u32[]{:S(2)}, u32[]{:S(2)}) %collective-permute-start.6) | collective-permute-done | bytes 262176 | tf_op jit(solution)/shard_map/ppermute | solution.py:161
  25.5 2.7 %collective-permute-start.7 = (bf16[2,32,16,128]{3,2,1,0:T(8,128)(2,1)}, bf16[2,32,16,128]{3,2,1,0:T(8,128)(2,1)S(1)}, u32[]{:S(2)}, u32[]{:S(2)}) collective-permute-start(bf16[2,32,16,128]{3,2,1,0:T(8,128)(2,1)} %get-tuple-element.70), channel_id=1, source_target_pairs={{0,3},{1,2},{2,5},{3,4},{4,7},{5,6},{6,1},{7,0},{8,11},{9,10},{10,... | collective-permute-start | bytes 786440 | tf_op jit(solution)/shard_map/ppermute | solution.py:161
  28.2 0.2 collective-permute-start.10
  28.5 0.1 copy.8
  28.6 1.7 %collective-permute-start.5 = (bf16[2,32,16,128]{3,2,1,0:T(8,128)(2,1)}, bf16[2,32,16,128]{3,2,1,0:T(8,128)(2,1)S(1)}, u32[]{:S(2)}, u32[]{:S(2)}) collective-permute-start(bf16[2,32,16,128]{3,2,1,0:T(8,128)(2,1)} %get-tuple-element.66), channel_id=1, source_target_pairs={{0,4},{1,5},{2,6},{3,7},{4,0},{5,1},{6,2},{7,3},{8,12},{9,13},{10,... | collective-permute-start | bytes 786440 | tf_op jit(solution)/shard_map/ppermute | solution.py:161
  30.3 0.7 collective-permute-done.1.refs_0_
  30.9 5.9 %collective-permute-done.7.refs_5_ = bf16[2,32,16,128]{3,2,1,0:T(8,128)(2,1)S(1)} collective-permute-done((bf16[2,32,16,128]{3,2,1,0:T(8,128)(2,1)}, bf16[2,32,16,128]{3,2,1,0:T(8,128)(2,1)S(1)}, u32[]{:S(2)}, u32[]{:S(2)}) %collective-permute-start.7) | collective-permute-done | bytes 262176 | tf_op jit(solution)/shard_map/ppermute | solution.py:161
  36.8 4.1 %collective-permute-start.8 = (bf16[2,32,16,128]{3,2,1,0:T(8,128)(2,1)}, bf16[2,32,16,128]{3,2,1,0:T(8,128)(2,1)S(1)}, u32[]{:S(2)}, u32[]{:S(2)}) collective-permute-start(bf16[2,32,16,128]{3,2,1,0:T(8,128)(2,1)} %get-tuple-element.71), channel_id=1, source_target_pairs={{0,5},{1,4},{2,7},{3,6},{4,1},{5,0},{6,3},{7,2},{8,13},{9,12},{10,... | collective-permute-start | bytes 786440 | tf_op jit(solution)/shard_map/ppermute | solution.py:161
  40.9 0.1 collective-permute-start.11
  41.0 3.0 %collective-permute-start.13 = (bf16[2,32,16,128]{3,2,1,0:T(8,128)(2,1)S(1)}, bf16[2,32,16,128]{3,2,1,0:T(8,128)(2,1)S(1)}, u32[]{:S(2)}, u32[]{:S(2)}) collective-permute-start(bf16[2,32,16,128]{3,2,1,0:T(8,128)(2,1)S(1)} %copy-done.6), channel_id=1, source_target_pairs={{0,7},{1,6},{2,1},{3,0},{4,3},{5,2},{6,5},{7,4},{8,15},{9,14},{10,... | collective-permute-start | bytes 786440 | tf_op jit(solution)/shard_map/ppermute | solution.py:161
  44.0 0.9 copy-done.2
  45.0 2.7 %grads.2 = (f32[128,128]{1,0:T(8,128)S(1)}, f32[128,128]{1,0:T(8,128)S(1)}) custom-call(bf16[2,32,16,128]{3,2,1,0:T(8,128)(2,1)S(1)} %collective-permute-done.6.refs_0_, bf16[2,32,16,128]{3,2,1,0:T(8,128)(2,1)S(1)} %collective-permute-done.9.refs_1_, bf16[2,32,16,128]{3,2,1,0:T(8,128)(2,1)S(1)} %collective-permute-done.refs_2_, ...), custom_call_target="tpu_custom_call" | custom-call | flops 671088640 | bytes 2097152 | tf_op jit(solution)/shard_map/grads/pallas_call | solution.py:106
  47.7 0.3 collective-permute-done.8.refs_3_
  48.0 5.5 %collective-permute-done.12.refs_5_ = bf16[2,32,16,128]{3,2,1,0:T(8,128)(2,1)S(1)} collective-permute-done((bf16[2,32,16,128]{3,2,1,0:T(8,128)(2,1)S(1)}, bf16[2,32,16,128]{3,2,1,0:T(8,128)(2,1)S(1)}, u32[]{:S(2)}, u32[]{:S(2)}) %collective-permute-start.12) | collective-permute-done | bytes 262176 | tf_op jit(solution)/shard_map/ppermute | solution.py:161
  53.5 0.0 collective-permute-done.13.refs_6_
  53.6 2.7 %grads.3 = (f32[128,128]{1,0:T(8,128)S(1)}, f32[128,128]{1,0:T(8,128)S(1)}) custom-call(bf16[2,32,16,128]{3,2,1,0:T(8,128)(2,1)S(1)} %collective-permute-done.1.refs_0_, bf16[2,32,16,128]{3,2,1,0:T(8,128)(2,1)S(1)} %collective-permute-done.3.refs_1_, bf16[2,32,16,128]{3,2,1,0:T(8,128)(2,1)S(1)} %collective-permute-done.5.refs_2_, ...), custom_call_target="tpu_custom_call" | custom-call | flops 671088640 | bytes 2097152 | tf_op jit(solution)/shard_map/grads/pallas_call | solution.py:106
  56.3 0.5 collective-permute-start.14
  56.7 0.9 collective-permute-done.14
  57.7 1.3 %collective-permute-start.16 = (f32[128,128]{1,0:T(8,128)S(1)}, f32[128,128]{1,0:T(8,128)S(1)}, u32[]{:S(2)}, u32[]{:S(2)}) collective-permute-start(f32[128,128]{1,0:T(8,128)S(1)} %select_add_fusion), channel_id=1, source_target_pairs={{0,2},{1,3},{2,4},{3,5},{4,6},{5,7},{6,0},{7,1},{8,10},{9,11},{10,... | collective-permute-start | bytes 196616 | tf_op jit(solution)/shard_map/ppermute | solution.py:123
  59.0 1.5 %collective-permute-start.17 = (f32[128,128]{1,0:T(8,128)S(1)}, f32[128,128]{1,0:T(8,128)S(1)}, u32[]{:S(2)}, u32[]{:S(2)}) collective-permute-start(f32[128,128]{1,0:T(8,128)S(1)} %select_add_fusion), channel_id=1, source_target_pairs={{0,6},{1,7},{2,0},{3,1},{4,2},{5,3},{6,4},{7,5},{8,14},{9,15},{10,... | collective-permute-start | bytes 196616 | tf_op jit(solution)/shard_map/ppermute | solution.py:123
  60.5 1.6 %collective-permute-start.15 = (f32[128,128]{1,0:T(8,128)S(1)}, f32[128,128]{1,0:T(8,128)S(1)}, u32[]{:S(2)}, u32[]{:S(2)}) collective-permute-start(f32[128,128]{1,0:T(8,128)S(1)} %select_add_fusion), channel_id=1, source_target_pairs={{0,4},{1,5},{2,6},{3,7},{4,0},{5,1},{6,2},{7,3},{8,12},{9,13},{10,... | collective-permute-start | bytes 196616 | tf_op jit(solution)/shard_map/ppermute | solution.py:123
  62.0 0.0 collective-permute-done.16
  62.1 0.0 collective-permute-done.17
  62.1 3.0 %collective-permute-done.15 = f32[128,128]{1,0:T(8,128)S(1)} collective-permute-done((f32[128,128]{1,0:T(8,128)S(1)}, f32[128,128]{1,0:T(8,128)S(1)}, u32[]{:S(2)}, u32[]{:S(2)}) %collective-permute-start.15) | collective-permute-done | bytes 65568 | tf_op jit(solution)/shard_map/ppermute | solution.py:123
  65.1 1.3 %collective-permute-start.19 = (f32[128,128]{1,0:T(8,128)S(1)}, f32[128,128]{1,0:T(8,128)S(1)}, u32[]{:S(2)}, u32[]{:S(2)}) collective-permute-start(f32[128,128]{1,0:T(8,128)S(1)} %add_add_fusion.1), channel_id=1, source_target_pairs={{0,8},{8,16},{16,24},{24,0},{32,40},{40,48},{48,56},{56,32},{64,72... | collective-permute-start | bytes 196616 | tf_op jit(solution)/shard_map/ppermute | solution.py:123
  66.4 1.5 %collective-permute-start.20 = (f32[128,128]{1,0:T(8,128)S(1)}, f32[128,128]{1,0:T(8,128)S(1)}, u32[]{:S(2)}, u32[]{:S(2)}) collective-permute-start(f32[128,128]{1,0:T(8,128)S(1)} %add_add_fusion.1), channel_id=1, source_target_pairs={{0,24},{8,0},{16,8},{24,16},{32,56},{40,32},{48,40},{56,48},{64,88... | collective-permute-start | bytes 196616 | tf_op jit(solution)/shard_map/ppermute | solution.py:123
  67.9 1.5 %collective-permute-start.18 = (f32[128,128]{1,0:T(8,128)S(1)}, f32[128,128]{1,0:T(8,128)S(1)}, u32[]{:S(2)}, u32[]{:S(2)}) collective-permute-start(f32[128,128]{1,0:T(8,128)S(1)} %add_add_fusion.1), channel_id=1, source_target_pairs={{0,16},{8,24},{16,0},{24,8},{32,48},{40,56},{48,32},{56,40},{64,80... | collective-permute-start | bytes 196616 | tf_op jit(solution)/shard_map/ppermute | solution.py:123
  69.4 0.1 collective-permute-done.19
  69.5 3.3 %collective-permute-done.18 = f32[128,128]{1,0:T(8,128)S(1)} collective-permute-done((f32[128,128]{1,0:T(8,128)S(1)}, f32[128,128]{1,0:T(8,128)S(1)}, u32[]{:S(2)}, u32[]{:S(2)}) %collective-permute-start.18) | collective-permute-done | bytes 65568 | tf_op jit(solution)/shard_map/ppermute | solution.py:123
  72.8 1.7 %collective-permute-start.21 = (f32[128,128]{1,0:T(8,128)S(1)}, f32[128,128]{1,0:T(8,128)S(1)}, u32[]{:S(2)}, u32[]{:S(2)}) collective-permute-start(f32[128,128]{1,0:T(8,128)S(1)} %add_add_fusion), channel_id=1, source_target_pairs={{0,32},{8,40},{16,48},{24,56},{32,0},{40,8},{48,16},{56,24},{64,96... | collective-permute-start | bytes 196616 | tf_op jit(solution)/shard_map/ppermute | solution.py:119
  74.5 1.7 %collective-permute-done.21 = f32[128,128]{1,0:T(8,128)S(1)} collective-permute-done((f32[128,128]{1,0:T(8,128)S(1)}, f32[128,128]{1,0:T(8,128)S(1)}, u32[]{:S(2)}, u32[]{:S(2)}) %collective-permute-start.21) | collective-permute-done | bytes 65568 | tf_op jit(solution)/shard_map/ppermute | solution.py:119
  76.2 3.1 %collective-permute-start.22 = (f32[128,128]{1,0:T(8,128)S(1)}, f32[128,128]{1,0:T(8,128)S(1)}, u32[]{:S(2)}, u32[]{:S(2)}) collective-permute-start(f32[128,128]{1,0:T(8,128)S(1)} %add.44), channel_id=1, source_target_pairs={{0,64},{8,72},{16,80},{24,88},{32,96},{40,104},{48,112},{56,120},{... | collective-permute-start | bytes 196616 | tf_op jit(solution)/shard_map/ppermute | solution.py:119
  79.3 1.7 %collective-permute-done.22 = f32[128,128]{1,0:T(8,128)S(1)} collective-permute-done((f32[128,128]{1,0:T(8,128)S(1)}, f32[128,128]{1,0:T(8,128)S(1)}, u32[]{:S(2)}, u32[]{:S(2)}) %collective-permute-start.22) | collective-permute-done | bytes 65568 | tf_op jit(solution)/shard_map/ppermute | solution.py:119
  80.9 6.7 %collective-permute-start.23 = (f32[128,128]{1,0:T(8,128)S(1)}, f32[128,128]{1,0:T(8,128)S(1)}, u32[]{:S(2)}, u32[]{:S(2)}) collective-permute-start(f32[128,128]{1,0:T(8,128)S(1)} %add.45), channel_id=1, source_target_pairs={{0,128},{8,136},{16,144},{24,152},{32,160},{40,168},{48,176},{56,1... | collective-permute-start | bytes 196616 | tf_op jit(solution)/shard_map/ppermute | solution.py:119
  87.6 1.7 %collective-permute-done.23 = f32[128,128]{1,0:T(8,128)S(1)} collective-permute-done((f32[128,128]{1,0:T(8,128)S(1)}, f32[128,128]{1,0:T(8,128)S(1)}, u32[]{:S(2)}, u32[]{:S(2)}) %collective-permute-start.23) | collective-permute-done | bytes 65568 | tf_op jit(solution)/shard_map/ppermute | solution.py:119
  89.3 7.6 %collective-permute-start.24 = (f32[128,128]{1,0:T(8,128)S(1)}, f32[128,128]{1,0:T(8,128)S(1)}, u32[]{:S(2)}, u32[]{:S(2)}) collective-permute-start(f32[128,128]{1,0:T(8,128)S(1)} %add.46), channel_id=1, source_target_pairs={{0,1},{1,0},{2,3},{3,2},{4,5},{5,4},{6,7},{7,6},{8,9},{9,8},{10,11... | collective-permute-start | bytes 196616 | tf_op jit(solution)/shard_map/ppermute | solution.py:138
  96.9 0.9 collective-permute-done.24
  97.8 0.7 broadcast_select_fusion
  (34 shorter events, 0.2 us)
Async XLA Ops:
  3.2 14.5 %collective-permute-start = (bf16[2,32,16,128]{3,2,1,0:T(8,128)(2,1)}, bf16[2,32,16,128]{3,2,1,0:T(8,128)(2,1)S(1)}, u32[]{:S(2)}, u32[]{:S(2)}) collective-permute-start(bf16[2,32,16,128]{3,2,1,0:T(8,128)(2,1)} %get-tuple-element.56), channel_id=1, source_target_pairs={{0,4},{1,5},{2,6},{3,7},{4,0},{5,1},{6,2},{7,3},{8,12},{9,13},{10,... | collective-permute-start | bytes 786440 | tf_op jit(solution)/shard_map/ppermute | solution.py:161
  7.0 14.5 %collective-permute-start.2 = (bf16[2,32,16,128]{3,2,1,0:T(8,128)(2,1)}, bf16[2,32,16,128]{3,2,1,0:T(8,128)(2,1)S(1)}, u32[]{:S(2)}, u32[]{:S(2)}) collective-permute-start(bf16[2,32,16,128]{3,2,1,0:T(8,128)(2,1)} %get-tuple-element.61), channel_id=1, source_target_pairs={{0,5},{1,4},{2,7},{3,6},{4,1},{5,0},{6,3},{7,2},{8,13},{9,12},{10,... | collective-permute-start | bytes 786440 | tf_op jit(solution)/shard_map/ppermute | solution.py:161
  9.6 15.9 %collective-permute-start.6 = (bf16[2,32,16,128]{3,2,1,0:T(8,128)(2,1)}, bf16[2,32,16,128]{3,2,1,0:T(8,128)(2,1)S(1)}, u32[]{:S(2)}, u32[]{:S(2)}) collective-permute-start(bf16[2,32,16,128]{3,2,1,0:T(8,128)(2,1)} %get-tuple-element.69), channel_id=1, source_target_pairs={{0,2},{1,3},{2,4},{3,5},{4,6},{5,7},{6,0},{7,1},{8,10},{9,11},{10,... | collective-permute-start | bytes 786440 | tf_op jit(solution)/shard_map/ppermute | solution.py:161
  9.6 18.6 %collective-permute-start.9 = (bf16[2,32,16,128]{3,2,1,0:T(8,128)(2,1)}, bf16[2,32,16,128]{3,2,1,0:T(8,128)(2,1)S(1)}, u32[]{:S(2)}, u32[]{:S(2)}) collective-permute-start(bf16[2,32,16,128]{3,2,1,0:T(8,128)(2,1)} %get-tuple-element.74), channel_id=1, source_target_pairs={{0,6},{1,7},{2,0},{3,1},{4,2},{5,3},{6,4},{7,5},{8,14},{9,15},{10,... | collective-permute-start | bytes 786440 | tf_op jit(solution)/shard_map/ppermute | solution.py:161
  12.3 16.3 %collective-permute-start.4 = (bf16[2,32,16,128]{3,2,1,0:T(8,128)(2,1)}, bf16[2,32,16,128]{3,2,1,0:T(8,128)(2,1)S(1)}, u32[]{:S(2)}, u32[]{:S(2)}) collective-permute-start(bf16[2,32,16,128]{3,2,1,0:T(8,128)(2,1)} %get-tuple-element.65), channel_id=1, source_target_pairs={{0,1},{1,0},{2,3},{3,2},{4,5},{5,4},{6,7},{7,6},{8,9},{9,8},{10,11... | collective-permute-start | bytes 786440 | tf_op jit(solution)/shard_map/ppermute | solution.py:161
  15.4 13.1 %copy-start = (bf16[128,128]{1,0:T(8,128)(2,1)S(1)}, bf16[128,128]{1,0:T(8,128)(2,1)}, u32[]{:S(2)}) copy-start(bf16[128,128]{1,0:T(8,128)(2,1)} %refs_8_.3) | copy-start | bytes 98308
  15.4 25.6 %copy-start.7 = (bf16[2,32,16,128]{3,2,1,0:T(8,128)(2,1)S(1)}, bf16[2,32,16,128]{3,2,1,0:T(8,128)(2,1)}, u32[]{:S(2)}) copy-start(bf16[2,32,16,128]{3,2,1,0:T(8,128)(2,1)} %get-tuple-element.77) | copy-start | bytes 786436
  15.4 25.6 %copy-start.6 = (bf16[2,32,16,128]{3,2,1,0:T(8,128)(2,1)S(1)}, bf16[2,32,16,128]{3,2,1,0:T(8,128)(2,1)}, u32[]{:S(2)}) copy-start(bf16[2,32,16,128]{3,2,1,0:T(8,128)(2,1)} %get-tuple-element.78) | copy-start | bytes 786436
  15.4 28.5 %copy-start.4 = (s32[128,128]{1,0:T(8,128)S(1)}, s32[128,128]{1,0:T(8,128)}, u32[]{:S(2)}) copy-start(s32[128,128]{1,0:T(8,128)} %param.10) | copy-start | bytes 196612
  15.4 28.5 %copy-start.5 = (s32[128,128]{1,0:T(8,128)S(1)}, s32[128,128]{1,0:T(8,128)}, u32[]{:S(2)}) copy-start(s32[128,128]{1,0:T(8,128)} %param.11) | copy-start | bytes 196612
  15.4 28.6 %copy-start.3 = (bf16[128,128]{1,0:T(8,128)(2,1)S(1)}, bf16[128,128]{1,0:T(8,128)(2,1)}, u32[]{:S(2)}) copy-start(bf16[128,128]{1,0:T(8,128)(2,1)} %refs_10_.3) | copy-start | bytes 98308
  17.7 35.9 %copy-start.1 = (bf16[2,32,16,128]{3,2,1,0:T(8,128)(2,1)S(1)}, bf16[2,32,16,128]{3,2,1,0:T(8,128)(2,1)}, u32[]{:S(2)}) copy-start(bf16[2,32,16,128]{3,2,1,0:T(8,128)(2,1)} %get-tuple-element.79.refs_7_) | copy-start | bytes 786436
  17.7 13.2 %collective-permute-start.1 = (bf16[2,32,16,128]{3,2,1,0:T(8,128)(2,1)}, bf16[2,32,16,128]{3,2,1,0:T(8,128)(2,1)S(1)}, u32[]{:S(2)}, u32[]{:S(2)}) collective-permute-start(bf16[2,32,16,128]{3,2,1,0:T(8,128)(2,1)} %get-tuple-element.57), channel_id=1, source_target_pairs={{0,2},{1,3},{2,4},{3,5},{4,6},{5,7},{6,0},{7,1},{8,10},{9,11},{10,... | collective-permute-start | bytes 786440 | tf_op jit(solution)/shard_map/ppermute | solution.py:161
  21.5 9.5 %collective-permute-start.3 = (bf16[2,32,16,128]{3,2,1,0:T(8,128)(2,1)}, bf16[2,32,16,128]{3,2,1,0:T(8,128)(2,1)S(1)}, u32[]{:S(2)}, u32[]{:S(2)}) collective-permute-start(bf16[2,32,16,128]{3,2,1,0:T(8,128)(2,1)} %get-tuple-element.62), channel_id=1, source_target_pairs={{0,6},{1,7},{2,0},{3,1},{4,2},{5,3},{6,4},{7,5},{8,14},{9,15},{10,... | collective-permute-start | bytes 786440 | tf_op jit(solution)/shard_map/ppermute | solution.py:161
  25.5 11.3 %collective-permute-start.7 = (bf16[2,32,16,128]{3,2,1,0:T(8,128)(2,1)}, bf16[2,32,16,128]{3,2,1,0:T(8,128)(2,1)S(1)}, u32[]{:S(2)}, u32[]{:S(2)}) collective-permute-start(bf16[2,32,16,128]{3,2,1,0:T(8,128)(2,1)} %get-tuple-element.70), channel_id=1, source_target_pairs={{0,3},{1,2},{2,5},{3,4},{4,7},{5,6},{6,1},{7,0},{8,11},{9,10},{10,... | collective-permute-start | bytes 786440 | tf_op jit(solution)/shard_map/ppermute | solution.py:161
  28.2 12.7 %collective-permute-start.10 = (bf16[2,32,16,128]{3,2,1,0:T(8,128)(2,1)}, bf16[2,32,16,128]{3,2,1,0:T(8,128)(2,1)S(1)}, u32[]{:S(2)}, u32[]{:S(2)}) collective-permute-start(bf16[2,32,16,128]{3,2,1,0:T(8,128)(2,1)} %get-tuple-element.75), channel_id=1, source_target_pairs={{0,7},{1,6},{2,1},{3,0},{4,3},{5,2},{6,5},{7,4},{8,15},{9,14},{10,... | collective-permute-start | bytes 786440 | tf_op jit(solution)/shard_map/ppermute | solution.py:161
  28.6 19.1 %collective-permute-start.5 = (bf16[2,32,16,128]{3,2,1,0:T(8,128)(2,1)}, bf16[2,32,16,128]{3,2,1,0:T(8,128)(2,1)S(1)}, u32[]{:S(2)}, u32[]{:S(2)}) collective-permute-start(bf16[2,32,16,128]{3,2,1,0:T(8,128)(2,1)} %get-tuple-element.66), channel_id=1, source_target_pairs={{0,4},{1,5},{2,6},{3,7},{4,0},{5,1},{6,2},{7,3},{8,12},{9,13},{10,... | collective-permute-start | bytes 786440 | tf_op jit(solution)/shard_map/ppermute | solution.py:161
  36.8 11.2 %collective-permute-start.8 = (bf16[2,32,16,128]{3,2,1,0:T(8,128)(2,1)}, bf16[2,32,16,128]{3,2,1,0:T(8,128)(2,1)S(1)}, u32[]{:S(2)}, u32[]{:S(2)}) collective-permute-start(bf16[2,32,16,128]{3,2,1,0:T(8,128)(2,1)} %get-tuple-element.71), channel_id=1, source_target_pairs={{0,5},{1,4},{2,7},{3,6},{4,1},{5,0},{6,3},{7,2},{8,13},{9,12},{10,... | collective-permute-start | bytes 786440 | tf_op jit(solution)/shard_map/ppermute | solution.py:161
  40.9 7.1 %collective-permute-start.11 = (bf16[2,32,16,128]{3,2,1,0:T(8,128)(2,1)}, bf16[2,32,16,128]{3,2,1,0:T(8,128)(2,1)S(1)}, u32[]{:S(2)}, u32[]{:S(2)}) collective-permute-start(bf16[2,32,16,128]{3,2,1,0:T(8,128)(2,1)} %get-tuple-element.76), channel_id=1, source_target_pairs={{0,1},{1,0},{2,3},{3,2},{4,5},{5,4},{6,7},{7,6},{8,9},{9,8},{10,11... | collective-permute-start | bytes 786440 | tf_op jit(solution)/shard_map/ppermute | solution.py:161
  41.0 12.5 %collective-permute-start.12 = (bf16[2,32,16,128]{3,2,1,0:T(8,128)(2,1)S(1)}, bf16[2,32,16,128]{3,2,1,0:T(8,128)(2,1)S(1)}, u32[]{:S(2)}, u32[]{:S(2)}) collective-permute-start(bf16[2,32,16,128]{3,2,1,0:T(8,128)(2,1)S(1)} %copy-done.7), channel_id=1, source_target_pairs={{0,3},{1,2},{2,5},{3,4},{4,7},{5,6},{6,1},{7,0},{8,11},{9,10},{10,... | collective-permute-start | bytes 786440 | tf_op jit(solution)/shard_map/ppermute | solution.py:161
  41.0 12.5 %collective-permute-start.13 = (bf16[2,32,16,128]{3,2,1,0:T(8,128)(2,1)S(1)}, bf16[2,32,16,128]{3,2,1,0:T(8,128)(2,1)S(1)}, u32[]{:S(2)}, u32[]{:S(2)}) collective-permute-start(bf16[2,32,16,128]{3,2,1,0:T(8,128)(2,1)S(1)} %copy-done.6), channel_id=1, source_target_pairs={{0,7},{1,6},{2,1},{3,0},{4,3},{5,2},{6,5},{7,4},{8,15},{9,14},{10,... | collective-permute-start | bytes 786440 | tf_op jit(solution)/shard_map/ppermute | solution.py:161
  44.0 1.0 copy-start.2
  56.3 1.4 %collective-permute-start.14 = (f32[128,128]{1,0:T(8,128)S(1)}, f32[128,128]{1,0:T(8,128)S(1)}, u32[]{:S(2)}, u32[]{:S(2)}) collective-permute-start(f32[128,128]{1,0:T(8,128)S(1)} %broadcast_select_fusion.2), channel_id=1, source_target_pairs={{0,1},{1,0},{2,3},{3,2},{4,5},{5,4},{6,7},{7,6},{8,9},{9,8},{10,11... | collective-permute-start | bytes 196616 | tf_op jit(solution)/shard_map/ppermute | solution.py:133
  57.7 4.4 %collective-permute-start.16 = (f32[128,128]{1,0:T(8,128)S(1)}, f32[128,128]{1,0:T(8,128)S(1)}, u32[]{:S(2)}, u32[]{:S(2)}) collective-permute-start(f32[128,128]{1,0:T(8,128)S(1)} %select_add_fusion), channel_id=1, source_target_pairs={{0,2},{1,3},{2,4},{3,5},{4,6},{5,7},{6,0},{7,1},{8,10},{9,11},{10,... | collective-permute-start | bytes 196616 | tf_op jit(solution)/shard_map/ppermute | solution.py:123
  59.0 3.1 %collective-permute-start.17 = (f32[128,128]{1,0:T(8,128)S(1)}, f32[128,128]{1,0:T(8,128)S(1)}, u32[]{:S(2)}, u32[]{:S(2)}) collective-permute-start(f32[128,128]{1,0:T(8,128)S(1)} %select_add_fusion), channel_id=1, source_target_pairs={{0,6},{1,7},{2,0},{3,1},{4,2},{5,3},{6,4},{7,5},{8,14},{9,15},{10,... | collective-permute-start | bytes 196616 | tf_op jit(solution)/shard_map/ppermute | solution.py:123
  60.5 4.6 %collective-permute-start.15 = (f32[128,128]{1,0:T(8,128)S(1)}, f32[128,128]{1,0:T(8,128)S(1)}, u32[]{:S(2)}, u32[]{:S(2)}) collective-permute-start(f32[128,128]{1,0:T(8,128)S(1)} %select_add_fusion), channel_id=1, source_target_pairs={{0,4},{1,5},{2,6},{3,7},{4,0},{5,1},{6,2},{7,3},{8,12},{9,13},{10,... | collective-permute-start | bytes 196616 | tf_op jit(solution)/shard_map/ppermute | solution.py:123
  65.1 4.4 %collective-permute-start.19 = (f32[128,128]{1,0:T(8,128)S(1)}, f32[128,128]{1,0:T(8,128)S(1)}, u32[]{:S(2)}, u32[]{:S(2)}) collective-permute-start(f32[128,128]{1,0:T(8,128)S(1)} %add_add_fusion.1), channel_id=1, source_target_pairs={{0,8},{8,16},{16,24},{24,0},{32,40},{40,48},{48,56},{56,32},{64,72... | collective-permute-start | bytes 196616 | tf_op jit(solution)/shard_map/ppermute | solution.py:123
  66.4 3.1 %collective-permute-start.20 = (f32[128,128]{1,0:T(8,128)S(1)}, f32[128,128]{1,0:T(8,128)S(1)}, u32[]{:S(2)}, u32[]{:S(2)}) collective-permute-start(f32[128,128]{1,0:T(8,128)S(1)} %add_add_fusion.1), channel_id=1, source_target_pairs={{0,24},{8,0},{16,8},{24,16},{32,56},{40,32},{48,40},{56,48},{64,88... | collective-permute-start | bytes 196616 | tf_op jit(solution)/shard_map/ppermute | solution.py:123
  67.9 4.9 %collective-permute-start.18 = (f32[128,128]{1,0:T(8,128)S(1)}, f32[128,128]{1,0:T(8,128)S(1)}, u32[]{:S(2)}, u32[]{:S(2)}) collective-permute-start(f32[128,128]{1,0:T(8,128)S(1)} %add_add_fusion.1), channel_id=1, source_target_pairs={{0,16},{8,24},{16,0},{24,8},{32,48},{40,56},{48,32},{56,40},{64,80... | collective-permute-start | bytes 196616 | tf_op jit(solution)/shard_map/ppermute | solution.py:123
  72.8 3.4 %collective-permute-start.21 = (f32[128,128]{1,0:T(8,128)S(1)}, f32[128,128]{1,0:T(8,128)S(1)}, u32[]{:S(2)}, u32[]{:S(2)}) collective-permute-start(f32[128,128]{1,0:T(8,128)S(1)} %add_add_fusion), channel_id=1, source_target_pairs={{0,32},{8,40},{16,48},{24,56},{32,0},{40,8},{48,16},{56,24},{64,96... | collective-permute-start | bytes 196616 | tf_op jit(solution)/shard_map/ppermute | solution.py:119
  76.2 4.7 %collective-permute-start.22 = (f32[128,128]{1,0:T(8,128)S(1)}, f32[128,128]{1,0:T(8,128)S(1)}, u32[]{:S(2)}, u32[]{:S(2)}) collective-permute-start(f32[128,128]{1,0:T(8,128)S(1)} %add.44), channel_id=1, source_target_pairs={{0,64},{8,72},{16,80},{24,88},{32,96},{40,104},{48,112},{56,120},{... | collective-permute-start | bytes 196616 | tf_op jit(solution)/shard_map/ppermute | solution.py:119
  80.9 8.3 %collective-permute-start.23 = (f32[128,128]{1,0:T(8,128)S(1)}, f32[128,128]{1,0:T(8,128)S(1)}, u32[]{:S(2)}, u32[]{:S(2)}) collective-permute-start(f32[128,128]{1,0:T(8,128)S(1)} %add.45), channel_id=1, source_target_pairs={{0,128},{8,136},{16,144},{24,152},{32,160},{40,168},{48,176},{56,1... | collective-permute-start | bytes 196616 | tf_op jit(solution)/shard_map/ppermute | solution.py:119
  89.3 8.5 %collective-permute-start.24 = (f32[128,128]{1,0:T(8,128)S(1)}, f32[128,128]{1,0:T(8,128)S(1)}, u32[]{:S(2)}, u32[]{:S(2)}) collective-permute-start(f32[128,128]{1,0:T(8,128)S(1)} %add.46), channel_id=1, source_target_pairs={{0,1},{1,0},{2,3},{3,2},{4,5},{5,4},{6,7},{7,6},{8,9},{9,8},{10,11... | collective-permute-start | bytes 196616 | tf_op jit(solution)/shard_map/ppermute | solution.py:138

commit v3 on v2

--- a/solution.py
+++ b/solution.py
@@ -13,19 +13,15 @@
 ROWS = 16
 PARTS = (32, 32)
 WINDOW = 5
-HOPS = ((1, 0), (3, 0), (2, 0), (2, 1), (0, 1), (1, 1), (3, 1))
+HOPS = (
+    ((1, 0), (3, 0), (2, 0), (2, 1), (0, 1), (1, 1), (3, 1)),
+    ((1, 0), (3, 0), (2, 0), (2, 1), (0, 1), (1, 1), (3, 1)),
+)
+OWN = ((0, 0),)
 
 
 def tensor_shift(y, core):
     return [(i, ((i // 2 + y) % 4) * 2 + ((i % 2) ^ core)) for i in range(8)]
-
-
-def x_shift(s):
-    return [(i, (i // 4) * 4 + (i % 4 + s) % 4) for i in range(32)]
-
-
-def z_flip(b):
-    return [(i, ((i // 4) ^ b) * 4 + i % 4) for i in range(32)]
 
 
 def place():
@@ -67,7 +63,7 @@
     )(act, cot)
 
 
-def grads_kernel(*refs):
+def grads_kernel(hops, *refs):
     parts, refs = refs[:8], refs[8:]
     (left_ref, left_t_ref, right_ref, lower_ref, upper_ref, gl_in, gr_in), refs = refs[:7], refs[7:]
     gl_ref, gr_ref, act_all, cot_all = refs
@@ -76,7 +72,7 @@
     total = parts[0].shape[1]
     tokens = min(STEP_TOKENS, total)
     grad_left, grad_right = gl_in[...], gr_in[...]
-    for k, (dy, dc) in enumerate(HOPS + ((0, 0),)):
+    for k, (dy, dc) in enumerate(hops + OWN):
         source = peer(-dy, dc)
         for t in range(total):
             rows = pl.ds(pl.multiple_of(t * 128 + source * ROWS, ROWS), ROWS)
@@ -101,10 +97,10 @@
     gr_ref[...] = grad_right
 
 
-def local_grads(parts, *rest):
+def local_grads(hops, parts, *rest):
     tokens = parts[0].shape[1]
     return pl.pallas_call(
-        grads_kernel,
+        functools.partial(grads_kernel, hops),
         in_specs=[pl.BlockSpec(memory_space=pltpu.VMEM)] * 15,
         out_specs=[pl.BlockSpec(memory_space=pltpu.VMEM)] * 2,
         out_shape=[jax.ShapeDtypeStruct((128, 128), F32)] * 2,
@@ -115,12 +111,33 @@
     )(*parts, *rest)
 
 
-def add_pair(x, axis, perm):
-    return x + lax.ppermute(x, axis, perm)
-
-
-def add_four(x, axis, shift):
-    one, two, three = (lax.ppermute(x, axis, shift(s)) for s in (1, 2, 3))
+ALL = ("dp", "tensor")
+
+
+ACROSS = (6, 7, 4, 5, 2, 3, 0, 1)
+
+
+def along(axis, s):
+    if axis == "y":
+        return lambda z, x, y: (z, x, (y + s) % 4)
+    if axis == "x":
+        return lambda z, x, y: (z, (x + s) % 4, y)
+    if axis == "z":
+        return lambda z, x, y: (z // 4 * 4 + (z + s) % 4, x, y)
+    return lambda z, x, y: (ACROSS[z], x, y)
+
+
+def route(axes, s):
+    pairs = []
+    for i in range(256):
+        z, x, y, core = i // 32, i // 8 % 4, i // 2 % 4, i % 2
+        z, x, y = along(axes[core], s)(z, x, y)
+        pairs.append((i, ((z * 4 + x) * 4 + y) * 2 + core))
+    return pairs
+
+
+def add_four(x, axes):
+    one, two, three = (lax.ppermute(x, ALL, route(axes, s)) for s in (1, 2, 3))
     return (x + two) + (one + three)
 
 
@@ -131,29 +148,27 @@
     give = jnp.where(first, grad_right, grad_left)
     swap = tensor_shift(0, 1)
     x = keep + lax.ppermute(give, "tensor", swap)
-    x = add_four(x, "tensor", lambda s: tensor_shift(s, 0))
-    x = add_four(x, "dp", x_shift)
-    for b in (1, 2, 4):
-        x = add_pair(x, "dp", z_flip(b))
+    x = add_four(x, "yx")
+    x = add_four(x, "xy")
+    x = add_four(x, "zz")
+    x = x + lax.ppermute(x, ALL, route("hh", 1))
     other = lax.ppermute(x, "tensor", swap)
     return jnp.where(first, x, other), jnp.where(first, other, x)
 
 
 def exchange(act, cot):
-    plan, first = [], 0
+    plan, first = [], []
     for p, tokens in enumerate(PARTS):
-        plan += [(p, first, tokens, hop) for hop in HOPS + ((0, 0),)]
-        first += tokens
-    lead = pack(act, cot, 0, PARTS[0], tuple(h for _, _, _, h in plan[:WINDOW]))
+        plan += [(p, hop) for hop in HOPS[p] + OWN]
+        first.append(sum(PARTS[:p]))
+    lead = pack(act, cot, 0, PARTS[0], HOPS[0][:WINDOW])
     act, cot, *lead = lax.optimization_barrier((act, cot, *lead))
     blocks = list(lead)
-    blocks += pack(act, cot, 0, PARTS[0], (HOPS + ((0, 0),))[WINDOW:])
-    first = PARTS[0]
-    for tokens in PARTS[1:]:
-        blocks += pack(act, cot, first, tokens, HOPS + ((0, 0),))
-        first += tokens
+    blocks += pack(act, cot, 0, PARTS[0], HOPS[0][WINDOW:] + OWN)
+    for p in range(1, len(PARTS)):
+        blocks += pack(act, cot, first[p], PARTS[p], HOPS[p] + OWN)
     got, sent = [], []
-    for (p, _, _, (dy, dc)), block in zip(plan, blocks):
+    for (p, (dy, dc)), block in zip(plan, blocks):
         if (dy, dc) != (0, 0):
             if len(sent) >= WINDOW:
                 w = sent[-WINDOW]
@@ -171,8 +186,8 @@
     lower = -half_grid * step_size
     upper = (half_grid - 1.0) * step_size
     grads = jnp.zeros((128, 128), F32), jnp.zeros((128, 128), F32)
-    for part in exchange(act, cot):
-        grads = local_grads(part, left_factor, left_factor.T, right_factor, lower, upper, *grads)
+    for hops, part in zip(HOPS, exchange(act, cot)):
+        grads = local_grads(hops, part, left_factor, left_factor.T, right_factor, lower, upper, *grads)
     return sum_all(*grads)
 
 

time: 98.6 us -> 95.3 us (0.967)
  starting transfers between devices: 51 us -> 45.3 us
  waiting for transfers between devices: 31.4 us -> 33.8 us
    ppermute x1, starting transfers between devices: 7.6 us -> 4.64 us  [sum_all(): other = lax.ppermute(x, 'tensor', swap)]
    ppermute x9 -> x10, starting transfers between devices: 20.1 us -> 17.4 us  [the longest x9 13.4 us: add_four(): one, two, three = (lax.ppermute(x, ALL, route(axes, s)) for s in (1, 2, 3))]
    ppermute x9 -> x10, waiting for transfers between devices: 11.4 us -> 13.8 us  [the longest x9 10.7 us: add_four(): one, two, three = (lax.ppermute(x, ALL, route(axes, s)) for s in (1, 2, 3))]
  transfers between devices with their start and end apart: 25 -> 26, of which waited for: 14 -> 15; matrix products, arithmetic and copies ran while one was open for 0% -> 0% of each run, Pallas kernels for 8% -> 8%
where the time goes in v3:
time: 95.3 us; the launch traced here: 95.1 us
  starting transfers between devices  45.3 us (48%)
  waiting for transfers between devices  33.8 us (35%)
  Pallas kernels  13.3 us (14%)
  local copies, waits for them, and re-layouts  1.1 us (1%)
    ppermute x14, starting transfers between devices, exchange(): block = lax.ppermute(block, 'tensor', tensor_shift(dy, dc))  22.8 us
    ppermute x14, waiting for transfers between devices, exchange(): block = lax.ppermute(block, 'tensor', tensor_shift(dy, dc))  18.2 us
    ppermute x9, starting transfers between devices, add_four(): one, two, three = (lax.ppermute(x, ALL, route(axes, s)) for s in (1, 2, 3))  13.4 us
    ppermute x9, waiting for transfers between devices, add_four(): one, two, three = (lax.ppermute(x, ALL, route(axes, s)) for s in (1, 2, 3))  10.7 us
    pallas_call x3, Pallas kernels, pack(): pl.pallas_call(functools.partial(pack_kernel, first, hops), in_specs=[pl....  7.88 us
    pallas_call x2, Pallas kernels, local_grads(): pl.pallas_call(functools.partial(grads_kernel, hops), in_specs=[pl.BlockS...  5.41 us
    ppermute x1, starting transfers between devices, sum_all(): other = lax.ppermute(x, 'tensor', swap)  4.64 us
    ppermute x1, starting transfers between devices, sum_all(): x = x + lax.ppermute(x, ALL, route('hh', 1))  4.02 us
  transfers between devices with their start and end apart: 26, of which 15 were waited for; matrix products, arithmetic and copies ran while one was open for 0% of the time, Pallas kernels for 8%

profile of v3, /device:TPU:1, one launch (start us, length us, event | category | flops | bytes accessed | tf_op | source)
XLA Modules:
  0.0 95.1 jit_solution(1942253387230801754)
XLA Ops:
  0.6 2.6 %pack.3 = (bf16[2,32,16,128]{3,2,1,0:T(8,128)(2,1)}, bf16[2,32,16,128]{3,2,1,0:T(8,128)(2,1)}, bf16[2,32,16,128]{3,2,1,0:T(8,128)(2,1)}, bf16[2,32,16,128]{3,2,1,0:T(8,128)(2,1)}, bf16[2,32,16,128]{3,2,1,0:T(8,128)(2,1)}) custom-call(bf16[8,64,16,128]{3,2,1,0:T(8,128)(2,1)} %bitcast.5, bf16[8,64,16,128]{3,2,1,0:T(8,128)(2,1)} %bitcast.8), custom_call_target="tpu_custom_call" | custom-call | bytes 2621440 | tf_op jit(solution)/shard_map/pack/pallas_call | solution.py:55
  3.2 3.8 %collective-permute-start = (bf16[2,32,16,128]{3,2,1,0:T(8,128)(2,1)}, bf16[2,32,16,128]{3,2,1,0:T(8,128)(2,1)S(1)}, u32[]{:S(2)}, u32[]{:S(2)}) collective-permute-start(bf16[2,32,16,128]{3,2,1,0:T(8,128)(2,1)} %get-tuple-element.56), channel_id=1, source_target_pairs={{0,4},{1,5},{2,6},{3,7},{4,0},{5,1},{6,2},{7,3},{8,12},{9,13},{10,... | collective-permute-start | bytes 786440 | tf_op jit(solution)/shard_map/ppermute | solution.py:176
  7.0 2.6 %collective-permute-start.2 = (bf16[2,32,16,128]{3,2,1,0:T(8,128)(2,1)}, bf16[2,32,16,128]{3,2,1,0:T(8,128)(2,1)S(1)}, u32[]{:S(2)}, u32[]{:S(2)}) collective-permute-start(bf16[2,32,16,128]{3,2,1,0:T(8,128)(2,1)} %get-tuple-element.61), channel_id=1, source_target_pairs={{0,5},{1,4},{2,7},{3,6},{4,1},{5,0},{6,3},{7,2},{8,13},{9,12},{10,... | collective-permute-start | bytes 786440 | tf_op jit(solution)/shard_map/ppermute | solution.py:176
  9.7 2.7 %collective-permute-start.9 = (bf16[2,32,16,128]{3,2,1,0:T(8,128)(2,1)}, bf16[2,32,16,128]{3,2,1,0:T(8,128)(2,1)S(1)}, u32[]{:S(2)}, u32[]{:S(2)}) collective-permute-start(bf16[2,32,16,128]{3,2,1,0:T(8,128)(2,1)} %get-tuple-element.74), channel_id=1, source_target_pairs={{0,6},{1,7},{2,0},{3,1},{4,2},{5,3},{6,4},{7,5},{8,14},{9,15},{10,... | collective-permute-start | bytes 786440 | tf_op jit(solution)/shard_map/ppermute | solution.py:176
  12.3 3.1 %pack.4 = (bf16[2,32,16,128]{3,2,1,0:T(8,128)(2,1)}, bf16[2,32,16,128]{3,2,1,0:T(8,128)(2,1)}, bf16[2,32,16,128]{3,2,1,0:T(8,128)(2,1)}, bf16[2,32,16,128]{3,2,1...) custom-call(bf16[8,64,16,128]{3,2,1,0:T(8,128)(2,1)} %bitcast.6, ...), custom_call_target="tpu_custom_call" | custom-call | bytes 4194304 | tf_op jit(solution)/shard_map/pack/pallas_call | solution.py:55
  15.4 0.0 copy-start
  15.5 2.2 %pack.5 = (bf16[2,32,16,128]{3,2,1,0:T(8,128)(2,1)}, bf16[2,32,16,128]{3,2,1,0:T(8,128)(2,1)}, bf16[2,32,16,128]{3,2,1,0:T(8,128)(2,1)}) custom-call(bf16[8,64,16,128]{3,2,1,0:T(8,128)(2,1)} %bitcast.7, bf16[8,64,16,128]{3,2,1,0:T(8,128)(2,1)} %bitcast.10), custom_call_target="tpu_custom_call" | custom-call | bytes 1572864 | tf_op jit(solution)/shard_map/pack/pallas_call | solution.py:55
  17.8 0.1 collective-permute-start.1
  17.9 3.7 %collective-permute-done.2.refs_3_ = bf16[2,32,16,128]{3,2,1,0:T(8,128)(2,1)S(1)} collective-permute-done((bf16[2,32,16,128]{3,2,1,0:T(8,128)(2,1)}, bf16[2,32,16,128]{3,2,1,0:T(8,128)(2,1)S(1)}, u32[]{:S(2)}, u32[]{:S(2)}) %collective-permute-start.2) | collective-permute-done | bytes 262176 | tf_op jit(solution)/shard_map/ppermute | solution.py:176
  21.5 1.9 %collective-permute-start.3 = (bf16[2,32,16,128]{3,2,1,0:T(8,128)(2,1)}, bf16[2,32,16,128]{3,2,1,0:T(8,128)(2,1)S(1)}, u32[]{:S(2)}, u32[]{:S(2)}) collective-permute-start(bf16[2,32,16,128]{3,2,1,0:T(8,128)(2,1)} %get-tuple-element.62), channel_id=1, source_target_pairs={{0,6},{1,7},{2,0},{3,1},{4,2},{5,3},{6,4},{7,5},{8,14},{9,15},{10,... | collective-permute-start | bytes 786440 | tf_op jit(solution)/shard_map/ppermute | solution.py:176
  23.4 2.1 %collective-permute-done.6.refs_0_ = bf16[2,32,16,128]{3,2,1,0:T(8,128)(2,1)S(1)} collective-permute-done((bf16[2,32,16,128]{3,2,1,0:T(8,128)(2,1)}, bf16[2,32,16,128]{3,2,1,0:T(8,128)(2,1)S(1)}, u32[]{:S(2)}, u32[]{:S(2)}) %collective-permute-start.6) | collective-permute-done | bytes 262176 | tf_op jit(solution)/shard_map/ppermute | solution.py:176
  25.5 2.7 %collective-permute-start.7 = (bf16[2,32,16,128]{3,2,1,0:T(8,128)(2,1)}, bf16[2,32,16,128]{3,2,1,0:T(8,128)(2,1)S(1)}, u32[]{:S(2)}, u32[]{:S(2)}) collective-permute-start(bf16[2,32,16,128]{3,2,1,0:T(8,128)(2,1)} %get-tuple-element.70), channel_id=1, source_target_pairs={{0,3},{1,2},{2,5},{3,4},{4,7},{5,6},{6,1},{7,0},{8,11},{9,10},{10,... | collective-permute-start | bytes 786440 | tf_op jit(solution)/shard_map/ppermute | solution.py:176
  28.3 0.2 collective-permute-start.10
  28.5 0.1 copy.8
  28.6 1.7 %collective-permute-start.5 = (bf16[2,32,16,128]{3,2,1,0:T(8,128)(2,1)}, bf16[2,32,16,128]{3,2,1,0:T(8,128)(2,1)S(1)}, u32[]{:S(2)}, u32[]{:S(2)}) collective-permute-start(bf16[2,32,16,128]{3,2,1,0:T(8,128)(2,1)} %get-tuple-element.66), channel_id=1, source_target_pairs={{0,4},{1,5},{2,6},{3,7},{4,0},{5,1},{6,2},{7,3},{8,12},{9,13},{10,... | collective-permute-start | bytes 786440 | tf_op jit(solution)/shard_map/ppermute | solution.py:176
  30.3 0.7 collective-permute-done.1.refs_0_
  31.0 5.9 %collective-permute-done.7.refs_5_ = bf16[2,32,16,128]{3,2,1,0:T(8,128)(2,1)S(1)} collective-permute-done((bf16[2,32,16,128]{3,2,1,0:T(8,128)(2,1)}, bf16[2,32,16,128]{3,2,1,0:T(8,128)(2,1)S(1)}, u32[]{:S(2)}, u32[]{:S(2)}) %collective-permute-start.7) | collective-permute-done | bytes 262176 | tf_op jit(solution)/shard_map/ppermute | solution.py:176
  36.9 4.1 %collective-permute-start.8 = (bf16[2,32,16,128]{3,2,1,0:T(8,128)(2,1)}, bf16[2,32,16,128]{3,2,1,0:T(8,128)(2,1)S(1)}, u32[]{:S(2)}, u32[]{:S(2)}) collective-permute-start(bf16[2,32,16,128]{3,2,1,0:T(8,128)(2,1)} %get-tuple-element.71), channel_id=1, source_target_pairs={{0,5},{1,4},{2,7},{3,6},{4,1},{5,0},{6,3},{7,2},{8,13},{9,12},{10,... | collective-permute-start | bytes 786440 | tf_op jit(solution)/shard_map/ppermute | solution.py:176
  40.9 0.1 collective-permute-start.11
  41.0 3.0 %collective-permute-start.13 = (bf16[2,32,16,128]{3,2,1,0:T(8,128)(2,1)S(1)}, bf16[2,32,16,128]{3,2,1,0:T(8,128)(2,1)S(1)}, u32[]{:S(2)}, u32[]{:S(2)}) collective-permute-start(bf16[2,32,16,128]{3,2,1,0:T(8,128)(2,1)S(1)} %copy-done.6), channel_id=1, source_target_pairs={{0,7},{1,6},{2,1},{3,0},{4,3},{5,2},{6,5},{7,4},{8,15},{9,14},{10,... | collective-permute-start | bytes 786440 | tf_op jit(solution)/shard_map/ppermute | solution.py:176
  44.1 0.9 copy-done.2
  45.0 2.7 %grads.2 = (f32[128,128]{1,0:T(8,128)S(1)}, f32[128,128]{1,0:T(8,128)S(1)}) custom-call(bf16[2,32,16,128]{3,2,1,0:T(8,128)(2,1)S(1)} %collective-permute-done.6.refs_0_, bf16[2,32,16,128]{3,2,1,0:T(8,128)(2,1)S(1)} %collective-permute-done.9.refs_1_, bf16[2,32,16,128]{3,2,1,0:T(8,128)(2,1)S(1)} %collective-permute-done.refs_2_, ...), custom_call_target="tpu_custom_call" | custom-call | flops 671088640 | bytes 2097152 | tf_op jit(solution)/shard_map/grads/pallas_call | solution.py:102
  47.7 0.3 collective-permute-done.8.refs_3_
  48.0 5.5 %collective-permute-done.12.refs_5_ = bf16[2,32,16,128]{3,2,1,0:T(8,128)(2,1)S(1)} collective-permute-done((bf16[2,32,16,128]{3,2,1,0:T(8,128)(2,1)S(1)}, bf16[2,32,16,128]{3,2,1,0:T(8,128)(2,1)S(1)}, u32[]{:S(2)}, u32[]{:S(2)}) %collective-permute-start.12) | collective-permute-done | bytes 262176 | tf_op jit(solution)/shard_map/ppermute | solution.py:176
  53.6 0.0 collective-permute-done.13.refs_6_
  53.6 2.7 %grads.3 = (f32[128,128]{1,0:T(8,128)S(1)}, f32[128,128]{1,0:T(8,128)S(1)}) custom-call(bf16[2,32,16,128]{3,2,1,0:T(8,128)(2,1)S(1)} %collective-permute-done.1.refs_0_, bf16[2,32,16,128]{3,2,1,0:T(8,128)(2,1)S(1)} %collective-permute-done.3.refs_1_, bf16[2,32,16,128]{3,2,1,0:T(8,128)(2,1)S(1)} %collective-permute-done.5.refs_2_, ...), custom_call_target="tpu_custom_call" | custom-call | flops 671088640 | bytes 2097152 | tf_op jit(solution)/shard_map/grads/pallas_call | solution.py:102
  56.3 0.5 collective-permute-start.14
  56.8 0.9 collective-permute-done.14
  57.7 1.3 %collective-permute-start.16 = (f32[128,128]{1,0:T(8,128)S(1)}, f32[128,128]{1,0:T(8,128)S(1)}, u32[]{:S(2)}, u32[]{:S(2)}) collective-permute-start(f32[128,128]{1,0:T(8,128)S(1)} %select_add_fusion), channel_id=1, source_target_pairs={{0,2},{1,9},{2,4},{3,11},{4,6},{5,13},{6,0},{7,15},{8,10},{9,17},{... | collective-permute-start | bytes 196616 | tf_op jit(solution)/shard_map/ppermute | solution.py:140
  59.0 1.5 %collective-permute-start.17 = (f32[128,128]{1,0:T(8,128)S(1)}, f32[128,128]{1,0:T(8,128)S(1)}, u32[]{:S(2)}, u32[]{:S(2)}) collective-permute-start(f32[128,128]{1,0:T(8,128)S(1)} %select_add_fusion), channel_id=1, source_target_pairs={{0,6},{1,25},{2,0},{3,27},{4,2},{5,29},{6,4},{7,31},{8,14},{9,1},{... | collective-permute-start | bytes 196616 | tf_op jit(solution)/shard_map/ppermute | solution.py:140
  60.4 1.5 %collective-permute-start.15 = (f32[128,128]{1,0:T(8,128)S(1)}, f32[128,128]{1,0:T(8,128)S(1)}, u32[]{:S(2)}, u32[]{:S(2)}) collective-permute-start(f32[128,128]{1,0:T(8,128)S(1)} %select_add_fusion), channel_id=1, source_target_pairs={{0,4},{1,17},{2,6},{3,19},{4,0},{5,21},{6,2},{7,23},{8,12},{9,25},... | collective-permute-start | bytes 196616 | tf_op jit(solution)/shard_map/ppermute | solution.py:140
  62.0 0.1 collective-permute-done.16
  62.1 3.0 %collective-permute-done.15 = f32[128,128]{1,0:T(8,128)S(1)} collective-permute-done((f32[128,128]{1,0:T(8,128)S(1)}, f32[128,128]{1,0:T(8,128)S(1)}, u32[]{:S(2)}, u32[]{:S(2)}) %collective-permute-start.15) | collective-permute-done | bytes 65568 | tf_op jit(solution)/shard_map/ppermute | solution.py:140
  65.1 1.3 %collective-permute-start.19 = (f32[128,128]{1,0:T(8,128)S(1)}, f32[128,128]{1,0:T(8,128)S(1)}, u32[]{:S(2)}, u32[]{:S(2)}) collective-permute-start(f32[128,128]{1,0:T(8,128)S(1)} %add_add_fusion.2), channel_id=1, source_target_pairs={{0,8},{1,3},{2,10},{3,5},{4,12},{5,7},{6,14},{7,1},{8,16},{9,11},{... | collective-permute-start | bytes 196616 | tf_op jit(solution)/shard_map/ppermute | solution.py:140
  66.4 1.8 %collective-permute-start.20 = (f32[128,128]{1,0:T(8,128)S(1)}, f32[128,128]{1,0:T(8,128)S(1)}, u32[]{:S(2)}, u32[]{:S(2)}) collective-permute-start(f32[128,128]{1,0:T(8,128)S(1)} %add_add_fusion.2), channel_id=1, source_target_pairs={{0,24},{1,7},{2,26},{3,1},{4,28},{5,3},{6,30},{7,5},{8,0},{9,15},{... | collective-permute-start | bytes 196616 | tf_op jit(solution)/shard_map/ppermute | solution.py:140
  68.2 1.3 %collective-permute-start.18 = (f32[128,128]{1,0:T(8,128)S(1)}, f32[128,128]{1,0:T(8,128)S(1)}, u32[]{:S(2)}, u32[]{:S(2)}) collective-permute-start(f32[128,128]{1,0:T(8,128)S(1)} %add_add_fusion.2), channel_id=1, source_target_pairs={{0,16},{1,5},{2,18},{3,7},{4,20},{5,1},{6,22},{7,3},{8,24},{9,13},... | collective-permute-start | bytes 196616 | tf_op jit(solution)/shard_map/ppermute | solution.py:140
  69.5 0.3 collective-permute-done.19
  69.7 3.1 %collective-permute-done.18 = f32[128,128]{1,0:T(8,128)S(1)} collective-permute-done((f32[128,128]{1,0:T(8,128)S(1)}, f32[128,128]{1,0:T(8,128)S(1)}, u32[]{:S(2)}, u32[]{:S(2)}) %collective-permute-start.18) | collective-permute-done | bytes 65568 | tf_op jit(solution)/shard_map/ppermute | solution.py:140
  72.8 1.7 %collective-permute-start.22 = (f32[128,128]{1,0:T(8,128)S(1)}, f32[128,128]{1,0:T(8,128)S(1)}, u32[]{:S(2)}, u32[]{:S(2)}) collective-permute-start(f32[128,128]{1,0:T(8,128)S(1)} %add_add_fusion.1), channel_id=1, source_target_pairs={{0,32},{1,33},{2,34},{3,35},{4,36},{5,37},{6,38},{7,39},{8,40},{9,... | collective-permute-start | bytes 196616 | tf_op jit(solution)/shard_map/ppermute | solution.py:140
  74.5 2.8 %collective-permute-start.23 = (f32[128,128]{1,0:T(8,128)S(1)}, f32[128,128]{1,0:T(8,128)S(1)}, u32[]{:S(2)}, u32[]{:S(2)}) collective-permute-start(f32[128,128]{1,0:T(8,128)S(1)} %add_add_fusion.1), channel_id=1, source_target_pairs={{0,96},{1,97},{2,98},{3,99},{4,100},{5,101},{6,102},{7,103},{8,104... | collective-permute-start | bytes 196616 | tf_op jit(solution)/shard_map/ppermute | solution.py:140
  77.3 0.2 collective-permute-start.21
  77.5 1.4 %collective-permute-done.22 = f32[128,128]{1,0:T(8,128)S(1)} collective-permute-done((f32[128,128]{1,0:T(8,128)S(1)}, f32[128,128]{1,0:T(8,128)S(1)}, u32[]{:S(2)}, u32[]{:S(2)}) %collective-permute-start.22) | collective-permute-done | bytes 65568 | tf_op jit(solution)/shard_map/ppermute | solution.py:140
  78.9 2.9 %collective-permute-done.21 = f32[128,128]{1,0:T(8,128)S(1)} collective-permute-done((f32[128,128]{1,0:T(8,128)S(1)}, f32[128,128]{1,0:T(8,128)S(1)}, u32[]{:S(2)}, u32[]{:S(2)}) %collective-permute-start.21) | collective-permute-done | bytes 65568 | tf_op jit(solution)/shard_map/ppermute | solution.py:140
  81.8 4.0 %collective-permute-start.24 = (f32[128,128]{1,0:T(8,128)S(1)}, f32[128,128]{1,0:T(8,128)S(1)}, u32[]{:S(2)}, u32[]{:S(2)}) collective-permute-start(f32[128,128]{1,0:T(8,128)S(1)} %add_add_fusion), channel_id=1, source_target_pairs={{0,192},{1,193},{2,194},{3,195},{4,196},{5,197},{6,198},{7,199},{8... | collective-permute-start | bytes 196616 | tf_op jit(solution)/shard_map/ppermute | solution.py:154
  85.9 3.1 %collective-permute-done.24 = f32[128,128]{1,0:T(8,128)S(1)} collective-permute-done((f32[128,128]{1,0:T(8,128)S(1)}, f32[128,128]{1,0:T(8,128)S(1)}, u32[]{:S(2)}, u32[]{:S(2)}) %collective-permute-start.24) | collective-permute-done | bytes 65568 | tf_op jit(solution)/shard_map/ppermute | solution.py:154
  88.9 4.6 %collective-permute-start.25 = (f32[128,128]{1,0:T(8,128)S(1)}, f32[128,128]{1,0:T(8,128)S(1)}, u32[]{:S(2)}, u32[]{:S(2)}) collective-permute-start(f32[128,128]{1,0:T(8,128)S(1)} %add.50), channel_id=1, source_target_pairs={{0,1},{1,0},{2,3},{3,2},{4,5},{5,4},{6,7},{7,6},{8,9},{9,8},{10,11... | collective-permute-start | bytes 196616 | tf_op jit(solution)/shard_map/ppermute | solution.py:155
  93.6 0.9 collective-permute-done.25
  94.5 0.7 broadcast_select_fusion
  (35 shorter events, 0.2 us)
Async XLA Ops:
  3.2 14.6 %collective-permute-start = (bf16[2,32,16,128]{3,2,1,0:T(8,128)(2,1)}, bf16[2,32,16,128]{3,2,1,0:T(8,128)(2,1)S(1)}, u32[]{:S(2)}, u32[]{:S(2)}) collective-permute-start(bf16[2,32,16,128]{3,2,1,0:T(8,128)(2,1)} %get-tuple-element.56), channel_id=1, source_target_pairs={{0,4},{1,5},{2,6},{3,7},{4,0},{5,1},{6,2},{7,3},{8,12},{9,13},{10,... | collective-permute-start | bytes 786440 | tf_op jit(solution)/shard_map/ppermute | solution.py:176
  7.0 14.5 %collective-permute-start.2 = (bf16[2,32,16,128]{3,2,1,0:T(8,128)(2,1)}, bf16[2,32,16,128]{3,2,1,0:T(8,128)(2,1)S(1)}, u32[]{:S(2)}, u32[]{:S(2)}) collective-permute-start(bf16[2,32,16,128]{3,2,1,0:T(8,128)(2,1)} %get-tuple-element.61), channel_id=1, source_target_pairs={{0,5},{1,4},{2,7},{3,6},{4,1},{5,0},{6,3},{7,2},{8,13},{9,12},{10,... | collective-permute-start | bytes 786440 | tf_op jit(solution)/shard_map/ppermute | solution.py:176
  9.7 15.9 %collective-permute-start.6 = (bf16[2,32,16,128]{3,2,1,0:T(8,128)(2,1)}, bf16[2,32,16,128]{3,2,1,0:T(8,128)(2,1)S(1)}, u32[]{:S(2)}, u32[]{:S(2)}) collective-permute-start(bf16[2,32,16,128]{3,2,1,0:T(8,128)(2,1)} %get-tuple-element.69), channel_id=1, source_target_pairs={{0,2},{1,3},{2,4},{3,5},{4,6},{5,7},{6,0},{7,1},{8,10},{9,11},{10,... | collective-permute-start | bytes 786440 | tf_op jit(solution)/shard_map/ppermute | solution.py:176
  9.7 18.6 %collective-permute-start.9 = (bf16[2,32,16,128]{3,2,1,0:T(8,128)(2,1)}, bf16[2,32,16,128]{3,2,1,0:T(8,128)(2,1)S(1)}, u32[]{:S(2)}, u32[]{:S(2)}) collective-permute-start(bf16[2,32,16,128]{3,2,1,0:T(8,128)(2,1)} %get-tuple-element.74), channel_id=1, source_target_pairs={{0,6},{1,7},{2,0},{3,1},{4,2},{5,3},{6,4},{7,5},{8,14},{9,15},{10,... | collective-permute-start | bytes 786440 | tf_op jit(solution)/shard_map/ppermute | solution.py:176
  12.3 16.3 %collective-permute-start.4 = (bf16[2,32,16,128]{3,2,1,0:T(8,128)(2,1)}, bf16[2,32,16,128]{3,2,1,0:T(8,128)(2,1)S(1)}, u32[]{:S(2)}, u32[]{:S(2)}) collective-permute-start(bf16[2,32,16,128]{3,2,1,0:T(8,128)(2,1)} %get-tuple-element.65), channel_id=1, source_target_pairs={{0,1},{1,0},{2,3},{3,2},{4,5},{5,4},{6,7},{7,6},{8,9},{9,8},{10,11... | collective-permute-start | bytes 786440 | tf_op jit(solution)/shard_map/ppermute | solution.py:176
  15.4 13.1 %copy-start = (bf16[128,128]{1,0:T(8,128)(2,1)S(1)}, bf16[128,128]{1,0:T(8,128)(2,1)}, u32[]{:S(2)}) copy-start(bf16[128,128]{1,0:T(8,128)(2,1)} %refs_8_.3) | copy-start | bytes 98308
  15.4 25.6 %copy-start.7 = (bf16[2,32,16,128]{3,2,1,0:T(8,128)(2,1)S(1)}, bf16[2,32,16,128]{3,2,1,0:T(8,128)(2,1)}, u32[]{:S(2)}) copy-start(bf16[2,32,16,128]{3,2,1,0:T(8,128)(2,1)} %get-tuple-element.77) | copy-start | bytes 786436
  15.4 25.6 %copy-start.6 = (bf16[2,32,16,128]{3,2,1,0:T(8,128)(2,1)S(1)}, bf16[2,32,16,128]{3,2,1,0:T(8,128)(2,1)}, u32[]{:S(2)}) copy-start(bf16[2,32,16,128]{3,2,1,0:T(8,128)(2,1)} %get-tuple-element.78) | copy-start | bytes 786436
  15.5 28.5 %copy-start.4 = (s32[128,128]{1,0:T(8,128)S(1)}, s32[128,128]{1,0:T(8,128)}, u32[]{:S(2)}) copy-start(s32[128,128]{1,0:T(8,128)} %param.10) | copy-start | bytes 196612
  15.5 28.5 %copy-start.5 = (s32[128,128]{1,0:T(8,128)S(1)}, s32[128,128]{1,0:T(8,128)}, u32[]{:S(2)}) copy-start(s32[128,128]{1,0:T(8,128)} %param.11) | copy-start | bytes 196612
  15.5 28.6 %copy-start.3 = (bf16[128,128]{1,0:T(8,128)(2,1)S(1)}, bf16[128,128]{1,0:T(8,128)(2,1)}, u32[]{:S(2)}) copy-start(bf16[128,128]{1,0:T(8,128)(2,1)} %refs_10_.3) | copy-start | bytes 98308
  17.7 35.8 %copy-start.1 = (bf16[2,32,16,128]{3,2,1,0:T(8,128)(2,1)S(1)}, bf16[2,32,16,128]{3,2,1,0:T(8,128)(2,1)}, u32[]{:S(2)}) copy-start(bf16[2,32,16,128]{3,2,1,0:T(8,128)(2,1)} %get-tuple-element.79.refs_7_) | copy-start | bytes 786436
  17.8 13.2 %collective-permute-start.1 = (bf16[2,32,16,128]{3,2,1,0:T(8,128)(2,1)}, bf16[2,32,16,128]{3,2,1,0:T(8,128)(2,1)S(1)}, u32[]{:S(2)}, u32[]{:S(2)}) collective-permute-start(bf16[2,32,16,128]{3,2,1,0:T(8,128)(2,1)} %get-tuple-element.57), channel_id=1, source_target_pairs={{0,2},{1,3},{2,4},{3,5},{4,6},{5,7},{6,0},{7,1},{8,10},{9,11},{10,... | collective-permute-start | bytes 786440 | tf_op jit(solution)/shard_map/ppermute | solution.py:176
  21.5 9.5 %collective-permute-start.3 = (bf16[2,32,16,128]{3,2,1,0:T(8,128)(2,1)}, bf16[2,32,16,128]{3,2,1,0:T(8,128)(2,1)S(1)}, u32[]{:S(2)}, u32[]{:S(2)}) collective-permute-start(bf16[2,32,16,128]{3,2,1,0:T(8,128)(2,1)} %get-tuple-element.62), channel_id=1, source_target_pairs={{0,6},{1,7},{2,0},{3,1},{4,2},{5,3},{6,4},{7,5},{8,14},{9,15},{10,... | collective-permute-start | bytes 786440 | tf_op jit(solution)/shard_map/ppermute | solution.py:176
  25.5 11.3 %collective-permute-start.7 = (bf16[2,32,16,128]{3,2,1,0:T(8,128)(2,1)}, bf16[2,32,16,128]{3,2,1,0:T(8,128)(2,1)S(1)}, u32[]{:S(2)}, u32[]{:S(2)}) collective-permute-start(bf16[2,32,16,128]{3,2,1,0:T(8,128)(2,1)} %get-tuple-element.70), channel_id=1, source_target_pairs={{0,3},{1,2},{2,5},{3,4},{4,7},{5,6},{6,1},{7,0},{8,11},{9,10},{10,... | collective-permute-start | bytes 786440 | tf_op jit(solution)/shard_map/ppermute | solution.py:176
  28.3 12.7 %collective-permute-start.10 = (bf16[2,32,16,128]{3,2,1,0:T(8,128)(2,1)}, bf16[2,32,16,128]{3,2,1,0:T(8,128)(2,1)S(1)}, u32[]{:S(2)}, u32[]{:S(2)}) collective-permute-start(bf16[2,32,16,128]{3,2,1,0:T(8,128)(2,1)} %get-tuple-element.75), channel_id=1, source_target_pairs={{0,7},{1,6},{2,1},{3,0},{4,3},{5,2},{6,5},{7,4},{8,15},{9,14},{10,... | collective-permute-start | bytes 786440 | tf_op jit(solution)/shard_map/ppermute | solution.py:176
  28.6 19.1 %collective-permute-start.5 = (bf16[2,32,16,128]{3,2,1,0:T(8,128)(2,1)}, bf16[2,32,16,128]{3,2,1,0:T(8,128)(2,1)S(1)}, u32[]{:S(2)}, u32[]{:S(2)}) collective-permute-start(bf16[2,32,16,128]{3,2,1,0:T(8,128)(2,1)} %get-tuple-element.66), channel_id=1, source_target_pairs={{0,4},{1,5},{2,6},{3,7},{4,0},{5,1},{6,2},{7,3},{8,12},{9,13},{10,... | collective-permute-start | bytes 786440 | tf_op jit(solution)/shard_map/ppermute | solution.py:176
  36.9 11.2 %collective-permute-start.8 = (bf16[2,32,16,128]{3,2,1,0:T(8,128)(2,1)}, bf16[2,32,16,128]{3,2,1,0:T(8,128)(2,1)S(1)}, u32[]{:S(2)}, u32[]{:S(2)}) collective-permute-start(bf16[2,32,16,128]{3,2,1,0:T(8,128)(2,1)} %get-tuple-element.71), channel_id=1, source_target_pairs={{0,5},{1,4},{2,7},{3,6},{4,1},{5,0},{6,3},{7,2},{8,13},{9,12},{10,... | collective-permute-start | bytes 786440 | tf_op jit(solution)/shard_map/ppermute | solution.py:176
  40.9 7.1 %collective-permute-start.11 = (bf16[2,32,16,128]{3,2,1,0:T(8,128)(2,1)}, bf16[2,32,16,128]{3,2,1,0:T(8,128)(2,1)S(1)}, u32[]{:S(2)}, u32[]{:S(2)}) collective-permute-start(bf16[2,32,16,128]{3,2,1,0:T(8,128)(2,1)} %get-tuple-element.76), channel_id=1, source_target_pairs={{0,1},{1,0},{2,3},{3,2},{4,5},{5,4},{6,7},{7,6},{8,9},{9,8},{10,11... | collective-permute-start | bytes 786440 | tf_op jit(solution)/shard_map/ppermute | solution.py:176
  41.0 12.5 %collective-permute-start.12 = (bf16[2,32,16,128]{3,2,1,0:T(8,128)(2,1)S(1)}, bf16[2,32,16,128]{3,2,1,0:T(8,128)(2,1)S(1)}, u32[]{:S(2)}, u32[]{:S(2)}) collective-permute-start(bf16[2,32,16,128]{3,2,1,0:T(8,128)(2,1)S(1)} %copy-done.7), channel_id=1, source_target_pairs={{0,3},{1,2},{2,5},{3,4},{4,7},{5,6},{6,1},{7,0},{8,11},{9,10},{10,... | collective-permute-start | bytes 786440 | tf_op jit(solution)/shard_map/ppermute | solution.py:176
  41.0 12.5 %collective-permute-start.13 = (bf16[2,32,16,128]{3,2,1,0:T(8,128)(2,1)S(1)}, bf16[2,32,16,128]{3,2,1,0:T(8,128)(2,1)S(1)}, u32[]{:S(2)}, u32[]{:S(2)}) collective-permute-start(bf16[2,32,16,128]{3,2,1,0:T(8,128)(2,1)S(1)} %copy-done.6), channel_id=1, source_target_pairs={{0,7},{1,6},{2,1},{3,0},{4,3},{5,2},{6,5},{7,4},{8,15},{9,14},{10,... | collective-permute-start | bytes 786440 | tf_op jit(solution)/shard_map/ppermute | solution.py:176
  44.1 1.0 copy-start.2
  56.3 1.4 %collective-permute-start.14 = (f32[128,128]{1,0:T(8,128)S(1)}, f32[128,128]{1,0:T(8,128)S(1)}, u32[]{:S(2)}, u32[]{:S(2)}) collective-permute-start(f32[128,128]{1,0:T(8,128)S(1)} %broadcast_select_fusion.2), channel_id=1, source_target_pairs={{0,1},{1,0},{2,3},{3,2},{4,5},{5,4},{6,7},{7,6},{8,9},{9,8},{10,11... | collective-permute-start | bytes 196616 | tf_op jit(solution)/shard_map/ppermute | solution.py:150
  57.7 4.4 %collective-permute-start.16 = (f32[128,128]{1,0:T(8,128)S(1)}, f32[128,128]{1,0:T(8,128)S(1)}, u32[]{:S(2)}, u32[]{:S(2)}) collective-permute-start(f32[128,128]{1,0:T(8,128)S(1)} %select_add_fusion), channel_id=1, source_target_pairs={{0,2},{1,9},{2,4},{3,11},{4,6},{5,13},{6,0},{7,15},{8,10},{9,17},{... | collective-permute-start | bytes 196616 | tf_op jit(solution)/shard_map/ppermute | solution.py:140
  59.0 3.1 %collective-permute-start.17 = (f32[128,128]{1,0:T(8,128)S(1)}, f32[128,128]{1,0:T(8,128)S(1)}, u32[]{:S(2)}, u32[]{:S(2)}) collective-permute-start(f32[128,128]{1,0:T(8,128)S(1)} %select_add_fusion), channel_id=1, source_target_pairs={{0,6},{1,25},{2,0},{3,27},{4,2},{5,29},{6,4},{7,31},{8,14},{9,1},{... | collective-permute-start | bytes 196616 | tf_op jit(solution)/shard_map/ppermute | solution.py:140
  60.4 4.6 %collective-permute-start.15 = (f32[128,128]{1,0:T(8,128)S(1)}, f32[128,128]{1,0:T(8,128)S(1)}, u32[]{:S(2)}, u32[]{:S(2)}) collective-permute-start(f32[128,128]{1,0:T(8,128)S(1)} %select_add_fusion), channel_id=1, source_target_pairs={{0,4},{1,17},{2,6},{3,19},{4,0},{5,21},{6,2},{7,23},{8,12},{9,25},... | collective-permute-start | bytes 196616 | tf_op jit(solution)/shard_map/ppermute | solution.py:140
  65.1 4.7 %collective-permute-start.19 = (f32[128,128]{1,0:T(8,128)S(1)}, f32[128,128]{1,0:T(8,128)S(1)}, u32[]{:S(2)}, u32[]{:S(2)}) collective-permute-start(f32[128,128]{1,0:T(8,128)S(1)} %add_add_fusion.2), channel_id=1, source_target_pairs={{0,8},{1,3},{2,10},{3,5},{4,12},{5,7},{6,14},{7,1},{8,16},{9,11},{... | collective-permute-start | bytes 196616 | tf_op jit(solution)/shard_map/ppermute | solution.py:140
  66.4 3.4 %collective-permute-start.20 = (f32[128,128]{1,0:T(8,128)S(1)}, f32[128,128]{1,0:T(8,128)S(1)}, u32[]{:S(2)}, u32[]{:S(2)}) collective-permute-start(f32[128,128]{1,0:T(8,128)S(1)} %add_add_fusion.2), channel_id=1, source_target_pairs={{0,24},{1,7},{2,26},{3,1},{4,28},{5,3},{6,30},{7,5},{8,0},{9,15},{... | collective-permute-start | bytes 196616 | tf_op jit(solution)/shard_map/ppermute | solution.py:140
  68.2 4.6 %collective-permute-start.18 = (f32[128,128]{1,0:T(8,128)S(1)}, f32[128,128]{1,0:T(8,128)S(1)}, u32[]{:S(2)}, u32[]{:S(2)}) collective-permute-start(f32[128,128]{1,0:T(8,128)S(1)} %add_add_fusion.2), channel_id=1, source_target_pairs={{0,16},{1,5},{2,18},{3,7},{4,20},{5,1},{6,22},{7,3},{8,24},{9,13},... | collective-permute-start | bytes 196616 | tf_op jit(solution)/shard_map/ppermute | solution.py:140
  72.8 6.1 %collective-permute-start.22 = (f32[128,128]{1,0:T(8,128)S(1)}, f32[128,128]{1,0:T(8,128)S(1)}, u32[]{:S(2)}, u32[]{:S(2)}) collective-permute-start(f32[128,128]{1,0:T(8,128)S(1)} %add_add_fusion.1), channel_id=1, source_target_pairs={{0,32},{1,33},{2,34},{3,35},{4,36},{5,37},{6,38},{7,39},{8,40},{9,... | collective-permute-start | bytes 196616 | tf_op jit(solution)/shard_map/ppermute | solution.py:140
  74.5 4.4 %collective-permute-start.23 = (f32[128,128]{1,0:T(8,128)S(1)}, f32[128,128]{1,0:T(8,128)S(1)}, u32[]{:S(2)}, u32[]{:S(2)}) collective-permute-start(f32[128,128]{1,0:T(8,128)S(1)} %add_add_fusion.1), channel_id=1, source_target_pairs={{0,96},{1,97},{2,98},{3,99},{4,100},{5,101},{6,102},{7,103},{8,104... | collective-permute-start | bytes 196616 | tf_op jit(solution)/shard_map/ppermute | solution.py:140
  77.3 4.5 %collective-permute-start.21 = (f32[128,128]{1,0:T(8,128)S(1)}, f32[128,128]{1,0:T(8,128)S(1)}, u32[]{:S(2)}, u32[]{:S(2)}) collective-permute-start(f32[128,128]{1,0:T(8,128)S(1)} %add_add_fusion.1), channel_id=1, source_target_pairs={{0,64},{1,65},{2,66},{3,67},{4,68},{5,69},{6,70},{7,71},{8,72},{9,... | collective-permute-start | bytes 196616 | tf_op jit(solution)/shard_map/ppermute | solution.py:140
  81.8 7.1 %collective-permute-start.24 = (f32[128,128]{1,0:T(8,128)S(1)}, f32[128,128]{1,0:T(8,128)S(1)}, u32[]{:S(2)}, u32[]{:S(2)}) collective-permute-start(f32[128,128]{1,0:T(8,128)S(1)} %add_add_fusion), channel_id=1, source_target_pairs={{0,192},{1,193},{2,194},{3,195},{4,196},{5,197},{6,198},{7,199},{8... | collective-permute-start | bytes 196616 | tf_op jit(solution)/shard_map/ppermute | solution.py:154
  88.9 5.5 %collective-permute-start.25 = (f32[128,128]{1,0:T(8,128)S(1)}, f32[128,128]{1,0:T(8,128)S(1)}, u32[]{:S(2)}, u32[]{:S(2)}) collective-permute-start(f32[128,128]{1,0:T(8,128)S(1)} %add.50), channel_id=1, source_target_pairs={{0,1},{1,0},{2,3},{3,2},{4,5},{5,4},{6,7},{7,6},{8,9},{9,8},{10,11... | collective-permute-start | bytes 196616 | tf_op jit(solution)/shard_map/ppermute | solution.py:155

commit v4 on v3

--- a/solution.py
+++ b/solution.py
@@ -137,7 +137,8 @@
 
 
 def add_four(x, axes):
-    one, two, three = (lax.ppermute(x, ALL, route(axes, s)) for s in (1, 2, 3))
+    x = x.astype(BF16)
+    x, one, two, three = (y.astype(F32) for y in [x] + [lax.ppermute(x, ALL, route(axes, s)) for s in (1, 2, 3)])
     return (x + two) + (one + three)
 
 

time: 95.3 us -> 93.7 us (0.983)
  waiting for transfers between devices: 33.8 us -> 32.7 us
    ppermute x1, starting transfers between devices: 4.02 us -> 2.22 us  [sum_all(): x = x + lax.ppermute(x, ALL, route('hh', 1))]
    ppermute x9, waiting for transfers between devices: 10.7 us -> 9.53 us  [add_four(): lax.ppermute(x, ALL, route(axes, s))]
    ppermute x1, starting transfers between devices: 4.64 us -> 5.74 us  [sum_all(): other = lax.ppermute(x, 'tensor', swap)]
  transfers between devices with their start and end apart: 26 -> 26, of which waited for: 15 -> 15; matrix products, arithmetic and copies ran while one was open for 0% -> 0% of each run, Pallas kernels for 8% -> 9%
where the time goes in v4:
time: 93.7 us; the launch traced here: 93.5 us
  starting transfers between devices  44.7 us (48%)
  waiting for transfers between devices  32.7 us (35%)
  Pallas kernels  13.3 us (14%)
  local copies, waits for them, and re-layouts  1.1 us (1%)
    ppermute x14, starting transfers between devices, exchange(): block = lax.ppermute(block, 'tensor', tensor_shift(dy, dc))  22.8 us
    ppermute x14, waiting for transfers between devices, exchange(): block = lax.ppermute(block, 'tensor', tensor_shift(dy, dc))  18.2 us
    ppermute x9, starting transfers between devices, add_four(): lax.ppermute(x, ALL, route(axes, s))  13.5 us
    ppermute x9, waiting for transfers between devices, add_four(): lax.ppermute(x, ALL, route(axes, s))  9.53 us
    pallas_call x3, Pallas kernels, pack(): pl.pallas_call(functools.partial(pack_kernel, first, hops), in_specs=[pl....  7.88 us
    ppermute x1, starting transfers between devices, sum_all(): other = lax.ppermute(x, 'tensor', swap)  5.74 us
    pallas_call x2, Pallas kernels, local_grads(): pl.pallas_call(functools.partial(grads_kernel, hops), in_specs=[pl.BlockS...  5.41 us
    ppermute x1, waiting for transfers between devices, sum_all(): x = x + lax.ppermute(x, ALL, route('hh', 1))  3.19 us
  transfers between devices with their start and end apart: 26, of which 15 were waited for; matrix products, arithmetic and copies ran while one was open for 0% of the time, Pallas kernels for 9%

profile of v4, /device:TPU:1, one launch (start us, length us, event | category | flops | bytes accessed | tf_op | source)
XLA Modules:
  0.0 93.5 jit_solution(5771830909897361786)
XLA Ops:
  0.6 2.6 %pack.3 = (bf16[2,32,16,128]{3,2,1,0:T(8,128)(2,1)}, bf16[2,32,16,128]{3,2,1,0:T(8,128)(2,1)}, bf16[2,32,16,128]{3,2,1,0:T(8,128)(2,1)}, bf16[2,32,16,128]{3,2,1,0:T(8,128)(2,1)}, bf16[2,32,16,128]{3,2,1,0:T(8,128)(2,1)}) custom-call(bf16[8,64,16,128]{3,2,1,0:T(8,128)(2,1)} %bitcast.5, bf16[8,64,16,128]{3,2,1,0:T(8,128)(2,1)} %bitcast.8), custom_call_target="tpu_custom_call" | custom-call | bytes 2621440 | tf_op jit(solution)/shard_map/pack/pallas_call | solution.py:55
  3.2 3.8 %collective-permute-start = (bf16[2,32,16,128]{3,2,1,0:T(8,128)(2,1)}, bf16[2,32,16,128]{3,2,1,0:T(8,128)(2,1)S(1)}, u32[]{:S(2)}, u32[]{:S(2)}) collective-permute-start(bf16[2,32,16,128]{3,2,1,0:T(8,128)(2,1)} %get-tuple-element.56), channel_id=1, source_target_pairs={{0,4},{1,5},{2,6},{3,7},{4,0},{5,1},{6,2},{7,3},{8,12},{9,13},{10,... | collective-permute-start | bytes 786440 | tf_op jit(solution)/shard_map/ppermute | solution.py:177
  7.0 2.6 %collective-permute-start.2 = (bf16[2,32,16,128]{3,2,1,0:T(8,128)(2,1)}, bf16[2,32,16,128]{3,2,1,0:T(8,128)(2,1)S(1)}, u32[]{:S(2)}, u32[]{:S(2)}) collective-permute-start(bf16[2,32,16,128]{3,2,1,0:T(8,128)(2,1)} %get-tuple-element.61), channel_id=1, source_target_pairs={{0,5},{1,4},{2,7},{3,6},{4,1},{5,0},{6,3},{7,2},{8,13},{9,12},{10,... | collective-permute-start | bytes 786440 | tf_op jit(solution)/shard_map/ppermute | solution.py:177
  9.7 2.7 %collective-permute-start.9 = (bf16[2,32,16,128]{3,2,1,0:T(8,128)(2,1)}, bf16[2,32,16,128]{3,2,1,0:T(8,128)(2,1)S(1)}, u32[]{:S(2)}, u32[]{:S(2)}) collective-permute-start(bf16[2,32,16,128]{3,2,1,0:T(8,128)(2,1)} %get-tuple-element.74), channel_id=1, source_target_pairs={{0,6},{1,7},{2,0},{3,1},{4,2},{5,3},{6,4},{7,5},{8,14},{9,15},{10,... | collective-permute-start | bytes 786440 | tf_op jit(solution)/shard_map/ppermute | solution.py:177
  12.3 3.1 %pack.4 = (bf16[2,32,16,128]{3,2,1,0:T(8,128)(2,1)}, bf16[2,32,16,128]{3,2,1,0:T(8,128)(2,1)}, bf16[2,32,16,128]{3,2,1,0:T(8,128)(2,1)}, bf16[2,32,16,128]{3,2,1...) custom-call(bf16[8,64,16,128]{3,2,1,0:T(8,128)(2,1)} %bitcast.6, ...), custom_call_target="tpu_custom_call" | custom-call | bytes 4194304 | tf_op jit(solution)/shard_map/pack/pallas_call | solution.py:55
  15.4 0.0 copy-start
  15.5 0.0 copy-start.4
  15.5 0.0 copy-start.5
  15.5 0.0 copy-start.3
  15.5 2.2 %pack.5 = (bf16[2,32,16,128]{3,2,1,0:T(8,128)(2,1)}, bf16[2,32,16,128]{3,2,1,0:T(8,128)(2,1)}, bf16[2,32,16,128]{3,2,1,0:T(8,128)(2,1)}) custom-call(bf16[8,64,16,128]{3,2,1,0:T(8,128)(2,1)} %bitcast.7, bf16[8,64,16,128]{3,2,1,0:T(8,128)(2,1)} %bitcast.10), custom_call_target="tpu_custom_call" | custom-call | bytes 1572864 | tf_op jit(solution)/shard_map/pack/pallas_call | solution.py:55
  17.8 0.1 collective-permute-start.1
  17.9 3.7 %collective-permute-done.2.refs_3_ = bf16[2,32,16,128]{3,2,1,0:T(8,128)(2,1)S(1)} collective-permute-done((bf16[2,32,16,128]{3,2,1,0:T(8,128)(2,1)}, bf16[2,32,16,128]{3,2,1,0:T(8,128)(2,1)S(1)}, u32[]{:S(2)}, u32[]{:S(2)}) %collective-permute-start.2) | collective-permute-done | bytes 262176 | tf_op jit(solution)/shard_map/ppermute | solution.py:177
  21.5 1.9 %collective-permute-start.3 = (bf16[2,32,16,128]{3,2,1,0:T(8,128)(2,1)}, bf16[2,32,16,128]{3,2,1,0:T(8,128)(2,1)S(1)}, u32[]{:S(2)}, u32[]{:S(2)}) collective-permute-start(bf16[2,32,16,128]{3,2,1,0:T(8,128)(2,1)} %get-tuple-element.62), channel_id=1, source_target_pairs={{0,6},{1,7},{2,0},{3,1},{4,2},{5,3},{6,4},{7,5},{8,14},{9,15},{10,... | collective-permute-start | bytes 786440 | tf_op jit(solution)/shard_map/ppermute | solution.py:177
  23.4 2.1 %collective-permute-done.6.refs_0_ = bf16[2,32,16,128]{3,2,1,0:T(8,128)(2,1)S(1)} collective-permute-done((bf16[2,32,16,128]{3,2,1,0:T(8,128)(2,1)}, bf16[2,32,16,128]{3,2,1,0:T(8,128)(2,1)S(1)}, u32[]{:S(2)}, u32[]{:S(2)}) %collective-permute-start.6) | collective-permute-done | bytes 262176 | tf_op jit(solution)/shard_map/ppermute | solution.py:177
  25.5 2.7 %collective-permute-start.7 = (bf16[2,32,16,128]{3,2,1,0:T(8,128)(2,1)}, bf16[2,32,16,128]{3,2,1,0:T(8,128)(2,1)S(1)}, u32[]{:S(2)}, u32[]{:S(2)}) collective-permute-start(bf16[2,32,16,128]{3,2,1,0:T(8,128)(2,1)} %get-tuple-element.70), channel_id=1, source_target_pairs={{0,3},{1,2},{2,5},{3,4},{4,7},{5,6},{6,1},{7,0},{8,11},{9,10},{10,... | collective-permute-start | bytes 786440 | tf_op jit(solution)/shard_map/ppermute | solution.py:177
  28.3 0.2 collective-permute-start.10
  28.5 0.1 copy.8
  28.6 1.7 %collective-permute-start.5 = (bf16[2,32,16,128]{3,2,1,0:T(8,128)(2,1)}, bf16[2,32,16,128]{3,2,1,0:T(8,128)(2,1)S(1)}, u32[]{:S(2)}, u32[]{:S(2)}) collective-permute-start(bf16[2,32,16,128]{3,2,1,0:T(8,128)(2,1)} %get-tuple-element.66), channel_id=1, source_target_pairs={{0,4},{1,5},{2,6},{3,7},{4,0},{5,1},{6,2},{7,3},{8,12},{9,13},{10,... | collective-permute-start | bytes 786440 | tf_op jit(solution)/shard_map/ppermute | solution.py:177
  30.3 0.7 collective-permute-done.1.refs_0_
  31.0 5.9 %collective-permute-done.7.refs_5_ = bf16[2,32,16,128]{3,2,1,0:T(8,128)(2,1)S(1)} collective-permute-done((bf16[2,32,16,128]{3,2,1,0:T(8,128)(2,1)}, bf16[2,32,16,128]{3,2,1,0:T(8,128)(2,1)S(1)}, u32[]{:S(2)}, u32[]{:S(2)}) %collective-permute-start.7) | collective-permute-done | bytes 262176 | tf_op jit(solution)/shard_map/ppermute | solution.py:177
  36.9 4.1 %collective-permute-start.8 = (bf16[2,32,16,128]{3,2,1,0:T(8,128)(2,1)}, bf16[2,32,16,128]{3,2,1,0:T(8,128)(2,1)S(1)}, u32[]{:S(2)}, u32[]{:S(2)}) collective-permute-start(bf16[2,32,16,128]{3,2,1,0:T(8,128)(2,1)} %get-tuple-element.71), channel_id=1, source_target_pairs={{0,5},{1,4},{2,7},{3,6},{4,1},{5,0},{6,3},{7,2},{8,13},{9,12},{10,... | collective-permute-start | bytes 786440 | tf_op jit(solution)/shard_map/ppermute | solution.py:177
  40.9 0.1 collective-permute-start.11
  41.0 3.0 %collective-permute-start.13 = (bf16[2,32,16,128]{3,2,1,0:T(8,128)(2,1)S(1)}, bf16[2,32,16,128]{3,2,1,0:T(8,128)(2,1)S(1)}, u32[]{:S(2)}, u32[]{:S(2)}) collective-permute-start(bf16[2,32,16,128]{3,2,1,0:T(8,128)(2,1)S(1)} %copy-done.6), channel_id=1, source_target_pairs={{0,7},{1,6},{2,1},{3,0},{4,3},{5,2},{6,5},{7,4},{8,15},{9,14},{10,... | collective-permute-start | bytes 786440 | tf_op jit(solution)/shard_map/ppermute | solution.py:177
  44.1 0.9 %copy-done.2 = bf16[2,32,16,128]{3,2,1,0:T(8,128)(2,1)S(1)} copy-done((bf16[2,32,16,128]{3,2,1,0:T(8,128)(2,1)S(1)}, bf16[2,32,16,128]{3,2,1,0:T(8,128)(2,1)}, u32[]{:S(2)}) %copy-start.2) | copy-done | bytes 262168
  45.0 2.7 %grads.2 = (f32[128,128]{1,0:T(8,128)S(1)}, f32[128,128]{1,0:T(8,128)S(1)}) custom-call(bf16[2,32,16,128]{3,2,1,0:T(8,128)(2,1)S(1)} %collective-permute-done.6.refs_0_, bf16[2,32,16,128]{3,2,1,0:T(8,128)(2,1)S(1)} %collective-permute-done.9.refs_1_, bf16[2,32,16,128]{3,2,1,0:T(8,128)(2,1)S(1)} %collective-permute-done.refs_2_, ...), custom_call_target="tpu_custom_call" | custom-call | flops 671088640 | bytes 2097152 | tf_op jit(solution)/shard_map/grads/pallas_call | solution.py:102
  47.7 0.3 collective-permute-done.8.refs_3_
  48.0 5.5 %collective-permute-done.12.refs_5_ = bf16[2,32,16,128]{3,2,1,0:T(8,128)(2,1)S(1)} collective-permute-done((bf16[2,32,16,128]{3,2,1,0:T(8,128)(2,1)S(1)}, bf16[2,32,16,128]{3,2,1,0:T(8,128)(2,1)S(1)}, u32[]{:S(2)}, u32[]{:S(2)}) %collective-permute-start.12) | collective-permute-done | bytes 262176 | tf_op jit(solution)/shard_map/ppermute | solution.py:177
  53.6 0.0 collective-permute-done.13.refs_6_
  53.6 2.7 %grads.3 = (f32[128,128]{1,0:T(8,128)S(1)}, f32[128,128]{1,0:T(8,128)S(1)}) custom-call(bf16[2,32,16,128]{3,2,1,0:T(8,128)(2,1)S(1)} %collective-permute-done.1.refs_0_, bf16[2,32,16,128]{3,2,1,0:T(8,128)(2,1)S(1)} %collective-permute-done.3.refs_1_, bf16[2,32,16,128]{3,2,1,0:T(8,128)(2,1)S(1)} %collective-permute-done.5.refs_2_, ...), custom_call_target="tpu_custom_call" | custom-call | flops 671088640 | bytes 2097152 | tf_op jit(solution)/shard_map/grads/pallas_call | solution.py:102
  56.3 0.5 collective-permute-start.14
  56.8 0.9 collective-permute-done.14
  57.7 2.6 %collective-permute-start.17 = (bf16[128,128]{1,0:T(8,128)(2,1)S(1)}, bf16[128,128]{1,0:T(8,128)(2,1)S(1)}, u32[]{:S(2)}, u32[]{:S(2)}) collective-permute-start(bf16[128,128]{1,0:T(8,128)(2,1)S(1)} %add_convert_fusion.2), channel_id=1, source_target_pairs={{0,6},{1,25},{2,0},{3,27},{4,2},{5,29},{6,4},{7,31},{8,14},{9,1},{... | collective-permute-start | bytes 98312 | tf_op jit(solution)/shard_map/ppermute | solution.py:141
  60.2 1.7 %collective-permute-start.15 = (bf16[128,128]{1,0:T(8,128)(2,1)S(1)}, bf16[128,128]{1,0:T(8,128)(2,1)S(1)}, u32[]{:S(2)}, u32[]{:S(2)}) collective-permute-start(bf16[128,128]{1,0:T(8,128)(2,1)S(1)} %add_convert_fusion.2), channel_id=1, source_target_pairs={{0,4},{1,17},{2,6},{3,19},{4,0},{5,21},{6,2},{7,23},{8,12},{9,25},... | collective-permute-start | bytes 98312 | tf_op jit(solution)/shard_map/ppermute | solution.py:141
  62.0 2.3 %collective-permute-done.16 = bf16[128,128]{1,0:T(8,128)(2,1)S(1)} collective-permute-done((bf16[128,128]{1,0:T(8,128)(2,1)S(1)}, bf16[128,128]{1,0:T(8,128)(2,1)S(1)}, u32[]{:S(2)}, u32[]{:S(2)}) %collective-permute-start.16) | collective-permute-done | bytes 32800 | tf_op jit(solution)/shard_map/ppermute | solution.py:141
  64.2 0.3 collective-permute-done.15
  64.6 2.7 %collective-permute-start.20 = (bf16[128,128]{1,0:T(8,128)(2,1)S(1)}, bf16[128,128]{1,0:T(8,128)(2,1)S(1)}, u32[]{:S(2)}, u32[]{:S(2)}) collective-permute-start(bf16[128,128]{1,0:T(8,128)(2,1)S(1)} %add_convert_fusion.1), channel_id=1, source_target_pairs={{0,24},{1,7},{2,26},{3,1},{4,28},{5,3},{6,30},{7,5},{8,0},{9,15},{... | collective-permute-start | bytes 98312 | tf_op jit(solution)/shard_map/ppermute | solution.py:141
  67.3 1.7 %collective-permute-start.18 = (bf16[128,128]{1,0:T(8,128)(2,1)S(1)}, bf16[128,128]{1,0:T(8,128)(2,1)S(1)}, u32[]{:S(2)}, u32[]{:S(2)}) collective-permute-start(bf16[128,128]{1,0:T(8,128)(2,1)S(1)} %add_convert_fusion.1), channel_id=1, source_target_pairs={{0,16},{1,5},{2,18},{3,7},{4,20},{5,1},{6,22},{7,3},{8,24},{9,13},... | collective-permute-start | bytes 98312 | tf_op jit(solution)/shard_map/ppermute | solution.py:141
  69.0 2.3 %collective-permute-done.19 = bf16[128,128]{1,0:T(8,128)(2,1)S(1)} collective-permute-done((bf16[128,128]{1,0:T(8,128)(2,1)S(1)}, bf16[128,128]{1,0:T(8,128)(2,1)S(1)}, u32[]{:S(2)}, u32[]{:S(2)}) %collective-permute-start.19) | collective-permute-done | bytes 32800 | tf_op jit(solution)/shard_map/ppermute | solution.py:141
  71.3 0.3 collective-permute-done.18
  71.7 4.4 %collective-permute-start.23 = (bf16[128,128]{1,0:T(8,128)(2,1)S(1)}, bf16[128,128]{1,0:T(8,128)(2,1)S(1)}, u32[]{:S(2)}, u32[]{:S(2)}) collective-permute-start(bf16[128,128]{1,0:T(8,128)(2,1)S(1)} %add_convert_fusion), channel_id=1, source_target_pairs={{0,96},{1,97},{2,98},{3,99},{4,100},{5,101},{6,102},{7,103},{8,104... | collective-permute-start | bytes 98312 | tf_op jit(solution)/shard_map/ppermute | solution.py:141
  76.1 0.4 collective-permute-start.21
  76.5 0.7 collective-permute-done.23
  77.1 3.6 %collective-permute-done.22 = bf16[128,128]{1,0:T(8,128)(2,1)S(1)} collective-permute-done((bf16[128,128]{1,0:T(8,128)(2,1)S(1)}, bf16[128,128]{1,0:T(8,128)(2,1)S(1)}, u32[]{:S(2)}, u32[]{:S(2)}) %collective-permute-start.22) | collective-permute-done | bytes 32800 | tf_op jit(solution)/shard_map/ppermute | solution.py:141
  80.8 2.2 %collective-permute-start.24 = (f32[128,128]{1,0:T(8,128)S(1)}, f32[128,128]{1,0:T(8,128)S(1)}, u32[]{:S(2)}, u32[]{:S(2)}) collective-permute-start(f32[128,128]{1,0:T(8,128)S(1)} %add_add_fusion), channel_id=1, source_target_pairs={{0,192},{1,193},{2,194},{3,195},{4,196},{5,197},{6,198},{7,199},{8... | collective-permute-start | bytes 196616 | tf_op jit(solution)/shard_map/ppermute | solution.py:155
  83.0 3.2 %collective-permute-done.24 = f32[128,128]{1,0:T(8,128)S(1)} collective-permute-done((f32[128,128]{1,0:T(8,128)S(1)}, f32[128,128]{1,0:T(8,128)S(1)}, u32[]{:S(2)}, u32[]{:S(2)}) %collective-permute-start.24) | collective-permute-done | bytes 65568 | tf_op jit(solution)/shard_map/ppermute | solution.py:155
  86.2 5.7 %collective-permute-start.25 = (f32[128,128]{1,0:T(8,128)S(1)}, f32[128,128]{1,0:T(8,128)S(1)}, u32[]{:S(2)}, u32[]{:S(2)}) collective-permute-start(f32[128,128]{1,0:T(8,128)S(1)} %add.50), channel_id=1, source_target_pairs={{0,1},{1,0},{2,3},{3,2},{4,5},{5,4},{6,7},{7,6},{8,9},{9,8},{10,11... | collective-permute-start | bytes 196616 | tf_op jit(solution)/shard_map/ppermute | solution.py:156
  91.9 0.9 collective-permute-done.25
  92.8 0.7 broadcast_select_fusion
  (35 shorter events, 0.2 us)
Async XLA Ops:
  3.2 14.6 %collective-permute-start = (bf16[2,32,16,128]{3,2,1,0:T(8,128)(2,1)}, bf16[2,32,16,128]{3,2,1,0:T(8,128)(2,1)S(1)}, u32[]{:S(2)}, u32[]{:S(2)}) collective-permute-start(bf16[2,32,16,128]{3,2,1,0:T(8,128)(2,1)} %get-tuple-element.56), channel_id=1, source_target_pairs={{0,4},{1,5},{2,6},{3,7},{4,0},{5,1},{6,2},{7,3},{8,12},{9,13},{10,... | collective-permute-start | bytes 786440 | tf_op jit(solution)/shard_map/ppermute | solution.py:177
  7.0 14.5 %collective-permute-start.2 = (bf16[2,32,16,128]{3,2,1,0:T(8,128)(2,1)}, bf16[2,32,16,128]{3,2,1,0:T(8,128)(2,1)S(1)}, u32[]{:S(2)}, u32[]{:S(2)}) collective-permute-start(bf16[2,32,16,128]{3,2,1,0:T(8,128)(2,1)} %get-tuple-element.61), channel_id=1, source_target_pairs={{0,5},{1,4},{2,7},{3,6},{4,1},{5,0},{6,3},{7,2},{8,13},{9,12},{10,... | collective-permute-start | bytes 786440 | tf_op jit(solution)/shard_map/ppermute | solution.py:177
  9.7 15.9 %collective-permute-start.6 = (bf16[2,32,16,128]{3,2,1,0:T(8,128)(2,1)}, bf16[2,32,16,128]{3,2,1,0:T(8,128)(2,1)S(1)}, u32[]{:S(2)}, u32[]{:S(2)}) collective-permute-start(bf16[2,32,16,128]{3,2,1,0:T(8,128)(2,1)} %get-tuple-element.69), channel_id=1, source_target_pairs={{0,2},{1,3},{2,4},{3,5},{4,6},{5,7},{6,0},{7,1},{8,10},{9,11},{10,... | collective-permute-start | bytes 786440 | tf_op jit(solution)/shard_map/ppermute | solution.py:177
  9.7 18.6 %collective-permute-start.9 = (bf16[2,32,16,128]{3,2,1,0:T(8,128)(2,1)}, bf16[2,32,16,128]{3,2,1,0:T(8,128)(2,1)S(1)}, u32[]{:S(2)}, u32[]{:S(2)}) collective-permute-start(bf16[2,32,16,128]{3,2,1,0:T(8,128)(2,1)} %get-tuple-element.74), channel_id=1, source_target_pairs={{0,6},{1,7},{2,0},{3,1},{4,2},{5,3},{6,4},{7,5},{8,14},{9,15},{10,... | collective-permute-start | bytes 786440 | tf_op jit(solution)/shard_map/ppermute | solution.py:177
  12.3 16.3 %collective-permute-start.4 = (bf16[2,32,16,128]{3,2,1,0:T(8,128)(2,1)}, bf16[2,32,16,128]{3,2,1,0:T(8,128)(2,1)S(1)}, u32[]{:S(2)}, u32[]{:S(2)}) collective-permute-start(bf16[2,32,16,128]{3,2,1,0:T(8,128)(2,1)} %get-tuple-element.65), channel_id=1, source_target_pairs={{0,1},{1,0},{2,3},{3,2},{4,5},{5,4},{6,7},{7,6},{8,9},{9,8},{10,11... | collective-permute-start | bytes 786440 | tf_op jit(solution)/shard_map/ppermute | solution.py:177
  15.4 13.1 %copy-start = (bf16[128,128]{1,0:T(8,128)(2,1)S(1)}, bf16[128,128]{1,0:T(8,128)(2,1)}, u32[]{:S(2)}) copy-start(bf16[128,128]{1,0:T(8,128)(2,1)} %refs_8_.3) | copy-start | bytes 98308
  15.4 25.6 %copy-start.7 = (bf16[2,32,16,128]{3,2,1,0:T(8,128)(2,1)S(1)}, bf16[2,32,16,128]{3,2,1,0:T(8,128)(2,1)}, u32[]{:S(2)}) copy-start(bf16[2,32,16,128]{3,2,1,0:T(8,128)(2,1)} %get-tuple-element.77) | copy-start | bytes 786436
  15.4 25.6 %copy-start.6 = (bf16[2,32,16,128]{3,2,1,0:T(8,128)(2,1)S(1)}, bf16[2,32,16,128]{3,2,1,0:T(8,128)(2,1)}, u32[]{:S(2)}) copy-start(bf16[2,32,16,128]{3,2,1,0:T(8,128)(2,1)} %get-tuple-element.78) | copy-start | bytes 786436
  15.5 28.5 %copy-start.4 = (s32[128,128]{1,0:T(8,128)S(1)}, s32[128,128]{1,0:T(8,128)}, u32[]{:S(2)}) copy-start(s32[128,128]{1,0:T(8,128)} %param.10) | copy-start | bytes 196612
  15.5 28.5 %copy-start.5 = (s32[128,128]{1,0:T(8,128)S(1)}, s32[128,128]{1,0:T(8,128)}, u32[]{:S(2)}) copy-start(s32[128,128]{1,0:T(8,128)} %param.11) | copy-start | bytes 196612
  15.5 28.6 %copy-start.3 = (bf16[128,128]{1,0:T(8,128)(2,1)S(1)}, bf16[128,128]{1,0:T(8,128)(2,1)}, u32[]{:S(2)}) copy-start(bf16[128,128]{1,0:T(8,128)(2,1)} %refs_10_.3) | copy-start | bytes 98308
  17.7 35.8 %copy-start.1 = (bf16[2,32,16,128]{3,2,1,0:T(8,128)(2,1)S(1)}, bf16[2,32,16,128]{3,2,1,0:T(8,128)(2,1)}, u32[]{:S(2)}) copy-start(bf16[2,32,16,128]{3,2,1,0:T(8,128)(2,1)} %get-tuple-element.79.refs_7_) | copy-start | bytes 786436
  17.8 13.2 %collective-permute-start.1 = (bf16[2,32,16,128]{3,2,1,0:T(8,128)(2,1)}, bf16[2,32,16,128]{3,2,1,0:T(8,128)(2,1)S(1)}, u32[]{:S(2)}, u32[]{:S(2)}) collective-permute-start(bf16[2,32,16,128]{3,2,1,0:T(8,128)(2,1)} %get-tuple-element.57), channel_id=1, source_target_pairs={{0,2},{1,3},{2,4},{3,5},{4,6},{5,7},{6,0},{7,1},{8,10},{9,11},{10,... | collective-permute-start | bytes 786440 | tf_op jit(solution)/shard_map/ppermute | solution.py:177
  21.5 9.5 %collective-permute-start.3 = (bf16[2,32,16,128]{3,2,1,0:T(8,128)(2,1)}, bf16[2,32,16,128]{3,2,1,0:T(8,128)(2,1)S(1)}, u32[]{:S(2)}, u32[]{:S(2)}) collective-permute-start(bf16[2,32,16,128]{3,2,1,0:T(8,128)(2,1)} %get-tuple-element.62), channel_id=1, source_target_pairs={{0,6},{1,7},{2,0},{3,1},{4,2},{5,3},{6,4},{7,5},{8,14},{9,15},{10,... | collective-permute-start | bytes 786440 | tf_op jit(solution)/shard_map/ppermute | solution.py:177
  25.5 11.3 %collective-permute-start.7 = (bf16[2,32,16,128]{3,2,1,0:T(8,128)(2,1)}, bf16[2,32,16,128]{3,2,1,0:T(8,128)(2,1)S(1)}, u32[]{:S(2)}, u32[]{:S(2)}) collective-permute-start(bf16[2,32,16,128]{3,2,1,0:T(8,128)(2,1)} %get-tuple-element.70), channel_id=1, source_target_pairs={{0,3},{1,2},{2,5},{3,4},{4,7},{5,6},{6,1},{7,0},{8,11},{9,10},{10,... | collective-permute-start | bytes 786440 | tf_op jit(solution)/shard_map/ppermute | solution.py:177
  28.3 12.7 %collective-permute-start.10 = (bf16[2,32,16,128]{3,2,1,0:T(8,128)(2,1)}, bf16[2,32,16,128]{3,2,1,0:T(8,128)(2,1)S(1)}, u32[]{:S(2)}, u32[]{:S(2)}) collective-permute-start(bf16[2,32,16,128]{3,2,1,0:T(8,128)(2,1)} %get-tuple-element.75), channel_id=1, source_target_pairs={{0,7},{1,6},{2,1},{3,0},{4,3},{5,2},{6,5},{7,4},{8,15},{9,14},{10,... | collective-permute-start | bytes 786440 | tf_op jit(solution)/shard_map/ppermute | solution.py:177
  28.6 19.1 %collective-permute-start.5 = (bf16[2,32,16,128]{3,2,1,0:T(8,128)(2,1)}, bf16[2,32,16,128]{3,2,1,0:T(8,128)(2,1)S(1)}, u32[]{:S(2)}, u32[]{:S(2)}) collective-permute-start(bf16[2,32,16,128]{3,2,1,0:T(8,128)(2,1)} %get-tuple-element.66), channel_id=1, source_target_pairs={{0,4},{1,5},{2,6},{3,7},{4,0},{5,1},{6,2},{7,3},{8,12},{9,13},{10,... | collective-permute-start | bytes 786440 | tf_op jit(solution)/shard_map/ppermute | solution.py:177
  36.9 11.2 %collective-permute-start.8 = (bf16[2,32,16,128]{3,2,1,0:T(8,128)(2,1)}, bf16[2,32,16,128]{3,2,1,0:T(8,128)(2,1)S(1)}, u32[]{:S(2)}, u32[]{:S(2)}) collective-permute-start(bf16[2,32,16,128]{3,2,1,0:T(8,128)(2,1)} %get-tuple-element.71), channel_id=1, source_target_pairs={{0,5},{1,4},{2,7},{3,6},{4,1},{5,0},{6,3},{7,2},{8,13},{9,12},{10,... | collective-permute-start | bytes 786440 | tf_op jit(solution)/shard_map/ppermute | solution.py:177
  40.9 7.1 %collective-permute-start.11 = (bf16[2,32,16,128]{3,2,1,0:T(8,128)(2,1)}, bf16[2,32,16,128]{3,2,1,0:T(8,128)(2,1)S(1)}, u32[]{:S(2)}, u32[]{:S(2)}) collective-permute-start(bf16[2,32,16,128]{3,2,1,0:T(8,128)(2,1)} %get-tuple-element.76), channel_id=1, source_target_pairs={{0,1},{1,0},{2,3},{3,2},{4,5},{5,4},{6,7},{7,6},{8,9},{9,8},{10,11... | collective-permute-start | bytes 786440 | tf_op jit(solution)/shard_map/ppermute | solution.py:177
  41.0 12.5 %collective-permute-start.12 = (bf16[2,32,16,128]{3,2,1,0:T(8,128)(2,1)S(1)}, bf16[2,32,16,128]{3,2,1,0:T(8,128)(2,1)S(1)}, u32[]{:S(2)}, u32[]{:S(2)}) collective-permute-start(bf16[2,32,16,128]{3,2,1,0:T(8,128)(2,1)S(1)} %copy-done.7), channel_id=1, source_target_pairs={{0,3},{1,2},{2,5},{3,4},{4,7},{5,6},{6,1},{7,0},{8,11},{9,10},{10,... | collective-permute-start | bytes 786440 | tf_op jit(solution)/shard_map/ppermute | solution.py:177
  41.0 12.5 %collective-permute-start.13 = (bf16[2,32,16,128]{3,2,1,0:T(8,128)(2,1)S(1)}, bf16[2,32,16,128]{3,2,1,0:T(8,128)(2,1)S(1)}, u32[]{:S(2)}, u32[]{:S(2)}) collective-permute-start(bf16[2,32,16,128]{3,2,1,0:T(8,128)(2,1)S(1)} %copy-done.6), channel_id=1, source_target_pairs={{0,7},{1,6},{2,1},{3,0},{4,3},{5,2},{6,5},{7,4},{8,15},{9,14},{10,... | collective-permute-start | bytes 786440 | tf_op jit(solution)/shard_map/ppermute | solution.py:177
  44.1 1.0 %copy-start.2 = (bf16[2,32,16,128]{3,2,1,0:T(8,128)(2,1)S(1)}, bf16[2,32,16,128]{3,2,1,0:T(8,128)(2,1)}, u32[]{:S(2)}) copy-start(bf16[2,32,16,128]{3,2,1,0:T(8,128)(2,1)} %get-tuple-element.87.refs_7_) | copy-start | bytes 786436
  56.3 1.4 %collective-permute-start.14 = (f32[128,128]{1,0:T(8,128)S(1)}, f32[128,128]{1,0:T(8,128)S(1)}, u32[]{:S(2)}, u32[]{:S(2)}) collective-permute-start(f32[128,128]{1,0:T(8,128)S(1)} %broadcast_select_fusion.2), channel_id=1, source_target_pairs={{0,1},{1,0},{2,3},{3,2},{4,5},{5,4},{6,7},{7,6},{8,9},{9,8},{10,11... | collective-permute-start | bytes 196616 | tf_op jit(solution)/shard_map/ppermute | solution.py:151
  57.7 4.3 %collective-permute-start.17 = (bf16[128,128]{1,0:T(8,128)(2,1)S(1)}, bf16[128,128]{1,0:T(8,128)(2,1)S(1)}, u32[]{:S(2)}, u32[]{:S(2)}) collective-permute-start(bf16[128,128]{1,0:T(8,128)(2,1)S(1)} %add_convert_fusion.2), channel_id=1, source_target_pairs={{0,6},{1,25},{2,0},{3,27},{4,2},{5,29},{6,4},{7,31},{8,14},{9,1},{... | collective-permute-start | bytes 98312 | tf_op jit(solution)/shard_map/ppermute | solution.py:141
  60.2 4.0 %collective-permute-start.16 = (bf16[128,128]{1,0:T(8,128)(2,1)S(1)}, bf16[128,128]{1,0:T(8,128)(2,1)S(1)}, u32[]{:S(2)}, u32[]{:S(2)}) collective-permute-start(bf16[128,128]{1,0:T(8,128)(2,1)S(1)} %add_convert_fusion.2), channel_id=1, source_target_pairs={{0,2},{1,9},{2,4},{3,11},{4,6},{5,13},{6,0},{7,15},{8,10},{9,17},{... | collective-permute-start | bytes 98312 | tf_op jit(solution)/shard_map/ppermute | solution.py:141
  60.2 4.3 %collective-permute-start.15 = (bf16[128,128]{1,0:T(8,128)(2,1)S(1)}, bf16[128,128]{1,0:T(8,128)(2,1)S(1)}, u32[]{:S(2)}, u32[]{:S(2)}) collective-permute-start(bf16[128,128]{1,0:T(8,128)(2,1)S(1)} %add_convert_fusion.2), channel_id=1, source_target_pairs={{0,4},{1,17},{2,6},{3,19},{4,0},{5,21},{6,2},{7,23},{8,12},{9,25},... | collective-permute-start | bytes 98312 | tf_op jit(solution)/shard_map/ppermute | solution.py:141
  64.6 4.4 %collective-permute-start.20 = (bf16[128,128]{1,0:T(8,128)(2,1)S(1)}, bf16[128,128]{1,0:T(8,128)(2,1)S(1)}, u32[]{:S(2)}, u32[]{:S(2)}) collective-permute-start(bf16[128,128]{1,0:T(8,128)(2,1)S(1)} %add_convert_fusion.1), channel_id=1, source_target_pairs={{0,24},{1,7},{2,26},{3,1},{4,28},{5,3},{6,30},{7,5},{8,0},{9,15},{... | collective-permute-start | bytes 98312 | tf_op jit(solution)/shard_map/ppermute | solution.py:141
  67.3 4.0 %collective-permute-start.19 = (bf16[128,128]{1,0:T(8,128)(2,1)S(1)}, bf16[128,128]{1,0:T(8,128)(2,1)S(1)}, u32[]{:S(2)}, u32[]{:S(2)}) collective-permute-start(bf16[128,128]{1,0:T(8,128)(2,1)S(1)} %add_convert_fusion.1), channel_id=1, source_target_pairs={{0,8},{1,3},{2,10},{3,5},{4,12},{5,7},{6,14},{7,1},{8,16},{9,11},{... | collective-permute-start | bytes 98312 | tf_op jit(solution)/shard_map/ppermute | solution.py:141
  67.3 4.3 %collective-permute-start.18 = (bf16[128,128]{1,0:T(8,128)(2,1)S(1)}, bf16[128,128]{1,0:T(8,128)(2,1)S(1)}, u32[]{:S(2)}, u32[]{:S(2)}) collective-permute-start(bf16[128,128]{1,0:T(8,128)(2,1)S(1)} %add_convert_fusion.1), channel_id=1, source_target_pairs={{0,16},{1,5},{2,18},{3,7},{4,20},{5,1},{6,22},{7,3},{8,24},{9,13},... | collective-permute-start | bytes 98312 | tf_op jit(solution)/shard_map/ppermute | solution.py:141
  71.7 5.4 %collective-permute-start.23 = (bf16[128,128]{1,0:T(8,128)(2,1)S(1)}, bf16[128,128]{1,0:T(8,128)(2,1)S(1)}, u32[]{:S(2)}, u32[]{:S(2)}) collective-permute-start(bf16[128,128]{1,0:T(8,128)(2,1)S(1)} %add_convert_fusion), channel_id=1, source_target_pairs={{0,96},{1,97},{2,98},{3,99},{4,100},{5,101},{6,102},{7,103},{8,104... | collective-permute-start | bytes 98312 | tf_op jit(solution)/shard_map/ppermute | solution.py:141
  76.1 4.7 %collective-permute-start.22 = (bf16[128,128]{1,0:T(8,128)(2,1)S(1)}, bf16[128,128]{1,0:T(8,128)(2,1)S(1)}, u32[]{:S(2)}, u32[]{:S(2)}) collective-permute-start(bf16[128,128]{1,0:T(8,128)(2,1)S(1)} %add_convert_fusion), channel_id=1, source_target_pairs={{0,32},{1,33},{2,34},{3,35},{4,36},{5,37},{6,38},{7,39},{8,40},{9,... | collective-permute-start | bytes 98312 | tf_op jit(solution)/shard_map/ppermute | solution.py:141
  76.1 4.7 %collective-permute-start.21 = (bf16[128,128]{1,0:T(8,128)(2,1)S(1)}, bf16[128,128]{1,0:T(8,128)(2,1)S(1)}, u32[]{:S(2)}, u32[]{:S(2)}) collective-permute-start(bf16[128,128]{1,0:T(8,128)(2,1)S(1)} %add_convert_fusion), channel_id=1, source_target_pairs={{0,64},{1,65},{2,66},{3,67},{4,68},{5,69},{6,70},{7,71},{8,72},{9,... | collective-permute-start | bytes 98312 | tf_op jit(solution)/shard_map/ppermute | solution.py:141
  80.8 5.4 %collective-permute-start.24 = (f32[128,128]{1,0:T(8,128)S(1)}, f32[128,128]{1,0:T(8,128)S(1)}, u32[]{:S(2)}, u32[]{:S(2)}) collective-permute-start(f32[128,128]{1,0:T(8,128)S(1)} %add_add_fusion), channel_id=1, source_target_pairs={{0,192},{1,193},{2,194},{3,195},{4,196},{5,197},{6,198},{7,199},{8... | collective-permute-start | bytes 196616 | tf_op jit(solution)/shard_map/ppermute | solution.py:155
  86.2 6.6 %collective-permute-start.25 = (f32[128,128]{1,0:T(8,128)S(1)}, f32[128,128]{1,0:T(8,128)S(1)}, u32[]{:S(2)}, u32[]{:S(2)}) collective-permute-start(f32[128,128]{1,0:T(8,128)S(1)} %add.50), channel_id=1, source_target_pairs={{0,1},{1,0},{2,3},{3,2},{4,5},{5,4},{6,7},{7,6},{8,9},{9,8},{10,11... | collective-permute-start | bytes 196616 | tf_op jit(solution)/shard_map/ppermute | solution.py:156

commit v5 on v4

--- a/solution.py
+++ b/solution.py
@@ -9,7 +9,7 @@
 
 F32 = jnp.float32
 BF16 = jnp.bfloat16
-STEP_TOKENS = 8
+STEP_TOKENS = 16
 ROWS = 16
 PARTS = (32, 32)
 WINDOW = 5
@@ -72,13 +72,13 @@
     total = parts[0].shape[1]
     tokens = min(STEP_TOKENS, total)
     grad_left, grad_right = gl_in[...], gr_in[...]
-    for k, (dy, dc) in enumerate(hops + OWN):
-        source = peer(-dy, dc)
-        for t in range(total):
-            rows = pl.ds(pl.multiple_of(t * 128 + source * ROWS, ROWS), ROWS)
-            act_all[rows, :] = parts[k][0, t]
-            cot_all[rows, :] = parts[k][1, t]
+    sources = [peer(-dy, dc) * ROWS for dy, dc in hops + OWN]
     for first in range(0, total, tokens):
+        for k, source in enumerate(sources):
+            for t in range(first, first + tokens):
+                rows = pl.ds(pl.multiple_of(t * 128 + source, ROWS), ROWS)
+                act_all[rows, :] = parts[k][0, t]
+                cot_all[rows, :] = parts[k][1, t]
         act = act_all[first * 128 : (first + tokens) * 128, :]
         rot = jnp.dot(act, right, preferred_element_type=F32).astype(BF16)
         rot = jnp.concatenate([rot[t * 128 : (t + 1) * 128] for t in range(tokens)], axis=1)

time: 93.7 us -> 93.1 us (level)
  Pallas kernels: 13.3 us -> 12.1 us
    pallas_call x2, Pallas kernels: 5.41 us -> 4.18 us  [local_grads(): pl.pallas_call(functools.partial(grads_kernel, hops), in_specs=[pl.BlockS...]
  transfers between devices with their start and end apart: 26 -> 26, of which waited for: 15 -> 15; matrix products, arithmetic and copies ran while one was open for 0% -> 0% of each run, Pallas kernels for 9% -> 8%
where the time goes in v5:
time: 93.1 us; the launch traced here: 92.9 us
  starting transfers between devices  44.8 us (48%)
  waiting for transfers between devices  33.3 us (36%)
  Pallas kernels  12.1 us (13%)
  local copies, waits for them, and re-layouts  1.1 us (1%)
    ppermute x14, starting transfers between devices, exchange(): block = lax.ppermute(block, 'tensor', tensor_shift(dy, dc))  22.8 us
    ppermute x14, waiting for transfers between devices, exchange(): block = lax.ppermute(block, 'tensor', tensor_shift(dy, dc))  18.8 us
    ppermute x9, starting transfers between devices, add_four(): lax.ppermute(x, ALL, route(axes, s))  13.5 us
    ppermute x9, waiting for transfers between devices, add_four(): lax.ppermute(x, ALL, route(axes, s))  9.53 us
    pallas_call x3, Pallas kernels, pack(): pl.pallas_call(functools.partial(pack_kernel, first, hops), in_specs=[pl....  7.88 us
    ppermute x1, starting transfers between devices, sum_all(): other = lax.ppermute(x, 'tensor', swap)  5.74 us
    pallas_call x2, Pallas kernels, local_grads(): pl.pallas_call(functools.partial(grads_kernel, hops), in_specs=[pl.BlockS...  4.18 us
    ppermute x1, waiting for transfers between devices, sum_all(): x = x + lax.ppermute(x, ALL, route('hh', 1))  3.18 us
  transfers between devices with their start and end apart: 26, of which 15 were waited for; matrix products, arithmetic and copies ran while one was open for 0% of the time, Pallas kernels for 8%

profile of v5, /device:TPU:1, one launch (start us, length us, event | category | flops | bytes accessed | tf_op | source)
XLA Modules:
  0.0 92.9 jit_solution(5453305990771860776)
XLA Ops:
  0.6 2.6 %pack.3 = (bf16[2,32,16,128]{3,2,1,0:T(8,128)(2,1)}, bf16[2,32,16,128]{3,2,1,0:T(8,128)(2,1)}, bf16[2,32,16,128]{3,2,1,0:T(8,128)(2,1)}, bf16[2,32,16,128]{3,2,1,0:T(8,128)(2,1)}, bf16[2,32,16,128]{3,2,1,0:T(8,128)(2,1)}) custom-call(bf16[8,64,16,128]{3,2,1,0:T(8,128)(2,1)} %bitcast.5, bf16[8,64,16,128]{3,2,1,0:T(8,128)(2,1)} %bitcast.8), custom_call_target="tpu_custom_call" | custom-call | bytes 2621440 | tf_op jit(solution)/shard_map/pack/pallas_call | solution.py:55
  3.2 3.8 %collective-permute-start = (bf16[2,32,16,128]{3,2,1,0:T(8,128)(2,1)}, bf16[2,32,16,128]{3,2,1,0:T(8,128)(2,1)S(1)}, u32[]{:S(2)}, u32[]{:S(2)}) collective-permute-start(bf16[2,32,16,128]{3,2,1,0:T(8,128)(2,1)} %get-tuple-element.56), channel_id=1, source_target_pairs={{0,4},{1,5},{2,6},{3,7},{4,0},{5,1},{6,2},{7,3},{8,12},{9,13},{10,... | collective-permute-start | bytes 786440 | tf_op jit(solution)/shard_map/ppermute | solution.py:177
  7.0 2.6 %collective-permute-start.2 = (bf16[2,32,16,128]{3,2,1,0:T(8,128)(2,1)}, bf16[2,32,16,128]{3,2,1,0:T(8,128)(2,1)S(1)}, u32[]{:S(2)}, u32[]{:S(2)}) collective-permute-start(bf16[2,32,16,128]{3,2,1,0:T(8,128)(2,1)} %get-tuple-element.61), channel_id=1, source_target_pairs={{0,5},{1,4},{2,7},{3,6},{4,1},{5,0},{6,3},{7,2},{8,13},{9,12},{10,... | collective-permute-start | bytes 786440 | tf_op jit(solution)/shard_map/ppermute | solution.py:177
  9.7 2.7 %collective-permute-start.9 = (bf16[2,32,16,128]{3,2,1,0:T(8,128)(2,1)}, bf16[2,32,16,128]{3,2,1,0:T(8,128)(2,1)S(1)}, u32[]{:S(2)}, u32[]{:S(2)}) collective-permute-start(bf16[2,32,16,128]{3,2,1,0:T(8,128)(2,1)} %get-tuple-element.74), channel_id=1, source_target_pairs={{0,6},{1,7},{2,0},{3,1},{4,2},{5,3},{6,4},{7,5},{8,14},{9,15},{10,... | collective-permute-start | bytes 786440 | tf_op jit(solution)/shard_map/ppermute | solution.py:177
  12.3 3.1 %pack.4 = (bf16[2,32,16,128]{3,2,1,0:T(8,128)(2,1)}, bf16[2,32,16,128]{3,2,1,0:T(8,128)(2,1)}, bf16[2,32,16,128]{3,2,1,0:T(8,128)(2,1)}, bf16[2,32,16,128]{3,2,1...) custom-call(bf16[8,64,16,128]{3,2,1,0:T(8,128)(2,1)} %bitcast.6, ...), custom_call_target="tpu_custom_call" | custom-call | bytes 4194304 | tf_op jit(solution)/shard_map/pack/pallas_call | solution.py:55
  15.4 0.0 copy-start
  15.5 0.0 copy-start.4
  15.5 0.0 copy-start.5
  15.5 0.0 copy-start.3
  15.5 2.2 %pack.5 = (bf16[2,32,16,128]{3,2,1,0:T(8,128)(2,1)}, bf16[2,32,16,128]{3,2,1,0:T(8,128)(2,1)}, bf16[2,32,16,128]{3,2,1,0:T(8,128)(2,1)}) custom-call(bf16[8,64,16,128]{3,2,1,0:T(8,128)(2,1)} %bitcast.7, bf16[8,64,16,128]{3,2,1,0:T(8,128)(2,1)} %bitcast.10), custom_call_target="tpu_custom_call" | custom-call | bytes 1572864 | tf_op jit(solution)/shard_map/pack/pallas_call | solution.py:55
  17.8 0.1 collective-permute-start.1
  17.9 3.7 %collective-permute-done.2.refs_3_ = bf16[2,32,16,128]{3,2,1,0:T(8,128)(2,1)S(1)} collective-permute-done((bf16[2,32,16,128]{3,2,1,0:T(8,128)(2,1)}, bf16[2,32,16,128]{3,2,1,0:T(8,128)(2,1)S(1)}, u32[]{:S(2)}, u32[]{:S(2)}) %collective-permute-start.2) | collective-permute-done | bytes 262176 | tf_op jit(solution)/shard_map/ppermute | solution.py:177
  21.5 1.9 %collective-permute-start.3 = (bf16[2,32,16,128]{3,2,1,0:T(8,128)(2,1)}, bf16[2,32,16,128]{3,2,1,0:T(8,128)(2,1)S(1)}, u32[]{:S(2)}, u32[]{:S(2)}) collective-permute-start(bf16[2,32,16,128]{3,2,1,0:T(8,128)(2,1)} %get-tuple-element.62), channel_id=1, source_target_pairs={{0,6},{1,7},{2,0},{3,1},{4,2},{5,3},{6,4},{7,5},{8,14},{9,15},{10,... | collective-permute-start | bytes 786440 | tf_op jit(solution)/shard_map/ppermute | solution.py:177
  23.4 2.1 %collective-permute-done.6.refs_0_ = bf16[2,32,16,128]{3,2,1,0:T(8,128)(2,1)S(1)} collective-permute-done((bf16[2,32,16,128]{3,2,1,0:T(8,128)(2,1)}, bf16[2,32,16,128]{3,2,1,0:T(8,128)(2,1)S(1)}, u32[]{:S(2)}, u32[]{:S(2)}) %collective-permute-start.6) | collective-permute-done | bytes 262176 | tf_op jit(solution)/shard_map/ppermute | solution.py:177
  25.5 2.7 %collective-permute-start.7 = (bf16[2,32,16,128]{3,2,1,0:T(8,128)(2,1)}, bf16[2,32,16,128]{3,2,1,0:T(8,128)(2,1)S(1)}, u32[]{:S(2)}, u32[]{:S(2)}) collective-permute-start(bf16[2,32,16,128]{3,2,1,0:T(8,128)(2,1)} %get-tuple-element.70), channel_id=1, source_target_pairs={{0,3},{1,2},{2,5},{3,4},{4,7},{5,6},{6,1},{7,0},{8,11},{9,10},{10,... | collective-permute-start | bytes 786440 | tf_op jit(solution)/shard_map/ppermute | solution.py:177
  28.3 0.2 collective-permute-start.10
  28.5 0.1 copy.8
  28.6 1.7 %collective-permute-start.5 = (bf16[2,32,16,128]{3,2,1,0:T(8,128)(2,1)}, bf16[2,32,16,128]{3,2,1,0:T(8,128)(2,1)S(1)}, u32[]{:S(2)}, u32[]{:S(2)}) collective-permute-start(bf16[2,32,16,128]{3,2,1,0:T(8,128)(2,1)} %get-tuple-element.66), channel_id=1, source_target_pairs={{0,4},{1,5},{2,6},{3,7},{4,0},{5,1},{6,2},{7,3},{8,12},{9,13},{10,... | collective-permute-start | bytes 786440 | tf_op jit(solution)/shard_map/ppermute | solution.py:177
  30.3 0.7 collective-permute-done.1.refs_0_
  31.0 5.9 %collective-permute-done.7.refs_5_ = bf16[2,32,16,128]{3,2,1,0:T(8,128)(2,1)S(1)} collective-permute-done((bf16[2,32,16,128]{3,2,1,0:T(8,128)(2,1)}, bf16[2,32,16,128]{3,2,1,0:T(8,128)(2,1)S(1)}, u32[]{:S(2)}, u32[]{:S(2)}) %collective-permute-start.7) | collective-permute-done | bytes 262176 | tf_op jit(solution)/shard_map/ppermute | solution.py:177
  36.9 4.1 %collective-permute-start.8 = (bf16[2,32,16,128]{3,2,1,0:T(8,128)(2,1)}, bf16[2,32,16,128]{3,2,1,0:T(8,128)(2,1)S(1)}, u32[]{:S(2)}, u32[]{:S(2)}) collective-permute-start(bf16[2,32,16,128]{3,2,1,0:T(8,128)(2,1)} %get-tuple-element.71), channel_id=1, source_target_pairs={{0,5},{1,4},{2,7},{3,6},{4,1},{5,0},{6,3},{7,2},{8,13},{9,12},{10,... | collective-permute-start | bytes 786440 | tf_op jit(solution)/shard_map/ppermute | solution.py:177
  40.9 0.1 collective-permute-start.11
  41.0 3.0 %collective-permute-start.13 = (bf16[2,32,16,128]{3,2,1,0:T(8,128)(2,1)S(1)}, bf16[2,32,16,128]{3,2,1,0:T(8,128)(2,1)S(1)}, u32[]{:S(2)}, u32[]{:S(2)}) collective-permute-start(bf16[2,32,16,128]{3,2,1,0:T(8,128)(2,1)S(1)} %copy-done.6), channel_id=1, source_target_pairs={{0,7},{1,6},{2,1},{3,0},{4,3},{5,2},{6,5},{7,4},{8,15},{9,14},{10,... | collective-permute-start | bytes 786440 | tf_op jit(solution)/shard_map/ppermute | solution.py:177
  44.1 0.9 %copy-done.2 = bf16[2,32,16,128]{3,2,1,0:T(8,128)(2,1)S(1)} copy-done((bf16[2,32,16,128]{3,2,1,0:T(8,128)(2,1)S(1)}, bf16[2,32,16,128]{3,2,1,0:T(8,128)(2,1)}, u32[]{:S(2)}) %copy-start.2) | copy-done | bytes 262168
  45.0 2.1 %grads.2 = (f32[128,128]{1,0:T(8,128)S(1)}, f32[128,128]{1,0:T(8,128)S(1)}) custom-call(bf16[2,32,16,128]{3,2,1,0:T(8,128)(2,1)S(1)} %collective-permute-done.6.refs_0_, bf16[2,32,16,128]{3,2,1,0:T(8,128)(2,1)S(1)} %collective-permute-done.9.refs_1_, bf16[2,32,16,128]{3,2,1,0:T(8,128)(2,1)S(1)} %collective-permute-done.refs_2_, ...), custom_call_target="tpu_custom_call" | custom-call | flops 671088640 | bytes 2097152 | tf_op jit(solution)/shard_map/grads/pallas_call | solution.py:102
  47.1 0.9 collective-permute-done.8.refs_3_
  48.0 5.5 %collective-permute-done.12.refs_5_ = bf16[2,32,16,128]{3,2,1,0:T(8,128)(2,1)S(1)} collective-permute-done((bf16[2,32,16,128]{3,2,1,0:T(8,128)(2,1)S(1)}, bf16[2,32,16,128]{3,2,1,0:T(8,128)(2,1)S(1)}, u32[]{:S(2)}, u32[]{:S(2)}) %collective-permute-start.12) | collective-permute-done | bytes 262176 | tf_op jit(solution)/shard_map/ppermute | solution.py:177
  53.6 0.0 collective-permute-done.13.refs_6_
  53.6 2.1 %grads.3 = (f32[128,128]{1,0:T(8,128)S(1)}, f32[128,128]{1,0:T(8,128)S(1)}) custom-call(bf16[2,32,16,128]{3,2,1,0:T(8,128)(2,1)S(1)} %collective-permute-done.1.refs_0_, bf16[2,32,16,128]{3,2,1,0:T(8,128)(2,1)S(1)} %collective-permute-done.3.refs_1_, bf16[2,32,16,128]{3,2,1,0:T(8,128)(2,1)S(1)} %collective-permute-done.5.refs_2_, ...), custom_call_target="tpu_custom_call" | custom-call | flops 671088640 | bytes 2097152 | tf_op jit(solution)/shard_map/grads/pallas_call | solution.py:102
  55.7 0.5 collective-permute-start.14
  56.1 0.9 collective-permute-done.14
  57.1 2.6 %collective-permute-start.17 = (bf16[128,128]{1,0:T(8,128)(2,1)S(1)}, bf16[128,128]{1,0:T(8,128)(2,1)S(1)}, u32[]{:S(2)}, u32[]{:S(2)}) collective-permute-start(bf16[128,128]{1,0:T(8,128)(2,1)S(1)} %add_convert_fusion.2), channel_id=1, source_target_pairs={{0,6},{1,25},{2,0},{3,27},{4,2},{5,29},{6,4},{7,31},{8,14},{9,1},{... | collective-permute-start | bytes 98312 | tf_op jit(solution)/shard_map/ppermute | solution.py:141
  59.6 1.7 %collective-permute-start.15 = (bf16[128,128]{1,0:T(8,128)(2,1)S(1)}, bf16[128,128]{1,0:T(8,128)(2,1)S(1)}, u32[]{:S(2)}, u32[]{:S(2)}) collective-permute-start(bf16[128,128]{1,0:T(8,128)(2,1)S(1)} %add_convert_fusion.2), channel_id=1, source_target_pairs={{0,4},{1,17},{2,6},{3,19},{4,0},{5,21},{6,2},{7,23},{8,12},{9,25},... | collective-permute-start | bytes 98312 | tf_op jit(solution)/shard_map/ppermute | solution.py:141
  61.4 2.3 %collective-permute-done.16 = bf16[128,128]{1,0:T(8,128)(2,1)S(1)} collective-permute-done((bf16[128,128]{1,0:T(8,128)(2,1)S(1)}, bf16[128,128]{1,0:T(8,128)(2,1)S(1)}, u32[]{:S(2)}, u32[]{:S(2)}) %collective-permute-start.16) | collective-permute-done | bytes 32800 | tf_op jit(solution)/shard_map/ppermute | solution.py:141
  63.6 0.3 collective-permute-done.15
  64.0 2.7 %collective-permute-start.20 = (bf16[128,128]{1,0:T(8,128)(2,1)S(1)}, bf16[128,128]{1,0:T(8,128)(2,1)S(1)}, u32[]{:S(2)}, u32[]{:S(2)}) collective-permute-start(bf16[128,128]{1,0:T(8,128)(2,1)S(1)} %add_convert_fusion.1), channel_id=1, source_target_pairs={{0,24},{1,7},{2,26},{3,1},{4,28},{5,3},{6,30},{7,5},{8,0},{9,15},{... | collective-permute-start | bytes 98312 | tf_op jit(solution)/shard_map/ppermute | solution.py:141
  66.7 1.7 %collective-permute-start.18 = (bf16[128,128]{1,0:T(8,128)(2,1)S(1)}, bf16[128,128]{1,0:T(8,128)(2,1)S(1)}, u32[]{:S(2)}, u32[]{:S(2)}) collective-permute-start(bf16[128,128]{1,0:T(8,128)(2,1)S(1)} %add_convert_fusion.1), channel_id=1, source_target_pairs={{0,16},{1,5},{2,18},{3,7},{4,20},{5,1},{6,22},{7,3},{8,24},{9,13},... | collective-permute-start | bytes 98312 | tf_op jit(solution)/shard_map/ppermute | solution.py:141
  68.4 2.3 %collective-permute-done.19 = bf16[128,128]{1,0:T(8,128)(2,1)S(1)} collective-permute-done((bf16[128,128]{1,0:T(8,128)(2,1)S(1)}, bf16[128,128]{1,0:T(8,128)(2,1)S(1)}, u32[]{:S(2)}, u32[]{:S(2)}) %collective-permute-start.19) | collective-permute-done | bytes 32800 | tf_op jit(solution)/shard_map/ppermute | solution.py:141
  70.7 0.3 collective-permute-done.18
  71.0 4.4 %collective-permute-start.23 = (bf16[128,128]{1,0:T(8,128)(2,1)S(1)}, bf16[128,128]{1,0:T(8,128)(2,1)S(1)}, u32[]{:S(2)}, u32[]{:S(2)}) collective-permute-start(bf16[128,128]{1,0:T(8,128)(2,1)S(1)} %add_convert_fusion), channel_id=1, source_target_pairs={{0,96},{1,97},{2,98},{3,99},{4,100},{5,101},{6,102},{7,103},{8,104... | collective-permute-start | bytes 98312 | tf_op jit(solution)/shard_map/ppermute | solution.py:141
  75.5 0.4 collective-permute-start.21
  75.8 0.7 collective-permute-done.23
  76.5 3.6 %collective-permute-done.22 = bf16[128,128]{1,0:T(8,128)(2,1)S(1)} collective-permute-done((bf16[128,128]{1,0:T(8,128)(2,1)S(1)}, bf16[128,128]{1,0:T(8,128)(2,1)S(1)}, u32[]{:S(2)}, u32[]{:S(2)}) %collective-permute-start.22) | collective-permute-done | bytes 32800 | tf_op jit(solution)/shard_map/ppermute | solution.py:141
  80.2 2.2 %collective-permute-start.24 = (f32[128,128]{1,0:T(8,128)S(1)}, f32[128,128]{1,0:T(8,128)S(1)}, u32[]{:S(2)}, u32[]{:S(2)}) collective-permute-start(f32[128,128]{1,0:T(8,128)S(1)} %add_add_fusion), channel_id=1, source_target_pairs={{0,192},{1,193},{2,194},{3,195},{4,196},{5,197},{6,198},{7,199},{8... | collective-permute-start | bytes 196616 | tf_op jit(solution)/shard_map/ppermute | solution.py:155
  82.4 3.2 %collective-permute-done.24 = f32[128,128]{1,0:T(8,128)S(1)} collective-permute-done((f32[128,128]{1,0:T(8,128)S(1)}, f32[128,128]{1,0:T(8,128)S(1)}, u32[]{:S(2)}, u32[]{:S(2)}) %collective-permute-start.24) | collective-permute-done | bytes 65568 | tf_op jit(solution)/shard_map/ppermute | solution.py:155
  85.6 5.7 %collective-permute-start.25 = (f32[128,128]{1,0:T(8,128)S(1)}, f32[128,128]{1,0:T(8,128)S(1)}, u32[]{:S(2)}, u32[]{:S(2)}) collective-permute-start(f32[128,128]{1,0:T(8,128)S(1)} %add.50), channel_id=1, source_target_pairs={{0,1},{1,0},{2,3},{3,2},{4,5},{5,4},{6,7},{7,6},{8,9},{9,8},{10,11... | collective-permute-start | bytes 196616 | tf_op jit(solution)/shard_map/ppermute | solution.py:156
  91.3 0.9 collective-permute-done.25
  92.2 0.7 broadcast_select_fusion
  (35 shorter events, 0.2 us)
Async XLA Ops:
  3.2 14.6 %collective-permute-start = (bf16[2,32,16,128]{3,2,1,0:T(8,128)(2,1)}, bf16[2,32,16,128]{3,2,1,0:T(8,128)(2,1)S(1)}, u32[]{:S(2)}, u32[]{:S(2)}) collective-permute-start(bf16[2,32,16,128]{3,2,1,0:T(8,128)(2,1)} %get-tuple-element.56), channel_id=1, source_target_pairs={{0,4},{1,5},{2,6},{3,7},{4,0},{5,1},{6,2},{7,3},{8,12},{9,13},{10,... | collective-permute-start | bytes 786440 | tf_op jit(solution)/shard_map/ppermute | solution.py:177
  7.0 14.5 %collective-permute-start.2 = (bf16[2,32,16,128]{3,2,1,0:T(8,128)(2,1)}, bf16[2,32,16,128]{3,2,1,0:T(8,128)(2,1)S(1)}, u32[]{:S(2)}, u32[]{:S(2)}) collective-permute-start(bf16[2,32,16,128]{3,2,1,0:T(8,128)(2,1)} %get-tuple-element.61), channel_id=1, source_target_pairs={{0,5},{1,4},{2,7},{3,6},{4,1},{5,0},{6,3},{7,2},{8,13},{9,12},{10,... | collective-permute-start | bytes 786440 | tf_op jit(solution)/shard_map/ppermute | solution.py:177
  9.7 15.9 %collective-permute-start.6 = (bf16[2,32,16,128]{3,2,1,0:T(8,128)(2,1)}, bf16[2,32,16,128]{3,2,1,0:T(8,128)(2,1)S(1)}, u32[]{:S(2)}, u32[]{:S(2)}) collective-permute-start(bf16[2,32,16,128]{3,2,1,0:T(8,128)(2,1)} %get-tuple-element.69), channel_id=1, source_target_pairs={{0,2},{1,3},{2,4},{3,5},{4,6},{5,7},{6,0},{7,1},{8,10},{9,11},{10,... | collective-permute-start | bytes 786440 | tf_op jit(solution)/shard_map/ppermute | solution.py:177
  9.7 18.6 %collective-permute-start.9 = (bf16[2,32,16,128]{3,2,1,0:T(8,128)(2,1)}, bf16[2,32,16,128]{3,2,1,0:T(8,128)(2,1)S(1)}, u32[]{:S(2)}, u32[]{:S(2)}) collective-permute-start(bf16[2,32,16,128]{3,2,1,0:T(8,128)(2,1)} %get-tuple-element.74), channel_id=1, source_target_pairs={{0,6},{1,7},{2,0},{3,1},{4,2},{5,3},{6,4},{7,5},{8,14},{9,15},{10,... | collective-permute-start | bytes 786440 | tf_op jit(solution)/shard_map/ppermute | solution.py:177
  12.3 16.3 %collective-permute-start.4 = (bf16[2,32,16,128]{3,2,1,0:T(8,128)(2,1)}, bf16[2,32,16,128]{3,2,1,0:T(8,128)(2,1)S(1)}, u32[]{:S(2)}, u32[]{:S(2)}) collective-permute-start(bf16[2,32,16,128]{3,2,1,0:T(8,128)(2,1)} %get-tuple-element.65), channel_id=1, source_target_pairs={{0,1},{1,0},{2,3},{3,2},{4,5},{5,4},{6,7},{7,6},{8,9},{9,8},{10,11... | collective-permute-start | bytes 786440 | tf_op jit(solution)/shard_map/ppermute | solution.py:177
  15.4 13.1 %copy-start = (bf16[128,128]{1,0:T(8,128)(2,1)S(1)}, bf16[128,128]{1,0:T(8,128)(2,1)}, u32[]{:S(2)}) copy-start(bf16[128,128]{1,0:T(8,128)(2,1)} %refs_8_.3) | copy-start | bytes 98308
  15.4 25.6 %copy-start.7 = (bf16[2,32,16,128]{3,2,1,0:T(8,128)(2,1)S(1)}, bf16[2,32,16,128]{3,2,1,0:T(8,128)(2,1)}, u32[]{:S(2)}) copy-start(bf16[2,32,16,128]{3,2,1,0:T(8,128)(2,1)} %get-tuple-element.77) | copy-start | bytes 786436
  15.4 25.6 %copy-start.6 = (bf16[2,32,16,128]{3,2,1,0:T(8,128)(2,1)S(1)}, bf16[2,32,16,128]{3,2,1,0:T(8,128)(2,1)}, u32[]{:S(2)}) copy-start(bf16[2,32,16,128]{3,2,1,0:T(8,128)(2,1)} %get-tuple-element.78) | copy-start | bytes 786436
  15.5 28.5 %copy-start.4 = (s32[128,128]{1,0:T(8,128)S(1)}, s32[128,128]{1,0:T(8,128)}, u32[]{:S(2)}) copy-start(s32[128,128]{1,0:T(8,128)} %param.10) | copy-start | bytes 196612
  15.5 28.5 %copy-start.5 = (s32[128,128]{1,0:T(8,128)S(1)}, s32[128,128]{1,0:T(8,128)}, u32[]{:S(2)}) copy-start(s32[128,128]{1,0:T(8,128)} %param.11) | copy-start | bytes 196612
  15.5 28.6 %copy-start.3 = (bf16[128,128]{1,0:T(8,128)(2,1)S(1)}, bf16[128,128]{1,0:T(8,128)(2,1)}, u32[]{:S(2)}) copy-start(bf16[128,128]{1,0:T(8,128)(2,1)} %refs_10_.3) | copy-start | bytes 98308
  17.7 35.8 %copy-start.1 = (bf16[2,32,16,128]{3,2,1,0:T(8,128)(2,1)S(1)}, bf16[2,32,16,128]{3,2,1,0:T(8,128)(2,1)}, u32[]{:S(2)}) copy-start(bf16[2,32,16,128]{3,2,1,0:T(8,128)(2,1)} %get-tuple-element.79.refs_7_) | copy-start | bytes 786436
  17.8 13.2 %collective-permute-start.1 = (bf16[2,32,16,128]{3,2,1,0:T(8,128)(2,1)}, bf16[2,32,16,128]{3,2,1,0:T(8,128)(2,1)S(1)}, u32[]{:S(2)}, u32[]{:S(2)}) collective-permute-start(bf16[2,32,16,128]{3,2,1,0:T(8,128)(2,1)} %get-tuple-element.57), channel_id=1, source_target_pairs={{0,2},{1,3},{2,4},{3,5},{4,6},{5,7},{6,0},{7,1},{8,10},{9,11},{10,... | collective-permute-start | bytes 786440 | tf_op jit(solution)/shard_map/ppermute | solution.py:177
  21.5 9.5 %collective-permute-start.3 = (bf16[2,32,16,128]{3,2,1,0:T(8,128)(2,1)}, bf16[2,32,16,128]{3,2,1,0:T(8,128)(2,1)S(1)}, u32[]{:S(2)}, u32[]{:S(2)}) collective-permute-start(bf16[2,32,16,128]{3,2,1,0:T(8,128)(2,1)} %get-tuple-element.62), channel_id=1, source_target_pairs={{0,6},{1,7},{2,0},{3,1},{4,2},{5,3},{6,4},{7,5},{8,14},{9,15},{10,... | collective-permute-start | bytes 786440 | tf_op jit(solution)/shard_map/ppermute | solution.py:177
  25.5 11.3 %collective-permute-start.7 = (bf16[2,32,16,128]{3,2,1,0:T(8,128)(2,1)}, bf16[2,32,16,128]{3,2,1,0:T(8,128)(2,1)S(1)}, u32[]{:S(2)}, u32[]{:S(2)}) collective-permute-start(bf16[2,32,16,128]{3,2,1,0:T(8,128)(2,1)} %get-tuple-element.70), channel_id=1, source_target_pairs={{0,3},{1,2},{2,5},{3,4},{4,7},{5,6},{6,1},{7,0},{8,11},{9,10},{10,... | collective-permute-start | bytes 786440 | tf_op jit(solution)/shard_map/ppermute | solution.py:177
  28.3 12.7 %collective-permute-start.10 = (bf16[2,32,16,128]{3,2,1,0:T(8,128)(2,1)}, bf16[2,32,16,128]{3,2,1,0:T(8,128)(2,1)S(1)}, u32[]{:S(2)}, u32[]{:S(2)}) collective-permute-start(bf16[2,32,16,128]{3,2,1,0:T(8,128)(2,1)} %get-tuple-element.75), channel_id=1, source_target_pairs={{0,7},{1,6},{2,1},{3,0},{4,3},{5,2},{6,5},{7,4},{8,15},{9,14},{10,... | collective-permute-start | bytes 786440 | tf_op jit(solution)/shard_map/ppermute | solution.py:177
  28.6 18.5 %collective-permute-start.5 = (bf16[2,32,16,128]{3,2,1,0:T(8,128)(2,1)}, bf16[2,32,16,128]{3,2,1,0:T(8,128)(2,1)S(1)}, u32[]{:S(2)}, u32[]{:S(2)}) collective-permute-start(bf16[2,32,16,128]{3,2,1,0:T(8,128)(2,1)} %get-tuple-element.66), channel_id=1, source_target_pairs={{0,4},{1,5},{2,6},{3,7},{4,0},{5,1},{6,2},{7,3},{8,12},{9,13},{10,... | collective-permute-start | bytes 786440 | tf_op jit(solution)/shard_map/ppermute | solution.py:177
  36.9 11.2 %collective-permute-start.8 = (bf16[2,32,16,128]{3,2,1,0:T(8,128)(2,1)}, bf16[2,32,16,128]{3,2,1,0:T(8,128)(2,1)S(1)}, u32[]{:S(2)}, u32[]{:S(2)}) collective-permute-start(bf16[2,32,16,128]{3,2,1,0:T(8,128)(2,1)} %get-tuple-element.71), channel_id=1, source_target_pairs={{0,5},{1,4},{2,7},{3,6},{4,1},{5,0},{6,3},{7,2},{8,13},{9,12},{10,... | collective-permute-start | bytes 786440 | tf_op jit(solution)/shard_map/ppermute | solution.py:177
  40.9 7.1 %collective-permute-start.11 = (bf16[2,32,16,128]{3,2,1,0:T(8,128)(2,1)}, bf16[2,32,16,128]{3,2,1,0:T(8,128)(2,1)S(1)}, u32[]{:S(2)}, u32[]{:S(2)}) collective-permute-start(bf16[2,32,16,128]{3,2,1,0:T(8,128)(2,1)} %get-tuple-element.76), channel_id=1, source_target_pairs={{0,1},{1,0},{2,3},{3,2},{4,5},{5,4},{6,7},{7,6},{8,9},{9,8},{10,11... | collective-permute-start | bytes 786440 | tf_op jit(solution)/shard_map/ppermute | solution.py:177
  41.0 12.5 %collective-permute-start.12 = (bf16[2,32,16,128]{3,2,1,0:T(8,128)(2,1)S(1)}, bf16[2,32,16,128]{3,2,1,0:T(8,128)(2,1)S(1)}, u32[]{:S(2)}, u32[]{:S(2)}) collective-permute-start(bf16[2,32,16,128]{3,2,1,0:T(8,128)(2,1)S(1)} %copy-done.7), channel_id=1, source_target_pairs={{0,3},{1,2},{2,5},{3,4},{4,7},{5,6},{6,1},{7,0},{8,11},{9,10},{10,... | collective-permute-start | bytes 786440 | tf_op jit(solution)/shard_map/ppermute | solution.py:177
  41.0 12.5 %collective-permute-start.13 = (bf16[2,32,16,128]{3,2,1,0:T(8,128)(2,1)S(1)}, bf16[2,32,16,128]{3,2,1,0:T(8,128)(2,1)S(1)}, u32[]{:S(2)}, u32[]{:S(2)}) collective-permute-start(bf16[2,32,16,128]{3,2,1,0:T(8,128)(2,1)S(1)} %copy-done.6), channel_id=1, source_target_pairs={{0,7},{1,6},{2,1},{3,0},{4,3},{5,2},{6,5},{7,4},{8,15},{9,14},{10,... | collective-permute-start | bytes 786440 | tf_op jit(solution)/shard_map/ppermute | solution.py:177
  44.1 1.0 %copy-start.2 = (bf16[2,32,16,128]{3,2,1,0:T(8,128)(2,1)S(1)}, bf16[2,32,16,128]{3,2,1,0:T(8,128)(2,1)}, u32[]{:S(2)}) copy-start(bf16[2,32,16,128]{3,2,1,0:T(8,128)(2,1)} %get-tuple-element.87.refs_7_) | copy-start | bytes 786436
  55.7 1.4 %collective-permute-start.14 = (f32[128,128]{1,0:T(8,128)S(1)}, f32[128,128]{1,0:T(8,128)S(1)}, u32[]{:S(2)}, u32[]{:S(2)}) collective-permute-start(f32[128,128]{1,0:T(8,128)S(1)} %broadcast_select_fusion.2), channel_id=1, source_target_pairs={{0,1},{1,0},{2,3},{3,2},{4,5},{5,4},{6,7},{7,6},{8,9},{9,8},{10,11... | collective-permute-start | bytes 196616 | tf_op jit(solution)/shard_map/ppermute | solution.py:151
  57.1 4.3 %collective-permute-start.17 = (bf16[128,128]{1,0:T(8,128)(2,1)S(1)}, bf16[128,128]{1,0:T(8,128)(2,1)S(1)}, u32[]{:S(2)}, u32[]{:S(2)}) collective-permute-start(bf16[128,128]{1,0:T(8,128)(2,1)S(1)} %add_convert_fusion.2), channel_id=1, source_target_pairs={{0,6},{1,25},{2,0},{3,27},{4,2},{5,29},{6,4},{7,31},{8,14},{9,1},{... | collective-permute-start | bytes 98312 | tf_op jit(solution)/shard_map/ppermute | solution.py:141
  59.6 4.0 %collective-permute-start.16 = (bf16[128,128]{1,0:T(8,128)(2,1)S(1)}, bf16[128,128]{1,0:T(8,128)(2,1)S(1)}, u32[]{:S(2)}, u32[]{:S(2)}) collective-permute-start(bf16[128,128]{1,0:T(8,128)(2,1)S(1)} %add_convert_fusion.2), channel_id=1, source_target_pairs={{0,2},{1,9},{2,4},{3,11},{4,6},{5,13},{6,0},{7,15},{8,10},{9,17},{... | collective-permute-start | bytes 98312 | tf_op jit(solution)/shard_map/ppermute | solution.py:141
  59.6 4.3 %collective-permute-start.15 = (bf16[128,128]{1,0:T(8,128)(2,1)S(1)}, bf16[128,128]{1,0:T(8,128)(2,1)S(1)}, u32[]{:S(2)}, u32[]{:S(2)}) collective-permute-start(bf16[128,128]{1,0:T(8,128)(2,1)S(1)} %add_convert_fusion.2), channel_id=1, source_target_pairs={{0,4},{1,17},{2,6},{3,19},{4,0},{5,21},{6,2},{7,23},{8,12},{9,25},... | collective-permute-start | bytes 98312 | tf_op jit(solution)/shard_map/ppermute | solution.py:141
  64.0 4.4 %collective-permute-start.20 = (bf16[128,128]{1,0:T(8,128)(2,1)S(1)}, bf16[128,128]{1,0:T(8,128)(2,1)S(1)}, u32[]{:S(2)}, u32[]{:S(2)}) collective-permute-start(bf16[128,128]{1,0:T(8,128)(2,1)S(1)} %add_convert_fusion.1), channel_id=1, source_target_pairs={{0,24},{1,7},{2,26},{3,1},{4,28},{5,3},{6,30},{7,5},{8,0},{9,15},{... | collective-permute-start | bytes 98312 | tf_op jit(solution)/shard_map/ppermute | solution.py:141
  66.7 4.0 %collective-permute-start.19 = (bf16[128,128]{1,0:T(8,128)(2,1)S(1)}, bf16[128,128]{1,0:T(8,128)(2,1)S(1)}, u32[]{:S(2)}, u32[]{:S(2)}) collective-permute-start(bf16[128,128]{1,0:T(8,128)(2,1)S(1)} %add_convert_fusion.1), channel_id=1, source_target_pairs={{0,8},{1,3},{2,10},{3,5},{4,12},{5,7},{6,14},{7,1},{8,16},{9,11},{... | collective-permute-start | bytes 98312 | tf_op jit(solution)/shard_map/ppermute | solution.py:141
  66.7 4.3 %collective-permute-start.18 = (bf16[128,128]{1,0:T(8,128)(2,1)S(1)}, bf16[128,128]{1,0:T(8,128)(2,1)S(1)}, u32[]{:S(2)}, u32[]{:S(2)}) collective-permute-start(bf16[128,128]{1,0:T(8,128)(2,1)S(1)} %add_convert_fusion.1), channel_id=1, source_target_pairs={{0,16},{1,5},{2,18},{3,7},{4,20},{5,1},{6,22},{7,3},{8,24},{9,13},... | collective-permute-start | bytes 98312 | tf_op jit(solution)/shard_map/ppermute | solution.py:141
  71.0 5.4 %collective-permute-start.23 = (bf16[128,128]{1,0:T(8,128)(2,1)S(1)}, bf16[128,128]{1,0:T(8,128)(2,1)S(1)}, u32[]{:S(2)}, u32[]{:S(2)}) collective-permute-start(bf16[128,128]{1,0:T(8,128)(2,1)S(1)} %add_convert_fusion), channel_id=1, source_target_pairs={{0,96},{1,97},{2,98},{3,99},{4,100},{5,101},{6,102},{7,103},{8,104... | collective-permute-start | bytes 98312 | tf_op jit(solution)/shard_map/ppermute | solution.py:141
  75.5 4.7 %collective-permute-start.22 = (bf16[128,128]{1,0:T(8,128)(2,1)S(1)}, bf16[128,128]{1,0:T(8,128)(2,1)S(1)}, u32[]{:S(2)}, u32[]{:S(2)}) collective-permute-start(bf16[128,128]{1,0:T(8,128)(2,1)S(1)} %add_convert_fusion), channel_id=1, source_target_pairs={{0,32},{1,33},{2,34},{3,35},{4,36},{5,37},{6,38},{7,39},{8,40},{9,... | collective-permute-start | bytes 98312 | tf_op jit(solution)/shard_map/ppermute | solution.py:141
  75.5 4.7 %collective-permute-start.21 = (bf16[128,128]{1,0:T(8,128)(2,1)S(1)}, bf16[128,128]{1,0:T(8,128)(2,1)S(1)}, u32[]{:S(2)}, u32[]{:S(2)}) collective-permute-start(bf16[128,128]{1,0:T(8,128)(2,1)S(1)} %add_convert_fusion), channel_id=1, source_target_pairs={{0,64},{1,65},{2,66},{3,67},{4,68},{5,69},{6,70},{7,71},{8,72},{9,... | collective-permute-start | bytes 98312 | tf_op jit(solution)/shard_map/ppermute | solution.py:141
  80.2 5.4 %collective-permute-start.24 = (f32[128,128]{1,0:T(8,128)S(1)}, f32[128,128]{1,0:T(8,128)S(1)}, u32[]{:S(2)}, u32[]{:S(2)}) collective-permute-start(f32[128,128]{1,0:T(8,128)S(1)} %add_add_fusion), channel_id=1, source_target_pairs={{0,192},{1,193},{2,194},{3,195},{4,196},{5,197},{6,198},{7,199},{8... | collective-permute-start | bytes 196616 | tf_op jit(solution)/shard_map/ppermute | solution.py:155
  85.6 6.6 %collective-permute-start.25 = (f32[128,128]{1,0:T(8,128)S(1)}, f32[128,128]{1,0:T(8,128)S(1)}, u32[]{:S(2)}, u32[]{:S(2)}) collective-permute-start(f32[128,128]{1,0:T(8,128)S(1)} %add.50), channel_id=1, source_target_pairs={{0,1},{1,0},{2,3},{3,2},{4,5},{5,4},{6,7},{7,6},{8,9},{9,8},{10,11... | collective-permute-start | bytes 196616 | tf_op jit(solution)/shard_map/ppermute | solution.py:156

commit v6 on v5

--- a/solution.py
+++ b/solution.py
@@ -149,10 +149,11 @@
     give = jnp.where(first, grad_right, grad_left)
     swap = tensor_shift(0, 1)
     x = keep + lax.ppermute(give, "tensor", swap)
+    x = add_four(x, "zz")
     x = add_four(x, "yx")
     x = add_four(x, "xy")
-    x = add_four(x, "zz")
-    x = x + lax.ppermute(x, ALL, route("hh", 1))
+    x = x.astype(BF16)
+    x = x.astype(F32) + lax.ppermute(x, ALL, route("hh", 1)).astype(F32)
     other = lax.ppermute(x, "tensor", swap)
     return jnp.where(first, x, other), jnp.where(first, other, x)
 

time: 93.1 us -> 92.7 us (level)
  no operation moved by 1% of the time
where the time goes in v6:
time: 92.7 us; the launch traced here: 92.5 us
  starting transfers between devices  45.3 us (49%)
  waiting for transfers between devices  32.4 us (35%)
  Pallas kernels  12.1 us (13%)
  local copies, waits for them, and re-layouts  1.1 us (1%)
    ppermute x14, starting transfers between devices, exchange(): block = lax.ppermute(block, 'tensor', tensor_shift(dy, dc))  22.8 us
    ppermute x14, waiting for transfers between devices, exchange(): block = lax.ppermute(block, 'tensor', tensor_shift(dy, dc))  18.8 us
    ppermute x9, starting transfers between devices, add_four(): lax.ppermute(x, ALL, route(axes, s))  13.5 us
    ppermute x9, waiting for transfers between devices, add_four(): lax.ppermute(x, ALL, route(axes, s))  9.44 us
    pallas_call x3, Pallas kernels, pack(): pl.pallas_call(functools.partial(pack_kernel, first, hops), in_specs=[pl....  7.88 us
    ppermute x1, starting transfers between devices, sum_all(): other = lax.ppermute(x, 'tensor', swap)  5.9 us
    pallas_call x2, Pallas kernels, local_grads(): pl.pallas_call(functools.partial(grads_kernel, hops), in_specs=[pl.BlockS...  4.18 us
    ppermute x1, starting transfers between devices, sum_all(): x = x.astype(F32) + lax.ppermute(x, ALL, route('hh', 1)).astype(F32)  2.67 us
  transfers between devices with their start and end apart: 26, of which 15 were waited for; matrix products, arithmetic and copies ran while one was open for 0% of the time, Pallas kernels for 8%

profile of v6, /device:TPU:1, one launch (start us, length us, event | category | flops | bytes accessed | tf_op | source)
XLA Modules:
  0.0 92.5 jit_solution(7716466166816526550)
XLA Ops:
  0.6 2.6 %pack.3 = (bf16[2,32,16,128]{3,2,1,0:T(8,128)(2,1)}, bf16[2,32,16,128]{3,2,1,0:T(8,128)(2,1)}, bf16[2,32,16,128]{3,2,1,0:T(8,128)(2,1)}, bf16[2,32,16,128]{3,2,1,0:T(8,128)(2,1)}, bf16[2,32,16,128]{3,2,1,0:T(8,128)(2,1)}) custom-call(bf16[8,64,16,128]{3,2,1,0:T(8,128)(2,1)} %bitcast.5, bf16[8,64,16,128]{3,2,1,0:T(8,128)(2,1)} %bitcast.8), custom_call_target="tpu_custom_call" | custom-call | bytes 2621440 | tf_op jit(solution)/shard_map/pack/pallas_call | solution.py:55
  3.2 3.8 %collective-permute-start = (bf16[2,32,16,128]{3,2,1,0:T(8,128)(2,1)}, bf16[2,32,16,128]{3,2,1,0:T(8,128)(2,1)S(1)}, u32[]{:S(2)}, u32[]{:S(2)}) collective-permute-start(bf16[2,32,16,128]{3,2,1,0:T(8,128)(2,1)} %get-tuple-element.56), channel_id=1, source_target_pairs={{0,4},{1,5},{2,6},{3,7},{4,0},{5,1},{6,2},{7,3},{8,12},{9,13},{10,... | collective-permute-start | bytes 786440 | tf_op jit(solution)/shard_map/ppermute | solution.py:178
  7.0 2.6 %collective-permute-start.2 = (bf16[2,32,16,128]{3,2,1,0:T(8,128)(2,1)}, bf16[2,32,16,128]{3,2,1,0:T(8,128)(2,1)S(1)}, u32[]{:S(2)}, u32[]{:S(2)}) collective-permute-start(bf16[2,32,16,128]{3,2,1,0:T(8,128)(2,1)} %get-tuple-element.61), channel_id=1, source_target_pairs={{0,5},{1,4},{2,7},{3,6},{4,1},{5,0},{6,3},{7,2},{8,13},{9,12},{10,... | collective-permute-start | bytes 786440 | tf_op jit(solution)/shard_map/ppermute | solution.py:178
  9.7 2.7 %collective-permute-start.9 = (bf16[2,32,16,128]{3,2,1,0:T(8,128)(2,1)}, bf16[2,32,16,128]{3,2,1,0:T(8,128)(2,1)S(1)}, u32[]{:S(2)}, u32[]{:S(2)}) collective-permute-start(bf16[2,32,16,128]{3,2,1,0:T(8,128)(2,1)} %get-tuple-element.74), channel_id=1, source_target_pairs={{0,6},{1,7},{2,0},{3,1},{4,2},{5,3},{6,4},{7,5},{8,14},{9,15},{10,... | collective-permute-start | bytes 786440 | tf_op jit(solution)/shard_map/ppermute | solution.py:178
  12.3 3.1 %pack.4 = (bf16[2,32,16,128]{3,2,1,0:T(8,128)(2,1)}, bf16[2,32,16,128]{3,2,1,0:T(8,128)(2,1)}, bf16[2,32,16,128]{3,2,1,0:T(8,128)(2,1)}, bf16[2,32,16,128]{3,2,1...) custom-call(bf16[8,64,16,128]{3,2,1,0:T(8,128)(2,1)} %bitcast.6, ...), custom_call_target="tpu_custom_call" | custom-call | bytes 4194304 | tf_op jit(solution)/shard_map/pack/pallas_call | solution.py:55
  15.4 0.0 copy-start
  15.5 0.0 copy-start.4
  15.5 0.0 copy-start.5
  15.5 0.0 copy-start.3
  15.5 2.2 %pack.5 = (bf16[2,32,16,128]{3,2,1,0:T(8,128)(2,1)}, bf16[2,32,16,128]{3,2,1,0:T(8,128)(2,1)}, bf16[2,32,16,128]{3,2,1,0:T(8,128)(2,1)}) custom-call(bf16[8,64,16,128]{3,2,1,0:T(8,128)(2,1)} %bitcast.7, bf16[8,64,16,128]{3,2,1,0:T(8,128)(2,1)} %bitcast.10), custom_call_target="tpu_custom_call" | custom-call | bytes 1572864 | tf_op jit(solution)/shard_map/pack/pallas_call | solution.py:55
  17.8 0.1 collective-permute-start.1
  17.9 3.7 %collective-permute-done.2.refs_3_ = bf16[2,32,16,128]{3,2,1,0:T(8,128)(2,1)S(1)} collective-permute-done((bf16[2,32,16,128]{3,2,1,0:T(8,128)(2,1)}, bf16[2,32,16,128]{3,2,1,0:T(8,128)(2,1)S(1)}, u32[]{:S(2)}, u32[]{:S(2)}) %collective-permute-start.2) | collective-permute-done | bytes 262176 | tf_op jit(solution)/shard_map/ppermute | solution.py:178
  21.5 1.9 %collective-permute-start.3 = (bf16[2,32,16,128]{3,2,1,0:T(8,128)(2,1)}, bf16[2,32,16,128]{3,2,1,0:T(8,128)(2,1)S(1)}, u32[]{:S(2)}, u32[]{:S(2)}) collective-permute-start(bf16[2,32,16,128]{3,2,1,0:T(8,128)(2,1)} %get-tuple-element.62), channel_id=1, source_target_pairs={{0,6},{1,7},{2,0},{3,1},{4,2},{5,3},{6,4},{7,5},{8,14},{9,15},{10,... | collective-permute-start | bytes 786440 | tf_op jit(solution)/shard_map/ppermute | solution.py:178
  23.4 2.1 %collective-permute-done.6.refs_0_ = bf16[2,32,16,128]{3,2,1,0:T(8,128)(2,1)S(1)} collective-permute-done((bf16[2,32,16,128]{3,2,1,0:T(8,128)(2,1)}, bf16[2,32,16,128]{3,2,1,0:T(8,128)(2,1)S(1)}, u32[]{:S(2)}, u32[]{:S(2)}) %collective-permute-start.6) | collective-permute-done | bytes 262176 | tf_op jit(solution)/shard_map/ppermute | solution.py:178
  25.5 2.7 %collective-permute-start.7 = (bf16[2,32,16,128]{3,2,1,0:T(8,128)(2,1)}, bf16[2,32,16,128]{3,2,1,0:T(8,128)(2,1)S(1)}, u32[]{:S(2)}, u32[]{:S(2)}) collective-permute-start(bf16[2,32,16,128]{3,2,1,0:T(8,128)(2,1)} %get-tuple-element.70), channel_id=1, source_target_pairs={{0,3},{1,2},{2,5},{3,4},{4,7},{5,6},{6,1},{7,0},{8,11},{9,10},{10,... | collective-permute-start | bytes 786440 | tf_op jit(solution)/shard_map/ppermute | solution.py:178
  28.3 0.2 collective-permute-start.10
  28.5 0.1 copy.8
  28.6 1.7 %collective-permute-start.5 = (bf16[2,32,16,128]{3,2,1,0:T(8,128)(2,1)}, bf16[2,32,16,128]{3,2,1,0:T(8,128)(2,1)S(1)}, u32[]{:S(2)}, u32[]{:S(2)}) collective-permute-start(bf16[2,32,16,128]{3,2,1,0:T(8,128)(2,1)} %get-tuple-element.66), channel_id=1, source_target_pairs={{0,4},{1,5},{2,6},{3,7},{4,0},{5,1},{6,2},{7,3},{8,12},{9,13},{10,... | collective-permute-start | bytes 786440 | tf_op jit(solution)/shard_map/ppermute | solution.py:178
  30.3 0.7 collective-permute-done.1.refs_0_
  31.0 5.9 %collective-permute-done.7.refs_5_ = bf16[2,32,16,128]{3,2,1,0:T(8,128)(2,1)S(1)} collective-permute-done((bf16[2,32,16,128]{3,2,1,0:T(8,128)(2,1)}, bf16[2,32,16,128]{3,2,1,0:T(8,128)(2,1)S(1)}, u32[]{:S(2)}, u32[]{:S(2)}) %collective-permute-start.7) | collective-permute-done | bytes 262176 | tf_op jit(solution)/shard_map/ppermute | solution.py:178
  36.9 4.1 %collective-permute-start.8 = (bf16[2,32,16,128]{3,2,1,0:T(8,128)(2,1)}, bf16[2,32,16,128]{3,2,1,0:T(8,128)(2,1)S(1)}, u32[]{:S(2)}, u32[]{:S(2)}) collective-permute-start(bf16[2,32,16,128]{3,2,1,0:T(8,128)(2,1)} %get-tuple-element.71), channel_id=1, source_target_pairs={{0,5},{1,4},{2,7},{3,6},{4,1},{5,0},{6,3},{7,2},{8,13},{9,12},{10,... | collective-permute-start | bytes 786440 | tf_op jit(solution)/shard_map/ppermute | solution.py:178
  40.9 0.1 collective-permute-start.11
  41.0 3.0 %collective-permute-start.13 = (bf16[2,32,16,128]{3,2,1,0:T(8,128)(2,1)S(1)}, bf16[2,32,16,128]{3,2,1,0:T(8,128)(2,1)S(1)}, u32[]{:S(2)}, u32[]{:S(2)}) collective-permute-start(bf16[2,32,16,128]{3,2,1,0:T(8,128)(2,1)S(1)} %copy-done.6), channel_id=1, source_target_pairs={{0,7},{1,6},{2,1},{3,0},{4,3},{5,2},{6,5},{7,4},{8,15},{9,14},{10,... | collective-permute-start | bytes 786440 | tf_op jit(solution)/shard_map/ppermute | solution.py:178
  44.1 0.9 %copy-done.2 = bf16[2,32,16,128]{3,2,1,0:T(8,128)(2,1)S(1)} copy-done((bf16[2,32,16,128]{3,2,1,0:T(8,128)(2,1)S(1)}, bf16[2,32,16,128]{3,2,1,0:T(8,128)(2,1)}, u32[]{:S(2)}) %copy-start.2) | copy-done | bytes 262168
  45.0 2.1 %grads.2 = (f32[128,128]{1,0:T(8,128)S(1)}, f32[128,128]{1,0:T(8,128)S(1)}) custom-call(bf16[2,32,16,128]{3,2,1,0:T(8,128)(2,1)S(1)} %collective-permute-done.6.refs_0_, bf16[2,32,16,128]{3,2,1,0:T(8,128)(2,1)S(1)} %collective-permute-done.9.refs_1_, bf16[2,32,16,128]{3,2,1,0:T(8,128)(2,1)S(1)} %collective-permute-done.refs_2_, ...), custom_call_target="tpu_custom_call" | custom-call | flops 671088640 | bytes 2097152 | tf_op jit(solution)/shard_map/grads/pallas_call | solution.py:102
  47.1 0.9 collective-permute-done.8.refs_3_
  48.0 5.5 %collective-permute-done.12.refs_5_ = bf16[2,32,16,128]{3,2,1,0:T(8,128)(2,1)S(1)} collective-permute-done((bf16[2,32,16,128]{3,2,1,0:T(8,128)(2,1)S(1)}, bf16[2,32,16,128]{3,2,1,0:T(8,128)(2,1)S(1)}, u32[]{:S(2)}, u32[]{:S(2)}) %collective-permute-start.12) | collective-permute-done | bytes 262176 | tf_op jit(solution)/shard_map/ppermute | solution.py:178
  53.6 0.0 collective-permute-done.13.refs_6_
  53.6 2.1 %grads.3 = (f32[128,128]{1,0:T(8,128)S(1)}, f32[128,128]{1,0:T(8,128)S(1)}) custom-call(bf16[2,32,16,128]{3,2,1,0:T(8,128)(2,1)S(1)} %collective-permute-done.1.refs_0_, bf16[2,32,16,128]{3,2,1,0:T(8,128)(2,1)S(1)} %collective-permute-done.3.refs_1_, bf16[2,32,16,128]{3,2,1,0:T(8,128)(2,1)S(1)} %collective-permute-done.5.refs_2_, ...), custom_call_target="tpu_custom_call" | custom-call | flops 671088640 | bytes 2097152 | tf_op jit(solution)/shard_map/grads/pallas_call | solution.py:102
  55.7 0.5 collective-permute-start.14
  56.1 0.9 collective-permute-done.14
  57.1 4.4 %collective-permute-start.17 = (bf16[128,128]{1,0:T(8,128)(2,1)S(1)}, bf16[128,128]{1,0:T(8,128)(2,1)S(1)}, u32[]{:S(2)}, u32[]{:S(2)}) collective-permute-start(bf16[128,128]{1,0:T(8,128)(2,1)S(1)} %add_convert_fusion.3), channel_id=1, source_target_pairs={{0,96},{1,97},{2,98},{3,99},{4,100},{5,101},{6,102},{7,103},{8,104... | collective-permute-start | bytes 98312 | tf_op jit(solution)/shard_map/ppermute | solution.py:141
  61.5 0.4 collective-permute-start.15
  61.9 0.7 collective-permute-done.17
  62.5 3.5 %collective-permute-done.16 = bf16[128,128]{1,0:T(8,128)(2,1)S(1)} collective-permute-done((bf16[128,128]{1,0:T(8,128)(2,1)S(1)}, bf16[128,128]{1,0:T(8,128)(2,1)S(1)}, u32[]{:S(2)}, u32[]{:S(2)}) %collective-permute-start.16) | collective-permute-done | bytes 32800 | tf_op jit(solution)/shard_map/ppermute | solution.py:141
  66.1 2.6 %collective-permute-start.20 = (bf16[128,128]{1,0:T(8,128)(2,1)S(1)}, bf16[128,128]{1,0:T(8,128)(2,1)S(1)}, u32[]{:S(2)}, u32[]{:S(2)}) collective-permute-start(bf16[128,128]{1,0:T(8,128)(2,1)S(1)} %add_convert_fusion.2), channel_id=1, source_target_pairs={{0,6},{1,25},{2,0},{3,27},{4,2},{5,29},{6,4},{7,31},{8,14},{9,1},{... | collective-permute-start | bytes 98312 | tf_op jit(solution)/shard_map/ppermute | solution.py:141
  68.6 1.7 %collective-permute-start.18 = (bf16[128,128]{1,0:T(8,128)(2,1)S(1)}, bf16[128,128]{1,0:T(8,128)(2,1)S(1)}, u32[]{:S(2)}, u32[]{:S(2)}) collective-permute-start(bf16[128,128]{1,0:T(8,128)(2,1)S(1)} %add_convert_fusion.2), channel_id=1, source_target_pairs={{0,4},{1,17},{2,6},{3,19},{4,0},{5,21},{6,2},{7,23},{8,12},{9,25},... | collective-permute-start | bytes 98312 | tf_op jit(solution)/shard_map/ppermute | solution.py:141
  70.4 2.3 %collective-permute-done.19 = bf16[128,128]{1,0:T(8,128)(2,1)S(1)} collective-permute-done((bf16[128,128]{1,0:T(8,128)(2,1)S(1)}, bf16[128,128]{1,0:T(8,128)(2,1)S(1)}, u32[]{:S(2)}, u32[]{:S(2)}) %collective-permute-start.19) | collective-permute-done | bytes 32800 | tf_op jit(solution)/shard_map/ppermute | solution.py:141
  72.6 0.3 collective-permute-done.18
  73.0 2.7 %collective-permute-start.23 = (bf16[128,128]{1,0:T(8,128)(2,1)S(1)}, bf16[128,128]{1,0:T(8,128)(2,1)S(1)}, u32[]{:S(2)}, u32[]{:S(2)}) collective-permute-start(bf16[128,128]{1,0:T(8,128)(2,1)S(1)} %add_convert_fusion.1), channel_id=1, source_target_pairs={{0,24},{1,7},{2,26},{3,1},{4,28},{5,3},{6,30},{7,5},{8,0},{9,15},{... | collective-permute-start | bytes 98312 | tf_op jit(solution)/shard_map/ppermute | solution.py:141
  75.7 1.7 %collective-permute-start.21 = (bf16[128,128]{1,0:T(8,128)(2,1)S(1)}, bf16[128,128]{1,0:T(8,128)(2,1)S(1)}, u32[]{:S(2)}, u32[]{:S(2)}) collective-permute-start(bf16[128,128]{1,0:T(8,128)(2,1)S(1)} %add_convert_fusion.1), channel_id=1, source_target_pairs={{0,16},{1,5},{2,18},{3,7},{4,20},{5,1},{6,22},{7,3},{8,24},{9,13},... | collective-permute-start | bytes 98312 | tf_op jit(solution)/shard_map/ppermute | solution.py:141
  77.4 2.3 %collective-permute-done.22 = bf16[128,128]{1,0:T(8,128)(2,1)S(1)} collective-permute-done((bf16[128,128]{1,0:T(8,128)(2,1)S(1)}, bf16[128,128]{1,0:T(8,128)(2,1)S(1)}, u32[]{:S(2)}, u32[]{:S(2)}) %collective-permute-start.22) | collective-permute-done | bytes 32800 | tf_op jit(solution)/shard_map/ppermute | solution.py:141
  79.7 0.3 collective-permute-done.21
  80.1 2.7 %collective-permute-start.24 = (bf16[128,128]{1,0:T(8,128)(2,1)S(1)}, bf16[128,128]{1,0:T(8,128)(2,1)S(1)}, u32[]{:S(2)}, u32[]{:S(2)}) collective-permute-start(bf16[128,128]{1,0:T(8,128)(2,1)S(1)} %add_convert_fusion), channel_id=1, source_target_pairs={{0,192},{1,193},{2,194},{3,195},{4,196},{5,197},{6,198},{7,199},{8... | collective-permute-start | bytes 98312 | tf_op jit(solution)/shard_map/ppermute | solution.py:156
  82.7 2.3 %collective-permute-done.24 = bf16[128,128]{1,0:T(8,128)(2,1)S(1)} collective-permute-done((bf16[128,128]{1,0:T(8,128)(2,1)S(1)}, bf16[128,128]{1,0:T(8,128)(2,1)S(1)}, u32[]{:S(2)}, u32[]{:S(2)}) %collective-permute-start.24) | collective-permute-done | bytes 32800 | tf_op jit(solution)/shard_map/ppermute | solution.py:156
  85.0 5.9 %collective-permute-start.25 = (f32[128,128]{1,0:T(8,128)S(1)}, f32[128,128]{1,0:T(8,128)S(1)}, u32[]{:S(2)}, u32[]{:S(2)}) collective-permute-start(f32[128,128]{1,0:T(8,128)S(1)} %convert_add_fusion), channel_id=1, source_target_pairs={{0,1},{1,0},{2,3},{3,2},{4,5},{5,4},{6,7},{7,6},{8,9},{9,8},{10,11... | collective-permute-start | bytes 196616 | tf_op jit(solution)/shard_map/ppermute | solution.py:157
  90.9 0.9 collective-permute-done.25
  91.8 0.7 broadcast_select_fusion
  (35 shorter events, 0.2 us)
Async XLA Ops:
  3.2 14.6 %collective-permute-start = (bf16[2,32,16,128]{3,2,1,0:T(8,128)(2,1)}, bf16[2,32,16,128]{3,2,1,0:T(8,128)(2,1)S(1)}, u32[]{:S(2)}, u32[]{:S(2)}) collective-permute-start(bf16[2,32,16,128]{3,2,1,0:T(8,128)(2,1)} %get-tuple-element.56), channel_id=1, source_target_pairs={{0,4},{1,5},{2,6},{3,7},{4,0},{5,1},{6,2},{7,3},{8,12},{9,13},{10,... | collective-permute-start | bytes 786440 | tf_op jit(solution)/shard_map/ppermute | solution.py:178
  7.0 14.5 %collective-permute-start.2 = (bf16[2,32,16,128]{3,2,1,0:T(8,128)(2,1)}, bf16[2,32,16,128]{3,2,1,0:T(8,128)(2,1)S(1)}, u32[]{:S(2)}, u32[]{:S(2)}) collective-permute-start(bf16[2,32,16,128]{3,2,1,0:T(8,128)(2,1)} %get-tuple-element.61), channel_id=1, source_target_pairs={{0,5},{1,4},{2,7},{3,6},{4,1},{5,0},{6,3},{7,2},{8,13},{9,12},{10,... | collective-permute-start | bytes 786440 | tf_op jit(solution)/shard_map/ppermute | solution.py:178
  9.7 15.9 %collective-permute-start.6 = (bf16[2,32,16,128]{3,2,1,0:T(8,128)(2,1)}, bf16[2,32,16,128]{3,2,1,0:T(8,128)(2,1)S(1)}, u32[]{:S(2)}, u32[]{:S(2)}) collective-permute-start(bf16[2,32,16,128]{3,2,1,0:T(8,128)(2,1)} %get-tuple-element.69), channel_id=1, source_target_pairs={{0,2},{1,3},{2,4},{3,5},{4,6},{5,7},{6,0},{7,1},{8,10},{9,11},{10,... | collective-permute-start | bytes 786440 | tf_op jit(solution)/shard_map/ppermute | solution.py:178
  9.7 18.6 %collective-permute-start.9 = (bf16[2,32,16,128]{3,2,1,0:T(8,128)(2,1)}, bf16[2,32,16,128]{3,2,1,0:T(8,128)(2,1)S(1)}, u32[]{:S(2)}, u32[]{:S(2)}) collective-permute-start(bf16[2,32,16,128]{3,2,1,0:T(8,128)(2,1)} %get-tuple-element.74), channel_id=1, source_target_pairs={{0,6},{1,7},{2,0},{3,1},{4,2},{5,3},{6,4},{7,5},{8,14},{9,15},{10,... | collective-permute-start | bytes 786440 | tf_op jit(solution)/shard_map/ppermute | solution.py:178
  12.3 16.3 %collective-permute-start.4 = (bf16[2,32,16,128]{3,2,1,0:T(8,128)(2,1)}, bf16[2,32,16,128]{3,2,1,0:T(8,128)(2,1)S(1)}, u32[]{:S(2)}, u32[]{:S(2)}) collective-permute-start(bf16[2,32,16,128]{3,2,1,0:T(8,128)(2,1)} %get-tuple-element.65), channel_id=1, source_target_pairs={{0,1},{1,0},{2,3},{3,2},{4,5},{5,4},{6,7},{7,6},{8,9},{9,8},{10,11... | collective-permute-start | bytes 786440 | tf_op jit(solution)/shard_map/ppermute | solution.py:178
  15.4 13.1 %copy-start = (bf16[128,128]{1,0:T(8,128)(2,1)S(1)}, bf16[128,128]{1,0:T(8,128)(2,1)}, u32[]{:S(2)}) copy-start(bf16[128,128]{1,0:T(8,128)(2,1)} %refs_8_.3) | copy-start | bytes 98308
  15.4 25.6 %copy-start.7 = (bf16[2,32,16,128]{3,2,1,0:T(8,128)(2,1)S(1)}, bf16[2,32,16,128]{3,2,1,0:T(8,128)(2,1)}, u32[]{:S(2)}) copy-start(bf16[2,32,16,128]{3,2,1,0:T(8,128)(2,1)} %get-tuple-element.77) | copy-start | bytes 786436
  15.4 25.6 %copy-start.6 = (bf16[2,32,16,128]{3,2,1,0:T(8,128)(2,1)S(1)}, bf16[2,32,16,128]{3,2,1,0:T(8,128)(2,1)}, u32[]{:S(2)}) copy-start(bf16[2,32,16,128]{3,2,1,0:T(8,128)(2,1)} %get-tuple-element.78) | copy-start | bytes 786436
  15.5 28.5 %copy-start.4 = (s32[128,128]{1,0:T(8,128)S(1)}, s32[128,128]{1,0:T(8,128)}, u32[]{:S(2)}) copy-start(s32[128,128]{1,0:T(8,128)} %param.10) | copy-start | bytes 196612
  15.5 28.5 %copy-start.5 = (s32[128,128]{1,0:T(8,128)S(1)}, s32[128,128]{1,0:T(8,128)}, u32[]{:S(2)}) copy-start(s32[128,128]{1,0:T(8,128)} %param.11) | copy-start | bytes 196612
  15.5 28.6 %copy-start.3 = (bf16[128,128]{1,0:T(8,128)(2,1)S(1)}, bf16[128,128]{1,0:T(8,128)(2,1)}, u32[]{:S(2)}) copy-start(bf16[128,128]{1,0:T(8,128)(2,1)} %refs_10_.3) | copy-start | bytes 98308
  17.7 35.8 %copy-start.1 = (bf16[2,32,16,128]{3,2,1,0:T(8,128)(2,1)S(1)}, bf16[2,32,16,128]{3,2,1,0:T(8,128)(2,1)}, u32[]{:S(2)}) copy-start(bf16[2,32,16,128]{3,2,1,0:T(8,128)(2,1)} %get-tuple-element.79.refs_7_) | copy-start | bytes 786436
  17.8 13.2 %collective-permute-start.1 = (bf16[2,32,16,128]{3,2,1,0:T(8,128)(2,1)}, bf16[2,32,16,128]{3,2,1,0:T(8,128)(2,1)S(1)}, u32[]{:S(2)}, u32[]{:S(2)}) collective-permute-start(bf16[2,32,16,128]{3,2,1,0:T(8,128)(2,1)} %get-tuple-element.57), channel_id=1, source_target_pairs={{0,2},{1,3},{2,4},{3,5},{4,6},{5,7},{6,0},{7,1},{8,10},{9,11},{10,... | collective-permute-start | bytes 786440 | tf_op jit(solution)/shard_map/ppermute | solution.py:178
  21.5 9.5 %collective-permute-start.3 = (bf16[2,32,16,128]{3,2,1,0:T(8,128)(2,1)}, bf16[2,32,16,128]{3,2,1,0:T(8,128)(2,1)S(1)}, u32[]{:S(2)}, u32[]{:S(2)}) collective-permute-start(bf16[2,32,16,128]{3,2,1,0:T(8,128)(2,1)} %get-tuple-element.62), channel_id=1, source_target_pairs={{0,6},{1,7},{2,0},{3,1},{4,2},{5,3},{6,4},{7,5},{8,14},{9,15},{10,... | collective-permute-start | bytes 786440 | tf_op jit(solution)/shard_map/ppermute | solution.py:178
  25.5 11.3 %collective-permute-start.7 = (bf16[2,32,16,128]{3,2,1,0:T(8,128)(2,1)}, bf16[2,32,16,128]{3,2,1,0:T(8,128)(2,1)S(1)}, u32[]{:S(2)}, u32[]{:S(2)}) collective-permute-start(bf16[2,32,16,128]{3,2,1,0:T(8,128)(2,1)} %get-tuple-element.70), channel_id=1, source_target_pairs={{0,3},{1,2},{2,5},{3,4},{4,7},{5,6},{6,1},{7,0},{8,11},{9,10},{10,... | collective-permute-start | bytes 786440 | tf_op jit(solution)/shard_map/ppermute | solution.py:178
  28.3 12.7 %collective-permute-start.10 = (bf16[2,32,16,128]{3,2,1,0:T(8,128)(2,1)}, bf16[2,32,16,128]{3,2,1,0:T(8,128)(2,1)S(1)}, u32[]{:S(2)}, u32[]{:S(2)}) collective-permute-start(bf16[2,32,16,128]{3,2,1,0:T(8,128)(2,1)} %get-tuple-element.75), channel_id=1, source_target_pairs={{0,7},{1,6},{2,1},{3,0},{4,3},{5,2},{6,5},{7,4},{8,15},{9,14},{10,... | collective-permute-start | bytes 786440 | tf_op jit(solution)/shard_map/ppermute | solution.py:178
  28.6 18.5 %collective-permute-start.5 = (bf16[2,32,16,128]{3,2,1,0:T(8,128)(2,1)}, bf16[2,32,16,128]{3,2,1,0:T(8,128)(2,1)S(1)}, u32[]{:S(2)}, u32[]{:S(2)}) collective-permute-start(bf16[2,32,16,128]{3,2,1,0:T(8,128)(2,1)} %get-tuple-element.66), channel_id=1, source_target_pairs={{0,4},{1,5},{2,6},{3,7},{4,0},{5,1},{6,2},{7,3},{8,12},{9,13},{10,... | collective-permute-start | bytes 786440 | tf_op jit(solution)/shard_map/ppermute | solution.py:178
  36.9 11.2 %collective-permute-start.8 = (bf16[2,32,16,128]{3,2,1,0:T(8,128)(2,1)}, bf16[2,32,16,128]{3,2,1,0:T(8,128)(2,1)S(1)}, u32[]{:S(2)}, u32[]{:S(2)}) collective-permute-start(bf16[2,32,16,128]{3,2,1,0:T(8,128)(2,1)} %get-tuple-element.71), channel_id=1, source_target_pairs={{0,5},{1,4},{2,7},{3,6},{4,1},{5,0},{6,3},{7,2},{8,13},{9,12},{10,... | collective-permute-start | bytes 786440 | tf_op jit(solution)/shard_map/ppermute | solution.py:178
  40.9 7.1 %collective-permute-start.11 = (bf16[2,32,16,128]{3,2,1,0:T(8,128)(2,1)}, bf16[2,32,16,128]{3,2,1,0:T(8,128)(2,1)S(1)}, u32[]{:S(2)}, u32[]{:S(2)}) collective-permute-start(bf16[2,32,16,128]{3,2,1,0:T(8,128)(2,1)} %get-tuple-element.76), channel_id=1, source_target_pairs={{0,1},{1,0},{2,3},{3,2},{4,5},{5,4},{6,7},{7,6},{8,9},{9,8},{10,11... | collective-permute-start | bytes 786440 | tf_op jit(solution)/shard_map/ppermute | solution.py:178
  41.0 12.5 %collective-permute-start.12 = (bf16[2,32,16,128]{3,2,1,0:T(8,128)(2,1)S(1)}, bf16[2,32,16,128]{3,2,1,0:T(8,128)(2,1)S(1)}, u32[]{:S(2)}, u32[]{:S(2)}) collective-permute-start(bf16[2,32,16,128]{3,2,1,0:T(8,128)(2,1)S(1)} %copy-done.7), channel_id=1, source_target_pairs={{0,3},{1,2},{2,5},{3,4},{4,7},{5,6},{6,1},{7,0},{8,11},{9,10},{10,... | collective-permute-start | bytes 786440 | tf_op jit(solution)/shard_map/ppermute | solution.py:178
  41.0 12.5 %collective-permute-start.13 = (bf16[2,32,16,128]{3,2,1,0:T(8,128)(2,1)S(1)}, bf16[2,32,16,128]{3,2,1,0:T(8,128)(2,1)S(1)}, u32[]{:S(2)}, u32[]{:S(2)}) collective-permute-start(bf16[2,32,16,128]{3,2,1,0:T(8,128)(2,1)S(1)} %copy-done.6), channel_id=1, source_target_pairs={{0,7},{1,6},{2,1},{3,0},{4,3},{5,2},{6,5},{7,4},{8,15},{9,14},{10,... | collective-permute-start | bytes 786440 | tf_op jit(solution)/shard_map/ppermute | solution.py:178
  44.1 1.0 %copy-start.2 = (bf16[2,32,16,128]{3,2,1,0:T(8,128)(2,1)S(1)}, bf16[2,32,16,128]{3,2,1,0:T(8,128)(2,1)}, u32[]{:S(2)}) copy-start(bf16[2,32,16,128]{3,2,1,0:T(8,128)(2,1)} %get-tuple-element.87.refs_7_) | copy-start | bytes 786436
  55.7 1.4 %collective-permute-start.14 = (f32[128,128]{1,0:T(8,128)S(1)}, f32[128,128]{1,0:T(8,128)S(1)}, u32[]{:S(2)}, u32[]{:S(2)}) collective-permute-start(f32[128,128]{1,0:T(8,128)S(1)} %broadcast_select_fusion.2), channel_id=1, source_target_pairs={{0,1},{1,0},{2,3},{3,2},{4,5},{5,4},{6,7},{7,6},{8,9},{9,8},{10,11... | collective-permute-start | bytes 196616 | tf_op jit(solution)/shard_map/ppermute | solution.py:151
  57.1 5.4 %collective-permute-start.17 = (bf16[128,128]{1,0:T(8,128)(2,1)S(1)}, bf16[128,128]{1,0:T(8,128)(2,1)S(1)}, u32[]{:S(2)}, u32[]{:S(2)}) collective-permute-start(bf16[128,128]{1,0:T(8,128)(2,1)S(1)} %add_convert_fusion.3), channel_id=1, source_target_pairs={{0,96},{1,97},{2,98},{3,99},{4,100},{5,101},{6,102},{7,103},{8,104... | collective-permute-start | bytes 98312 | tf_op jit(solution)/shard_map/ppermute | solution.py:141
  61.5 4.6 %collective-permute-start.16 = (bf16[128,128]{1,0:T(8,128)(2,1)S(1)}, bf16[128,128]{1,0:T(8,128)(2,1)S(1)}, u32[]{:S(2)}, u32[]{:S(2)}) collective-permute-start(bf16[128,128]{1,0:T(8,128)(2,1)S(1)} %add_convert_fusion.3), channel_id=1, source_target_pairs={{0,32},{1,33},{2,34},{3,35},{4,36},{5,37},{6,38},{7,39},{8,40},{9,... | collective-permute-start | bytes 98312 | tf_op jit(solution)/shard_map/ppermute | solution.py:141
  61.5 4.6 %collective-permute-start.15 = (bf16[128,128]{1,0:T(8,128)(2,1)S(1)}, bf16[128,128]{1,0:T(8,128)(2,1)S(1)}, u32[]{:S(2)}, u32[]{:S(2)}) collective-permute-start(bf16[128,128]{1,0:T(8,128)(2,1)S(1)} %add_convert_fusion.3), channel_id=1, source_target_pairs={{0,64},{1,65},{2,66},{3,67},{4,68},{5,69},{6,70},{7,71},{8,72},{9,... | collective-permute-start | bytes 98312 | tf_op jit(solution)/shard_map/ppermute | solution.py:141
  66.1 4.3 %collective-permute-start.20 = (bf16[128,128]{1,0:T(8,128)(2,1)S(1)}, bf16[128,128]{1,0:T(8,128)(2,1)S(1)}, u32[]{:S(2)}, u32[]{:S(2)}) collective-permute-start(bf16[128,128]{1,0:T(8,128)(2,1)S(1)} %add_convert_fusion.2), channel_id=1, source_target_pairs={{0,6},{1,25},{2,0},{3,27},{4,2},{5,29},{6,4},{7,31},{8,14},{9,1},{... | collective-permute-start | bytes 98312 | tf_op jit(solution)/shard_map/ppermute | solution.py:141
  68.6 4.0 %collective-permute-start.19 = (bf16[128,128]{1,0:T(8,128)(2,1)S(1)}, bf16[128,128]{1,0:T(8,128)(2,1)S(1)}, u32[]{:S(2)}, u32[]{:S(2)}) collective-permute-start(bf16[128,128]{1,0:T(8,128)(2,1)S(1)} %add_convert_fusion.2), channel_id=1, source_target_pairs={{0,2},{1,9},{2,4},{3,11},{4,6},{5,13},{6,0},{7,15},{8,10},{9,17},{... | collective-permute-start | bytes 98312 | tf_op jit(solution)/shard_map/ppermute | solution.py:141
  68.6 4.3 %collective-permute-start.18 = (bf16[128,128]{1,0:T(8,128)(2,1)S(1)}, bf16[128,128]{1,0:T(8,128)(2,1)S(1)}, u32[]{:S(2)}, u32[]{:S(2)}) collective-permute-start(bf16[128,128]{1,0:T(8,128)(2,1)S(1)} %add_convert_fusion.2), channel_id=1, source_target_pairs={{0,4},{1,17},{2,6},{3,19},{4,0},{5,21},{6,2},{7,23},{8,12},{9,25},... | collective-permute-start | bytes 98312 | tf_op jit(solution)/shard_map/ppermute | solution.py:141
  73.0 4.4 %collective-permute-start.23 = (bf16[128,128]{1,0:T(8,128)(2,1)S(1)}, bf16[128,128]{1,0:T(8,128)(2,1)S(1)}, u32[]{:S(2)}, u32[]{:S(2)}) collective-permute-start(bf16[128,128]{1,0:T(8,128)(2,1)S(1)} %add_convert_fusion.1), channel_id=1, source_target_pairs={{0,24},{1,7},{2,26},{3,1},{4,28},{5,3},{6,30},{7,5},{8,0},{9,15},{... | collective-permute-start | bytes 98312 | tf_op jit(solution)/shard_map/ppermute | solution.py:141
  75.7 4.0 %collective-permute-start.22 = (bf16[128,128]{1,0:T(8,128)(2,1)S(1)}, bf16[128,128]{1,0:T(8,128)(2,1)S(1)}, u32[]{:S(2)}, u32[]{:S(2)}) collective-permute-start(bf16[128,128]{1,0:T(8,128)(2,1)S(1)} %add_convert_fusion.1), channel_id=1, source_target_pairs={{0,8},{1,3},{2,10},{3,5},{4,12},{5,7},{6,14},{7,1},{8,16},{9,11},{... | collective-permute-start | bytes 98312 | tf_op jit(solution)/shard_map/ppermute | solution.py:141
  75.7 4.3 %collective-permute-start.21 = (bf16[128,128]{1,0:T(8,128)(2,1)S(1)}, bf16[128,128]{1,0:T(8,128)(2,1)S(1)}, u32[]{:S(2)}, u32[]{:S(2)}) collective-permute-start(bf16[128,128]{1,0:T(8,128)(2,1)S(1)} %add_convert_fusion.1), channel_id=1, source_target_pairs={{0,16},{1,5},{2,18},{3,7},{4,20},{5,1},{6,22},{7,3},{8,24},{9,13},... | collective-permute-start | bytes 98312 | tf_op jit(solution)/shard_map/ppermute | solution.py:141
  80.1 5.0 %collective-permute-start.24 = (bf16[128,128]{1,0:T(8,128)(2,1)S(1)}, bf16[128,128]{1,0:T(8,128)(2,1)S(1)}, u32[]{:S(2)}, u32[]{:S(2)}) collective-permute-start(bf16[128,128]{1,0:T(8,128)(2,1)S(1)} %add_convert_fusion), channel_id=1, source_target_pairs={{0,192},{1,193},{2,194},{3,195},{4,196},{5,197},{6,198},{7,199},{8... | collective-permute-start | bytes 98312 | tf_op jit(solution)/shard_map/ppermute | solution.py:156
  85.0 6.8 %collective-permute-start.25 = (f32[128,128]{1,0:T(8,128)S(1)}, f32[128,128]{1,0:T(8,128)S(1)}, u32[]{:S(2)}, u32[]{:S(2)}) collective-permute-start(f32[128,128]{1,0:T(8,128)S(1)} %convert_add_fusion), channel_id=1, source_target_pairs={{0,1},{1,0},{2,3},{3,2},{4,5},{5,4},{6,7},{7,6},{8,9},{9,8},{10,11... | collective-permute-start | bytes 196616 | tf_op jit(solution)/shard_map/ppermute | solution.py:157
